TPU v7x, 512 devices: a whole 4x8x8 slice. The times are simulated.
512 devices in a mesh: seq: 64 (over z, y_hi, core), head: 8 (over y_lo, x).
Axes of the slice: x: 4, y: 8 (y_hi: 4, y_lo: 2; y = y_hi * 2 + y_lo), z: 8, core: 2. Of those that a mesh axis runs over, the one named last changes fastest.
Arguments:
- noisy_q: bfloat16 [16640, 3072], P('seq', 'head'), may hold values from -38 to 38
- noisy_k: bfloat16 [16640, 1024], P('seq', 'head'), may hold values from -38 to 38
- noisy_value: bfloat16 [16640, 1024], P('seq', 'head'), may hold values from -6 to 6
- clean_k: bfloat16 [16640, 1024], P('seq', 'head'), may hold values from -38 to 38
- clean_value: bfloat16 [16640, 1024], P('seq', 'head'), may hold values from -6 to 6
- q_gain: float32 [3072], P('head'), may hold values from 0.1 to 1.9
- key_norm_gain: float32 [1024], P('head'), may hold values from 0.1 to 1.9
- out_grad: bfloat16 [16640, 3072], P('seq', 'head'), may hold values from -18 to 18
- window: int32 [32, 2], replicated, may hold values from -1 to 30, as said below
Outputs:
- attn_out: bfloat16 [16640, 3072], P('seq', 'head')
- grad_q: bfloat16 [16640, 3072], P('seq', 'head')
- grad_k: bfloat16 [16640, 1024], P('seq', 'head')
- grad_v: bfloat16 [16640, 1024], P('seq', 'head')
- grad_clean_k: bfloat16 [16640, 1024], P('seq', 'head')
- grad_clean_v: bfloat16 [16640, 1024], P('seq', 'head')
Inputs may be any that keep to these rules, and one draw needn't show every extreme that they name: `window`: row c lists, in an order drawn from the seed, the clean stretch c - 1 and one clean stretch from c - 3 to c - 2 that is 0 or later; an entry is -1 where no such stretch exists.
All inputs are finite; a program needn't handle non-finite values.
Results may differ from a plain program's by a relative error of at most 0.04.
Values may be sent and summed in bfloat16 or wider, within the bound.
No kernel may reach another device: no remote copies, remote signals or barrier semaphores. Data moves between devices by JAX's collectives and lax.ppermute only.
A program may use at most 64 MiB of HBM per device.

v0:
```python
import jax
import jax.numpy as jnp
from jax import lax
from jax.sharding import PartitionSpec as P

HEAD_SIZE = 128
KEY_VALUE_HEADS = 8
GROUP = 3
STRETCH = 520
WINDOW = 3
SLOTS = 2
HQ = 24


EPSILON = 1e-06
NEG_FILL = -1e30


def shifted(value, axis, steps):
    count = lax.axis_size(axis)
    initial, last = (max(0, -steps), min(count, count - steps))
    return lax.ppermute(value, axis, [(source, source + steps) for source in range(initial, last)])


def as_sent(array):
    return jax.tree.map(lambda a: a.astype(jnp.bfloat16) if a.dtype == jnp.float32 else a, array)


def assemble(pieces, slot_pos, stretch_span):
    stacked = jnp.stack(pieces[::-1], axis=0)
    taken = lax.dynamic_slice_in_dim(stacked, stretch_span - 1 - slot_pos, stretch_span, 0)
    return taken.reshape(stretch_span * pieces[0].shape[0], pieces[0].shape[1])


def attend(q_norm, out_grad, every_key, key_mask, local_kv):
    rows_dev = q_norm.shape[0]
    score_scale = HEAD_SIZE ** (-0.5)
    per_block = next(
        (count for count in range(1, GROUP + 1) if GROUP % count == 0 and count * rows_dev >= 512),
        GROUP,
    )
    out_parts, dq_parts, dk_parts, dv_parts = ([], [], [], [])
    key_cols = every_key[:, 0:HEAD_SIZE]
    value_columns = every_key[:, local_kv * HEAD_SIZE : (local_kv + 1) * HEAD_SIZE]
    dk_total = jnp.zeros((every_key.shape[0], HEAD_SIZE), dtype=jnp.float32)
    dv_total = jnp.zeros((every_key.shape[0], HEAD_SIZE), dtype=jnp.float32)
    for block_tile in range(GROUP // per_block):
        first_col = (0 + block_tile * per_block) * HEAD_SIZE
        last_col = first_col + per_block * HEAD_SIZE
        query_rows = q_norm[:, first_col:last_col].reshape(rows_dev * per_block, HEAD_SIZE)
        out_grads = out_grad[:, first_col:last_col].reshape(rows_dev * per_block, HEAD_SIZE)
        scores = (
            lax.dot_general(
                query_rows, key_cols, (((1,), (1,)), ((), ())), preferred_element_type=jnp.float32
            )
            * score_scale
        )
        scores = jnp.where(key_mask[None, :], scores, NEG_FILL)
        row_max = jnp.max(scores, axis=1, keepdims=True)
        weights = jnp.exp(scores - row_max)
        probs = weights / jnp.sum(weights, axis=1, keepdims=True)
        probs_low = probs.astype(jnp.bfloat16)
        head_out = jnp.dot(probs_low, value_columns, preferred_element_type=jnp.float32)
        out_parts.append(head_out.astype(jnp.bfloat16).reshape(rows_dev, per_block * HEAD_SIZE))
        dprobs = lax.dot_general(
            out_grads, value_columns, (((1,), (1,)), ((), ())), preferred_element_type=jnp.float32
        )
        row_delta = jnp.sum(out_grads.astype(jnp.float32) * head_out, axis=1, keepdims=True)
        dscores = (probs * (dprobs - row_delta) * score_scale).astype(jnp.bfloat16)
        dq_parts.append(
            jnp.dot(dscores, key_cols, preferred_element_type=jnp.float32).reshape(
                rows_dev, per_block * HEAD_SIZE
            )
        )
        dk_total = dk_total + lax.dot_general(
            dscores, query_rows, (((0,), (0,)), ((), ())), preferred_element_type=jnp.float32
        )
        dv_total = dv_total + lax.dot_general(
            probs_low, out_grads, (((0,), (0,)), ((), ())), preferred_element_type=jnp.float32
        )
    dk_parts.append(dk_total)
    dv_parts.append(dv_total)
    return (
        jnp.concatenate(out_parts, axis=1),
        jnp.concatenate(dq_parts, axis=1),
        jnp.concatenate(dk_parts + dv_parts, axis=1),
    )


def on_device(
    noisy_q, noisy_k, noisy_value, clean_k, clean_value, q_gain, key_norm_gain, out_grad, window
):
    rows_dev = noisy_q.shape[0]
    local_kv = noisy_k.shape[1] // HEAD_SIZE
    stretch_span = STRETCH // rows_dev
    seq_pos = lax.axis_index("seq")
    stretch_id = seq_pos // stretch_span
    slot_pos = seq_pos % stretch_span
    q_full = noisy_q.astype(jnp.float32)
    k_full = noisy_k.astype(jnp.float32)
    c_full = clean_k.astype(jnp.float32)
    totals = lax.psum(
        (
            jnp.sum(q_full * q_full, axis=1),
            jnp.sum(k_full * k_full, axis=1),
            jnp.sum(c_full * c_full, axis=1),
        ),
        "head",
    )
    q_width = HQ * HEAD_SIZE
    key_width = KEY_VALUE_HEADS * HEAD_SIZE
    q_inv = lax.rsqrt(totals[0] / q_width + EPSILON)[:, None]
    k_inv = lax.rsqrt(totals[1] / key_width + EPSILON)[:, None]
    c_inv = lax.rsqrt(totals[2] / key_width + EPSILON)[:, None]
    q_norm = (q_full * q_inv * q_gain[None, :]).astype(jnp.bfloat16)
    k_norm = (k_full * k_inv * key_norm_gain[None, :]).astype(jnp.bfloat16)
    c_norm = (c_full * c_inv * key_norm_gain[None, :]).astype(jnp.bfloat16)
    noisy_kv = jnp.concatenate([k_norm, noisy_value], axis=1)
    clean_kv = jnp.concatenate([c_norm, clean_value], axis=1)
    kv_width = noisy_kv.shape[1]
    offsets = list(range(1 - stretch_span, stretch_span))
    pair_list = []
    for shift_by in offsets:
        if shift_by == 0:
            pair_list.append((noisy_kv, clean_kv))
        else:
            pair_list.append(shifted((noisy_kv, clean_kv), "seq", shift_by))
    noisy_whole = assemble([item[0] for item in pair_list], slot_pos, stretch_span)
    clean_whole = assemble([item[1] for item in pair_list], slot_pos, stretch_span)
    earlier = []
    for back_by in range(WINDOW, 0, -1):
        earlier.append(shifted(clean_whole, "seq", stretch_span * back_by))
    clean_all = jnp.concatenate(earlier, axis=0)
    row_hit = jnp.arange(window.shape[0], dtype=jnp.int32)[:, None] == stretch_id
    listed = jnp.sum(jnp.where(row_hit, window, 0), axis=0)
    first_stretch = stretch_id - WINDOW
    blocks = [noisy_whole]
    mask_parts = [jnp.ones((STRETCH,), dtype=bool)]
    flags = []
    places = []
    for j in range(SLOTS):
        is_listed = listed[j] >= 0
        place_at = jnp.clip(listed[j] - first_stretch, 0, WINDOW - 1)
        blocks.append(lax.dynamic_slice_in_dim(clean_all, place_at * STRETCH, STRETCH, 0))
        mask_parts.append(jnp.broadcast_to(is_listed, (STRETCH,)))
        flags.append(is_listed)
        places.append(place_at)
    attn_out, dq_norm, dkv_all = attend(
        q_norm,
        out_grad,
        jnp.concatenate(blocks, axis=0),
        jnp.concatenate(mask_parts, axis=0),
        local_kv,
    )
    noisy_grad = dkv_all[:STRETCH]
    clean_grad = []
    for place_idx in range(WINDOW):
        summed = jnp.zeros((STRETCH, kv_width), dtype=jnp.float32)
        for j in range(SLOTS):
            summed = summed + jnp.where(
                flags[j] & (places[j] == place_idx),
                dkv_all[(1 + j) * STRETCH : (2 + j) * STRETCH],
                0.0,
            )
        clean_grad.append(summed)
    noisy_total = lax.dynamic_slice_in_dim(noisy_grad, slot_pos * rows_dev, rows_dev, 0)
    clean_own = jnp.zeros((STRETCH, kv_width), dtype=jnp.float32)
    for back_by in range(1, WINDOW + 1):
        clean_own = clean_own + shifted(
            as_sent(clean_grad[WINDOW - back_by]), "seq", -stretch_span * back_by
        )
    clean_total = lax.dynamic_slice_in_dim(clean_own, slot_pos * rows_dev, rows_dev, 0)
    for shift_by in offsets:
        if shift_by != 0:
            send_row = jnp.clip(slot_pos + shift_by, 0, stretch_span - 1) * rows_dev
            received = shifted(
                (
                    as_sent(lax.dynamic_slice_in_dim(noisy_grad, send_row, rows_dev, 0)),
                    as_sent(lax.dynamic_slice_in_dim(clean_own, send_row, rows_dev, 0)),
                ),
                "seq",
                shift_by,
            )
            inside = (slot_pos - shift_by >= 0) & (slot_pos - shift_by < stretch_span)
            noisy_total = noisy_total + jnp.where(inside, received[0], 0.0)
            clean_total = clean_total + jnp.where(inside, received[1], 0.0)
    key_columns = local_kv * HEAD_SIZE
    q_scaled = dq_norm * q_gain[None, :]
    k_scaled = noisy_total[:, :key_columns] * key_norm_gain[None, :]
    c_scaled = clean_total[:, :key_columns] * key_norm_gain[None, :]
    inner_sum = lax.psum(
        (
            jnp.sum(q_scaled * q_full, axis=1),
            jnp.sum(k_scaled * k_full, axis=1),
            jnp.sum(c_scaled * c_full, axis=1),
        ),
        "head",
    )
    grad_q = (
        q_inv * q_scaled - q_full * q_inv * q_inv * q_inv * (inner_sum[0] / q_width)[:, None]
    ).astype(jnp.bfloat16)
    grad_k = (
        k_inv * k_scaled - k_full * k_inv * k_inv * k_inv * (inner_sum[1] / key_width)[:, None]
    ).astype(jnp.bfloat16)
    grad_clean_k = (
        c_inv * c_scaled - c_full * c_inv * c_inv * c_inv * (inner_sum[2] / key_width)[:, None]
    ).astype(jnp.bfloat16)
    grad_v = noisy_total[:, key_columns:].astype(jnp.bfloat16)
    grad_clean_v = clean_total[:, key_columns:].astype(jnp.bfloat16)
    return (attn_out, grad_q, grad_k, grad_v, grad_clean_k, grad_clean_v)


def solution(mesh):
    placed = (
        P("seq", "head"),
        P("seq", "head"),
        P("seq", "head"),
        P("seq", "head"),
        P("seq", "head"),
        P("head"),
        P("head"),
        P("seq", "head"),
        P(),
    )
    return jax.shard_map(
        on_device,
        mesh=mesh,
        in_specs=placed,
        out_specs=(
            P("seq", "head"),
            P("seq", "head"),
            P("seq", "head"),
            P("seq", "head"),
            P("seq", "head"),
            P("seq", "head"),
        ),
        check_vma=False,
    )
```

profile of v0, /device:TPU:258, one launch (start us, length us, event | category | flops | bytes accessed | tf_op | source)
XLA Modules:
  0.0 156.6 jit_solution(9991927911875766899)
XLA Ops:
  0.6 1.1 fusion.18
  1.7 1.0 fusion.44
  2.7 1.0 fusion.46
  3.8 17.2 %all-reduce.1 = (f32[260]{0:T(512)S(1)}, f32[260]{0:T(512)S(1)}, f32[260]{0:T(512)S(1)}) all-reduce(f32[260]{0:T(512)S(1)} %fusion.18, f32[260]{0:T(512)S(1)} %fusion.46, f32[260]{0:T(512)S(1)} %fusion.44), channel_id=1, replica_groups=mesh['seq'=64,'head'=8] {'head'}, use_global_device_ids=true, to_apply=%region_2.3 | all-reduce | flops 780 | bytes 6240 | tf_op jit(solution)/shard_map/psum | solution.py:102
  21.0 1.1 fusion.39
  22.9 1.9 %collective-permute-start.2 = (bf16[260,256]{1,0:T(8,128)(2,1)S(1)}, bf16[260,256]{1,0:T(8,128)(2,1)S(1)}, u32[]{:S(2)}, u32[]{:S(2)}) collective-permute-start(bf16[260,256]{1,0:T(8,128)(2,1)S(1)} %get-tuple-element.30), channel_id=1, source_target_pairs={{0,8},{8,16},{16,24},{24,32},{32,40},{40,48},{48,56},{56,64},{64,7... | collective-permute-start | bytes 399368 | tf_op jit(solution)/shard_map/ppermute | solution.py:22
  24.9 7.9 %collective-permute-start.3 = (bf16[260,256]{1,0:T(8,128)(2,1)S(1)}, bf16[260,256]{1,0:T(8,128)(2,1)S(1)}, u32[]{:S(2)}, u32[]{:S(2)}) collective-permute-start(bf16[260,256]{1,0:T(8,128)(2,1)S(1)} %get-tuple-element.30), channel_id=1, source_target_pairs={{8,0},{16,8},{24,16},{32,24},{40,32},{48,40},{56,48},{64,56},{72,6... | collective-permute-start | bytes 399368 | tf_op jit(solution)/shard_map/ppermute | solution.py:22
  33.7 1.9 %collective-permute-start = (bf16[260,256]{1,0:T(8,128)(2,1)S(1)}, bf16[260,256]{1,0:T(8,128)(2,1)S(1)}, u32[]{:S(2)}, u32[]{:S(2)}) collective-permute-start(bf16[260,256]{1,0:T(8,128)(2,1)S(1)} %get-tuple-element.28), channel_id=1, source_target_pairs={{0,8},{8,16},{16,24},{24,32},{32,40},{40,48},{48,56},{56,64},{64,7... | collective-permute-start | bytes 399368 | tf_op jit(solution)/shard_map/ppermute | solution.py:22
  35.6 7.9 %collective-permute-start.1 = (bf16[260,256]{1,0:T(8,128)(2,1)S(1)}, bf16[260,256]{1,0:T(8,128)(2,1)S(1)}, u32[]{:S(2)}, u32[]{:S(2)}) collective-permute-start(bf16[260,256]{1,0:T(8,128)(2,1)S(1)} %get-tuple-element.28), channel_id=1, source_target_pairs={{8,0},{16,8},{24,16},{32,24},{40,32},{48,40},{56,48},{64,56},{72,6... | collective-permute-start | bytes 399368 | tf_op jit(solution)/shard_map/ppermute | solution.py:22
  43.5 1.0 fusion.13
  44.8 1.9 %collective-permute-start.4 = (bf16[520,256]{1,0:T(8,128)(2,1)S(1)}, bf16[520,256]{1,0:T(8,128)(2,1)S(1)}, u32[]{:S(2)}, u32[]{:S(2)}) collective-permute-start(bf16[520,256]{1,0:T(8,128)(2,1)S(1)} %reshape.49), channel_id=1, source_target_pairs={{0,48},{8,56},{16,64},{24,72},{32,80},{40,88},{48,96},{56,104},{64... | collective-permute-start | bytes 798728 | tf_op jit(solution)/shard_map/ppermute | solution.py:22
  47.5 3.0 %collective-permute-start.5 = (bf16[520,256]{1,0:T(8,128)(2,1)S(1)}, bf16[520,256]{1,0:T(8,128)(2,1)S(1)}, u32[]{:S(2)}, u32[]{:S(2)}) collective-permute-start(bf16[520,256]{1,0:T(8,128)(2,1)S(1)} %reshape.49), channel_id=1, source_target_pairs={{0,32},{8,40},{16,48},{24,56},{32,64},{40,72},{48,80},{56,88},{64,... | collective-permute-start | bytes 798728 | tf_op jit(solution)/shard_map/ppermute | solution.py:22
  53.9 1.0 reshape.51
  55.1 5.7 %collective-permute-start.6 = (bf16[520,256]{1,0:T(8,128)(2,1)S(1)}, bf16[520,256]{1,0:T(8,128)(2,1)S(1)}, u32[]{:S(2)}, u32[]{:S(2)}) collective-permute-start(bf16[520,256]{1,0:T(8,128)(2,1)S(1)} %reshape.49), channel_id=1, source_target_pairs={{0,16},{8,24},{16,32},{24,40},{32,48},{40,56},{48,64},{56,72},{64,... | collective-permute-start | bytes 798728 | tf_op jit(solution)/shard_map/ppermute | solution.py:22
  61.1 9.1 %collective-permute-done.4 = bf16[520,256]{1,0:T(8,128)(2,1)S(1)} collective-permute-done((bf16[520,256]{1,0:T(8,128)(2,1)S(1)}, bf16[520,256]{1,0:T(8,128)(2,1)S(1)}, u32[]{:S(2)}, u32[]{:S(2)}) %collective-permute-start.4) | collective-permute-done | bytes 266272 | tf_op jit(solution)/shard_map/ppermute | solution.py:22
  70.3 3.2 %collective-permute-done.6 = bf16[520,256]{1,0:T(8,128)(2,1)S(1)} collective-permute-done((bf16[520,256]{1,0:T(8,128)(2,1)S(1)}, bf16[520,256]{1,0:T(8,128)(2,1)S(1)}, u32[]{:S(2)}, u32[]{:S(2)}) %collective-permute-start.6) | collective-permute-done | bytes 266272 | tf_op jit(solution)/shard_map/ppermute | solution.py:22
  73.6 1.1 fusion.2
  74.7 1.2 fusion.4
  75.9 1.7 %fusion.3 = f32[780,1560]{1,0:T(8,128)S(1)} fusion(f32[780,1560]{1,0:T(8,128)S(1)} %get-tuple-element.38, f32[780]{0:T(1024)S(1)} %fusion.4, f32[780]{0:T(1024)S(1)} %get-tuple-element.37, pred[1560]{0:T(1024)(128)(4,1)S(1)} %concatenate.18), kind=kLoop, calls=%fused_computation.6 | loop fusion | flops 4867200 | bytes 9742200 | tf_op jit(solution)/shard_map/div | solution.py:61
  78.6 1.1 fusion.5
  80.6 1.1 fusion.51
  82.0 3.9 %collective-permute-start.10 = (bf16[520,256]{1,0:T(8,128)(2,1)S(1)}, bf16[520,256]{1,0:T(8,128)(2,1)S(1)}, u32[]{:S(2)}, u32[]{:S(2)}) collective-permute-start(bf16[520,256]{1,0:T(8,128)(2,1)S(1)} %get-tuple-element.16), channel_id=1, source_target_pairs={{32,0},{40,8},{48,16},{56,24},{64,32},{72,40},{80,48},{88,56},{96,... | collective-permute-start | bytes 798728 | tf_op jit(solution)/shard_map/ppermute | solution.py:22
  85.9 7.1 %collective-permute-start.11 = (bf16[520,256]{1,0:T(8,128)(2,1)S(1)}, bf16[520,256]{1,0:T(8,128)(2,1)S(1)}, u32[]{:S(2)}, u32[]{:S(2)}) collective-permute-start(bf16[520,256]{1,0:T(8,128)(2,1)S(1)} %get-tuple-element.17), channel_id=1, source_target_pairs={{48,0},{56,8},{64,16},{72,24},{80,32},{88,40},{96,48},{104,56},{11... | collective-permute-start | bytes 798728 | tf_op jit(solution)/shard_map/ppermute | solution.py:22
  93.1 3.1 %collective-permute-start.9 = (bf16[520,256]{1,0:T(8,128)(2,1)S(1)}, bf16[520,256]{1,0:T(8,128)(2,1)S(1)}, u32[]{:S(2)}, u32[]{:S(2)}) collective-permute-start(bf16[520,256]{1,0:T(8,128)(2,1)S(1)} %get-tuple-element.14), channel_id=1, source_target_pairs={{16,0},{24,8},{32,16},{40,24},{48,32},{56,40},{64,48},{72,56},{80,... | collective-permute-start | bytes 798728 | tf_op jit(solution)/shard_map/ppermute | solution.py:22
  97.9 1.9 %collective-permute-start.7 = (bf16[260,256]{1,0:T(8,128)(2,1)}, bf16[260,256]{1,0:T(8,128)(2,1)}, u32[]{:S(2)}, u32[]{:S(2)}) collective-permute-start(bf16[260,256]{1,0:T(8,128)(2,1)} %get-tuple-element.21), channel_id=1, source_target_pairs={{8,0},{16,8},{24,16},{32,24},{40,32},{48,40},{56,48},{64,56},{72,6... | collective-permute-start | bytes 399368 | tf_op jit(solution)/shard_map/ppermute | solution.py:22
  99.8 2.4 %collective-permute-start.8 = (bf16[260,256]{1,0:T(8,128)(2,1)}, bf16[260,256]{1,0:T(8,128)(2,1)}, u32[]{:S(2)}, u32[]{:S(2)}) collective-permute-start(bf16[260,256]{1,0:T(8,128)(2,1)} %get-tuple-element.22), channel_id=1, source_target_pairs={{0,8},{8,16},{16,24},{24,32},{32,40},{40,48},{48,56},{56,64},{64,7... | collective-permute-start | bytes 399368 | tf_op jit(solution)/shard_map/ppermute | solution.py:22
  103.3 1.7 %collective-permute-done.11 = bf16[520,256]{1,0:T(8,128)(2,1)S(1)} collective-permute-done((bf16[520,256]{1,0:T(8,128)(2,1)S(1)}, bf16[520,256]{1,0:T(8,128)(2,1)S(1)}, u32[]{:S(2)}, u32[]{:S(2)}) %collective-permute-start.11) | collective-permute-done | bytes 266272 | tf_op jit(solution)/shard_map/ppermute | solution.py:22
  105.0 12.7 %collective-permute-done.9 = bf16[520,256]{1,0:T(8,128)(2,1)S(1)} collective-permute-done((bf16[520,256]{1,0:T(8,128)(2,1)S(1)}, bf16[520,256]{1,0:T(8,128)(2,1)S(1)}, u32[]{:S(2)}, u32[]{:S(2)}) %collective-permute-start.9) | collective-permute-done | bytes 266272 | tf_op jit(solution)/shard_map/ppermute | solution.py:22
  117.9 5.6 %collective-permute-start.12 = (bf16[260,256]{1,0:T(8,128)(2,1)S(1)}, bf16[260,256]{1,0:T(8,128)(2,1)S(1)}, u32[]{:S(2)}, u32[]{:S(2)}) collective-permute-start(bf16[260,256]{1,0:T(8,128)(2,1)S(1)} %get-tuple-element.23), channel_id=1, source_target_pairs={{8,0},{16,8},{24,16},{32,24},{40,32},{48,40},{56,48},{64,56},{72,6... | collective-permute-start | bytes 399368 | tf_op jit(solution)/shard_map/ppermute | solution.py:22
  123.5 1.9 %collective-permute-start.13 = (bf16[260,256]{1,0:T(8,128)(2,1)S(1)}, bf16[260,256]{1,0:T(8,128)(2,1)S(1)}, u32[]{:S(2)}, u32[]{:S(2)}) collective-permute-start(bf16[260,256]{1,0:T(8,128)(2,1)S(1)} %get-tuple-element.24), channel_id=1, source_target_pairs={{0,8},{8,16},{16,24},{24,32},{32,40},{40,48},{48,56},{56,64},{64,7... | collective-permute-start | bytes 399368 | tf_op jit(solution)/shard_map/ppermute | solution.py:22
  127.5 6.7 %collective-permute-done.13 = bf16[260,256]{1,0:T(8,128)(2,1)S(1)} collective-permute-done((bf16[260,256]{1,0:T(8,128)(2,1)S(1)}, bf16[260,256]{1,0:T(8,128)(2,1)S(1)}, u32[]{:S(2)}, u32[]{:S(2)}) %collective-permute-start.13) | collective-permute-done | bytes 133152 | tf_op jit(solution)/shard_map/ppermute | solution.py:22
  135.1 19.7 %all-reduce = (f32[260]{0:T(512)S(1)}, f32[260]{0:T(512)S(1)}, f32[260]{0:T(512)S(1)}) all-reduce(f32[260]{0:T(512)S(1)} %fusion.19, f32[260]{0:T(512)S(1)} %get-tuple-element.7, f32[260]{0:T(512)S(1)} %get-tuple-element.6), channel_id=1, replica_groups=mesh['seq'=64,'head'=8] {'head'}, use_global_device_ids=true, to_apply=%region_11.12 | all-reduce | flops 780 | bytes 6240 | tf_op jit(solution)/shard_map/psum | solution.py:191
  (61 shorter events, 13.8 us)
Async XLA Ops:
  22.9 21.6 %collective-permute-start.2 = (bf16[260,256]{1,0:T(8,128)(2,1)S(1)}, bf16[260,256]{1,0:T(8,128)(2,1)S(1)}, u32[]{:S(2)}, u32[]{:S(2)}) collective-permute-start(bf16[260,256]{1,0:T(8,128)(2,1)S(1)} %get-tuple-element.30), channel_id=1, source_target_pairs={{0,8},{8,16},{16,24},{24,32},{32,40},{40,48},{48,56},{56,64},{64,7... | collective-permute-start | bytes 399368 | tf_op jit(solution)/shard_map/ppermute | solution.py:22
  24.9 19.7 %collective-permute-start.3 = (bf16[260,256]{1,0:T(8,128)(2,1)S(1)}, bf16[260,256]{1,0:T(8,128)(2,1)S(1)}, u32[]{:S(2)}, u32[]{:S(2)}) collective-permute-start(bf16[260,256]{1,0:T(8,128)(2,1)S(1)} %get-tuple-element.30), channel_id=1, source_target_pairs={{8,0},{16,8},{24,16},{32,24},{40,32},{48,40},{56,48},{64,56},{72,6... | collective-permute-start | bytes 399368 | tf_op jit(solution)/shard_map/ppermute | solution.py:22
  33.7 27.2 %collective-permute-start = (bf16[260,256]{1,0:T(8,128)(2,1)S(1)}, bf16[260,256]{1,0:T(8,128)(2,1)S(1)}, u32[]{:S(2)}, u32[]{:S(2)}) collective-permute-start(bf16[260,256]{1,0:T(8,128)(2,1)S(1)} %get-tuple-element.28), channel_id=1, source_target_pairs={{0,8},{8,16},{16,24},{24,32},{32,40},{40,48},{48,56},{56,64},{64,7... | collective-permute-start | bytes 399368 | tf_op jit(solution)/shard_map/ppermute | solution.py:22
  35.6 25.3 %collective-permute-start.1 = (bf16[260,256]{1,0:T(8,128)(2,1)S(1)}, bf16[260,256]{1,0:T(8,128)(2,1)S(1)}, u32[]{:S(2)}, u32[]{:S(2)}) collective-permute-start(bf16[260,256]{1,0:T(8,128)(2,1)S(1)} %get-tuple-element.28), channel_id=1, source_target_pairs={{8,0},{16,8},{24,16},{32,24},{40,32},{48,40},{56,48},{64,56},{72,6... | collective-permute-start | bytes 399368 | tf_op jit(solution)/shard_map/ppermute | solution.py:22
  44.8 25.4 %collective-permute-start.4 = (bf16[520,256]{1,0:T(8,128)(2,1)S(1)}, bf16[520,256]{1,0:T(8,128)(2,1)S(1)}, u32[]{:S(2)}, u32[]{:S(2)}) collective-permute-start(bf16[520,256]{1,0:T(8,128)(2,1)S(1)} %reshape.49), channel_id=1, source_target_pairs={{0,48},{8,56},{16,64},{24,72},{32,80},{40,88},{48,96},{56,104},{64... | collective-permute-start | bytes 798728 | tf_op jit(solution)/shard_map/ppermute | solution.py:22
  47.5 22.7 %collective-permute-start.5 = (bf16[520,256]{1,0:T(8,128)(2,1)S(1)}, bf16[520,256]{1,0:T(8,128)(2,1)S(1)}, u32[]{:S(2)}, u32[]{:S(2)}) collective-permute-start(bf16[520,256]{1,0:T(8,128)(2,1)S(1)} %reshape.49), channel_id=1, source_target_pairs={{0,32},{8,40},{16,48},{24,56},{32,64},{40,72},{48,80},{56,88},{64,... | collective-permute-start | bytes 798728 | tf_op jit(solution)/shard_map/ppermute | solution.py:22
  55.1 18.4 %collective-permute-start.6 = (bf16[520,256]{1,0:T(8,128)(2,1)S(1)}, bf16[520,256]{1,0:T(8,128)(2,1)S(1)}, u32[]{:S(2)}, u32[]{:S(2)}) collective-permute-start(bf16[520,256]{1,0:T(8,128)(2,1)S(1)} %reshape.49), channel_id=1, source_target_pairs={{0,16},{8,24},{16,32},{24,40},{32,48},{40,56},{48,64},{56,72},{64,... | collective-permute-start | bytes 798728 | tf_op jit(solution)/shard_map/ppermute | solution.py:22
  81.8 21.3 %copy-start = (bf16[260,384]{1,0:T(8,128)(2,1)S(1)}, bf16[260,384]{1,0:T(8,128)(2,1)}, u32[]{:S(2)}) copy-start(bf16[260,384]{1,0:T(8,128)(2,1)} %param.9) | copy-start | bytes 599044
  81.8 21.3 %copy-start.3 = (f32[384]{0:T(512)S(1)}, f32[384]{0:T(512)}, u32[]{:S(2)}) copy-start(f32[384]{0:T(512)} %param.14) | copy-start | bytes 4612
  82.0 21.3 %collective-permute-start.10 = (bf16[520,256]{1,0:T(8,128)(2,1)S(1)}, bf16[520,256]{1,0:T(8,128)(2,1)S(1)}, u32[]{:S(2)}, u32[]{:S(2)}) collective-permute-start(bf16[520,256]{1,0:T(8,128)(2,1)S(1)} %get-tuple-element.16), channel_id=1, source_target_pairs={{32,0},{40,8},{48,16},{56,24},{64,32},{72,40},{80,48},{88,56},{96,... | collective-permute-start | bytes 798728 | tf_op jit(solution)/shard_map/ppermute | solution.py:22
  85.9 19.0 %collective-permute-start.11 = (bf16[520,256]{1,0:T(8,128)(2,1)S(1)}, bf16[520,256]{1,0:T(8,128)(2,1)S(1)}, u32[]{:S(2)}, u32[]{:S(2)}) collective-permute-start(bf16[520,256]{1,0:T(8,128)(2,1)S(1)} %get-tuple-element.17), channel_id=1, source_target_pairs={{48,0},{56,8},{64,16},{72,24},{80,32},{88,40},{96,48},{104,56},{11... | collective-permute-start | bytes 798728 | tf_op jit(solution)/shard_map/ppermute | solution.py:22
  93.1 41.2 %copy-start.1 = (bf16[260,128]{1,0:T(8,128)(2,1)S(1)}, bf16[260,128]{1,0:T(8,128)(2,1)}, u32[]{:S(2)}) copy-start(bf16[260,128]{1,0:T(8,128)(2,1)} %param.10) | copy-start | bytes 199684
  93.1 41.2 %copy-start.2 = (bf16[260,128]{1,0:T(8,128)(2,1)S(1)}, bf16[260,128]{1,0:T(8,128)(2,1)}, u32[]{:S(2)}) copy-start(bf16[260,128]{1,0:T(8,128)(2,1)} %param.12) | copy-start | bytes 199684
  93.1 41.2 %copy-start.4 = (f32[128]{0:T(128)S(1)}, f32[128]{0:T(128)}, u32[]{:S(2)}) copy-start(f32[128]{0:T(128)} %param.15) | copy-start | bytes 1540
  93.1 24.6 %collective-permute-start.9 = (bf16[520,256]{1,0:T(8,128)(2,1)S(1)}, bf16[520,256]{1,0:T(8,128)(2,1)S(1)}, u32[]{:S(2)}, u32[]{:S(2)}) collective-permute-start(bf16[520,256]{1,0:T(8,128)(2,1)S(1)} %get-tuple-element.14), channel_id=1, source_target_pairs={{16,0},{24,8},{32,16},{40,24},{48,32},{56,40},{64,48},{72,56},{80,... | collective-permute-start | bytes 798728 | tf_op jit(solution)/shard_map/ppermute | solution.py:22
  97.9 27.5 %collective-permute-start.7 = (bf16[260,256]{1,0:T(8,128)(2,1)}, bf16[260,256]{1,0:T(8,128)(2,1)}, u32[]{:S(2)}, u32[]{:S(2)}) collective-permute-start(bf16[260,256]{1,0:T(8,128)(2,1)} %get-tuple-element.21), channel_id=1, source_target_pairs={{8,0},{16,8},{24,16},{32,24},{40,32},{48,40},{56,48},{64,56},{72,6... | collective-permute-start | bytes 399368 | tf_op jit(solution)/shard_map/ppermute | solution.py:22
  99.8 25.6 %collective-permute-start.8 = (bf16[260,256]{1,0:T(8,128)(2,1)}, bf16[260,256]{1,0:T(8,128)(2,1)}, u32[]{:S(2)}, u32[]{:S(2)}) collective-permute-start(bf16[260,256]{1,0:T(8,128)(2,1)} %get-tuple-element.22), channel_id=1, source_target_pairs={{0,8},{8,16},{16,24},{24,32},{32,40},{40,48},{48,56},{56,64},{64,7... | collective-permute-start | bytes 399368 | tf_op jit(solution)/shard_map/ppermute | solution.py:22
  117.9 9.6 %collective-permute-start.12 = (bf16[260,256]{1,0:T(8,128)(2,1)S(1)}, bf16[260,256]{1,0:T(8,128)(2,1)S(1)}, u32[]{:S(2)}, u32[]{:S(2)}) collective-permute-start(bf16[260,256]{1,0:T(8,128)(2,1)S(1)} %get-tuple-element.23), channel_id=1, source_target_pairs={{8,0},{16,8},{24,16},{32,24},{40,32},{48,40},{56,48},{64,56},{72,6... | collective-permute-start | bytes 399368 | tf_op jit(solution)/shard_map/ppermute | solution.py:22
  123.5 10.6 %collective-permute-start.13 = (bf16[260,256]{1,0:T(8,128)(2,1)S(1)}, bf16[260,256]{1,0:T(8,128)(2,1)S(1)}, u32[]{:S(2)}, u32[]{:S(2)}) collective-permute-start(bf16[260,256]{1,0:T(8,128)(2,1)S(1)} %get-tuple-element.24), channel_id=1, source_target_pairs={{0,8},{8,16},{16,24},{24,32},{32,40},{40,48},{48,56},{56,64},{64,7... | collective-permute-start | bytes 399368 | tf_op jit(solution)/shard_map/ppermute | solution.py:22
where the time goes:
time: 157 us
  starting transfers between devices  56.3 us (36%)
  blocking collectives  36.8 us (23%)
  waiting for transfers between devices  33.8 us (22%)
  other arithmetic  14.7 us (9%)
  matrix products  6.1 us (4%)
  local copies, waits for them, and re-layouts  5.05 us (3%)
  between operations  3.82 us (2%)
    ppermute x14, starting transfers between devices, shifted(): lax.ppermute(value, axis, [(source, source + steps) for source in range(i...  56.3 us
    ppermute x14, waiting for transfers between devices, shifted(): lax.ppermute(value, axis, [(source, source + steps) for source in range(i...  33.8 us
    psum x1, blocking collectives, on_device(): lax.psum((jnp.sum(q_scaled * q_full, axis=1), jnp.sum(k_scaled * k_full,...  19.7 us
    psum x1, blocking collectives, on_device(): lax.psum((jnp.sum(q_full * q_full, axis=1), jnp.sum(k_full * k_full, axis...  17.2 us
  transfers between devices with their start and end apart: 14, of which 6 were waited for; matrix products, arithmetic and copies ran while one was open for 6% of the time, Pallas kernels for 0%

commit v1 on v0

--- a/solution.py
+++ b/solution.py
@@ -16,20 +16,22 @@
 NEG_FILL = -1e30
 
 
-def shifted(value, axis, steps):
-    count = lax.axis_size(axis)
-    initial, last = (max(0, -steps), min(count, count - steps))
-    return lax.ppermute(value, axis, [(source, source + steps) for source in range(initial, last)])
-
-
-def as_sent(array):
-    return jax.tree.map(lambda a: a.astype(jnp.bfloat16) if a.dtype == jnp.float32 else a, array)
-
-
-def assemble(pieces, slot_pos, stretch_span):
-    stacked = jnp.stack(pieces[::-1], axis=0)
-    taken = lax.dynamic_slice_in_dim(stacked, stretch_span - 1 - slot_pos, stretch_span, 0)
-    return taken.reshape(stretch_span * pieces[0].shape[0], pieces[0].shape[1])
+def head_sums(parts):
+    stacked = jnp.stack(parts, axis=0)
+    count = lax.axis_size("head")
+    spread = jnp.broadcast_to(stacked[None], (count,) + stacked.shape)
+    return jnp.sum(lax.all_to_all(spread, "head", 0, 0), axis=0)
+
+
+def stretch_shift(value, steps):
+    count = lax.axis_size("seq")
+    pairs = [(i, i + 2 * steps) for i in range(count) if 0 <= i + 2 * steps < count]
+    return lax.ppermute(value, "seq", pairs)
+
+
+def core_swap(value):
+    count = lax.axis_size("seq")
+    return lax.ppermute(value, "seq", [(i, i ^ 1) for i in range(count)])
 
 
 def attend(q_norm, out_grad, every_key, key_mask, local_kv):
@@ -95,17 +97,15 @@
     stretch_span = STRETCH // rows_dev
     seq_pos = lax.axis_index("seq")
     stretch_id = seq_pos // stretch_span
-    slot_pos = seq_pos % stretch_span
     q_full = noisy_q.astype(jnp.float32)
     k_full = noisy_k.astype(jnp.float32)
     c_full = clean_k.astype(jnp.float32)
-    totals = lax.psum(
+    totals = head_sums(
         (
             jnp.sum(q_full * q_full, axis=1),
             jnp.sum(k_full * k_full, axis=1),
             jnp.sum(c_full * c_full, axis=1),
-        ),
-        "head",
+        )
     )
     q_width = HQ * HEAD_SIZE
     key_width = KEY_VALUE_HEADS * HEAD_SIZE
@@ -117,84 +117,49 @@
     c_norm = (c_full * c_inv * key_norm_gain[None, :]).astype(jnp.bfloat16)
     noisy_kv = jnp.concatenate([k_norm, noisy_value], axis=1)
     clean_kv = jnp.concatenate([c_norm, clean_value], axis=1)
-    kv_width = noisy_kv.shape[1]
-    offsets = list(range(1 - stretch_span, stretch_span))
-    pair_list = []
-    for shift_by in offsets:
-        if shift_by == 0:
-            pair_list.append((noisy_kv, clean_kv))
-        else:
-            pair_list.append(shifted((noisy_kv, clean_kv), "seq", shift_by))
-    noisy_whole = assemble([item[0] for item in pair_list], slot_pos, stretch_span)
-    clean_whole = assemble([item[1] for item in pair_list], slot_pos, stretch_span)
-    earlier = []
-    for back_by in range(WINDOW, 0, -1):
-        earlier.append(shifted(clean_whole, "seq", stretch_span * back_by))
-    clean_all = jnp.concatenate(earlier, axis=0)
     row_hit = jnp.arange(window.shape[0], dtype=jnp.int32)[:, None] == stretch_id
     listed = jnp.sum(jnp.where(row_hit, window, 0), axis=0)
-    first_stretch = stretch_id - WINDOW
-    blocks = [noisy_whole]
-    mask_parts = [jnp.ones((STRETCH,), dtype=bool)]
-    flags = []
-    places = []
-    for j in range(SLOTS):
-        is_listed = listed[j] >= 0
-        place_at = jnp.clip(listed[j] - first_stretch, 0, WINDOW - 1)
-        blocks.append(lax.dynamic_slice_in_dim(clean_all, place_at * STRETCH, STRETCH, 0))
-        mask_parts.append(jnp.broadcast_to(is_listed, (STRETCH,)))
-        flags.append(is_listed)
-        places.append(place_at)
+    use = [jnp.any((listed == stretch_id - back) & (listed >= 0)) for back in (1, 2, 3)]
+    got = [stretch_shift(clean_kv, back) for back in (1, 2, 3)]
+    other = jnp.where(use[1], got[1], got[2])
+    mine = jnp.concatenate([noisy_kv, got[0], other], axis=0)
+    theirs = core_swap(mine)
+    rows3 = 3 * rows_dev
+    part_mask = jnp.concatenate(
+        [
+            jnp.ones((rows_dev,), dtype=bool),
+            jnp.broadcast_to(use[0], (rows_dev,)),
+            jnp.broadcast_to(use[1] | use[2], (rows_dev,)),
+        ]
+    )
     attn_out, dq_norm, dkv_all = attend(
         q_norm,
         out_grad,
-        jnp.concatenate(blocks, axis=0),
-        jnp.concatenate(mask_parts, axis=0),
+        jnp.concatenate([mine, theirs], axis=0),
+        jnp.concatenate([part_mask, part_mask]),
         local_kv,
     )
-    noisy_grad = dkv_all[:STRETCH]
-    clean_grad = []
-    for place_idx in range(WINDOW):
-        summed = jnp.zeros((STRETCH, kv_width), dtype=jnp.float32)
-        for j in range(SLOTS):
-            summed = summed + jnp.where(
-                flags[j] & (places[j] == place_idx),
-                dkv_all[(1 + j) * STRETCH : (2 + j) * STRETCH],
-                0.0,
-            )
-        clean_grad.append(summed)
-    noisy_total = lax.dynamic_slice_in_dim(noisy_grad, slot_pos * rows_dev, rows_dev, 0)
-    clean_own = jnp.zeros((STRETCH, kv_width), dtype=jnp.float32)
-    for back_by in range(1, WINDOW + 1):
-        clean_own = clean_own + shifted(
-            as_sent(clean_grad[WINDOW - back_by]), "seq", -stretch_span * back_by
-        )
-    clean_total = lax.dynamic_slice_in_dim(clean_own, slot_pos * rows_dev, rows_dev, 0)
-    for shift_by in offsets:
-        if shift_by != 0:
-            send_row = jnp.clip(slot_pos + shift_by, 0, stretch_span - 1) * rows_dev
-            received = shifted(
-                (
-                    as_sent(lax.dynamic_slice_in_dim(noisy_grad, send_row, rows_dev, 0)),
-                    as_sent(lax.dynamic_slice_in_dim(clean_own, send_row, rows_dev, 0)),
-                ),
-                "seq",
-                shift_by,
-            )
-            inside = (slot_pos - shift_by >= 0) & (slot_pos - shift_by < stretch_span)
-            noisy_total = noisy_total + jnp.where(inside, received[0], 0.0)
-            clean_total = clean_total + jnp.where(inside, received[1], 0.0)
+    reduced = dkv_all[:rows3] + core_swap(dkv_all[rows3:].astype(jnp.bfloat16)).astype(jnp.float32)
+    noisy_total = reduced[:rows_dev]
+    back1 = jnp.where(use[0], reduced[rows_dev : 2 * rows_dev], 0.0).astype(jnp.bfloat16)
+    dother = reduced[2 * rows_dev :]
+    back2 = jnp.where(use[1], dother, 0.0).astype(jnp.bfloat16)
+    back3 = jnp.where(use[2], dother, 0.0).astype(jnp.bfloat16)
+    clean_total = (
+        stretch_shift(back2, -2).astype(jnp.float32)
+        + stretch_shift(back3, -3).astype(jnp.float32)
+        + stretch_shift(back1, -1).astype(jnp.float32)
+    )
     key_columns = local_kv * HEAD_SIZE
     q_scaled = dq_norm * q_gain[None, :]
     k_scaled = noisy_total[:, :key_columns] * key_norm_gain[None, :]
     c_scaled = clean_total[:, :key_columns] * key_norm_gain[None, :]
-    inner_sum = lax.psum(
+    inner_sum = head_sums(
         (
             jnp.sum(q_scaled * q_full, axis=1),
             jnp.sum(k_scaled * k_full, axis=1),
             jnp.sum(c_scaled * c_full, axis=1),
-        ),
-        "head",
+        )
     )
     grad_q = (
         q_inv * q_scaled - q_full * q_inv * q_inv * q_inv * (inner_sum[0] / q_width)[:, None]

time: 157 us -> 104 us (0.66)
  the two profiles are of different devices: /device:TPU:258 before, /device:TPU:336 now
where the time goes in v1:
time: 104 us; the launch traced here: 103 us
  starting transfers between devices  44.3 us (43%)
  waiting for transfers between devices  21.5 us (21%)
  other arithmetic  19.2 us (18%)
  local copies, waits for them, and re-layouts  8.8 us (8%)
  matrix products  6.68 us (6%)
  between operations  2.23 us (2%)
    ppermute x6, starting transfers between devices, stretch_shift(): return lax.ppermute(value, 'seq', pairs)  27.5 us
    all_to_all x2, starting transfers between devices, head_sums(): return jnp.sum(lax.all_to_all(spread, 'head', 0, 0), axis=0)  12.3 us
    ppermute x6, waiting for transfers between devices, stretch_shift(): return lax.ppermute(value, 'seq', pairs)  11.2 us
    all_to_all x2, waiting for transfers between devices, head_sums(): return jnp.sum(lax.all_to_all(spread, 'head', 0, 0), axis=0)  9.61 us
    ppermute x2, starting transfers between devices, core_swap(): return lax.ppermute(value, 'seq', [(i, i ^ 1) for i in range(count)])  4.46 us
    concatenate x1, local copies, waits for them, and re-layouts, on_device(): jnp.concatenate([mine, theirs], axis=0)  2.52 us
  transfers between devices with their start and end apart: 10, of which 7 were waited for; matrix products, arithmetic and copies ran while one was open for 10% of the time, Pallas kernels for 0%

profile of v1, /device:TPU:336, one launch (start us, length us, event | category | flops | bytes accessed | tf_op | source)
XLA Modules:
  0.0 102.7 jit_solution(3351056166106152378)
XLA Ops:
  0.6 1.1 %fusion.19 = f32[260]{0:T(512)S(1)} fusion(bf16[260,384]{1,0:T(8,128)(2,1)} %param.9), kind=kLoop, calls=%fused_computation.28 | loop fusion | flops 299260 | bytes 200720 | tf_op jit(solution)/shard_map/reduce_sum | solution.py:105
  1.7 1.0 %fusion.42 = f32[260]{0:T(512)S(1)} fusion(bf16[260,128]{1,0:T(8,128)(2,1)} %param.10), kind=kLoop, calls=%fused_computation.63 | loop fusion | flops 99580 | bytes 67600 | tf_op jit(solution)/shard_map/reduce_sum | solution.py:106
  2.8 1.0 %fusion.44 = f32[260]{0:T(512)S(1)} fusion(bf16[260,128]{1,0:T(8,128)(2,1)} %param.12), kind=kLoop, calls=%fused_computation.65 | loop fusion | flops 99580 | bytes 67600 | tf_op jit(solution)/shard_map/reduce_sum | solution.py:107
  4.4 5.3 %all-to-all-start = ((f32[8,3,260]{2,1,0:T(4,128)}), f32[8,3,260]{2,1,0:T(4,128)S(1)}, u32[]{:S(2)}, u32[]{:S(2)}) async-start(f32[8,3,260]{2,1,0:T(4,128)} %broadcast_in_dim.74), calls=%async_computation | async-start | bytes 98304 | tf_op jit(solution)/shard_map/all_to_all | solution.py:23
  9.8 6.3 %all-to-all-done = f32[8,3,260]{2,1,0:T(4,128)S(1)} async-done(((f32[8,3,260]{2,1,0:T(4,128)}), f32[8,3,260]{2,1,0:T(4,128)S(1)}, u32[]{:S(2)}, u32[]{:S(2)}) %all-to-all-start) | async-done | bytes 24992 | tf_op jit(solution)/shard_map/all_to_all | solution.py:23
  16.1 1.1 %fusion.32 = (bf16[260,128]{1,0:T(8,128)(2,1)S(1)}, bf16[260,128]{1,0:T(8,128)(2,1)S(1)}) fusion(bf16[260,128]{1,0:T(8,128)(2,1)} %param.12, f32[260]{0:T(512)S(1)} %get-tuple-element.9, f32[128]{0:T(128)} %param.15, f32[260]{0:T(512)S(1)} %get-tuple-element.10, bf16[260,128]{1,0:T(8,128)(2,1)} %param.10), kind=kLoop, calls=%fused_computation.53 | loop fusion | flops 266240 | bytes 268832 | tf_op jit(solution)/shard_map/convert_element_type | solution.py:117
  18.1 5.0 %collective-permute-start.1 = (bf16[260,256]{1,0:T(8,128)(2,1)S(1)}, bf16[260,256]{1,0:T(8,128)(2,1)S(1)}, u32[]{:S(2)}, u32[]{:S(2)}) collective-permute-start(bf16[260,256]{1,0:T(8,128)(2,1)S(1)} %pad_maximum_fusion.3), channel_id=1, source_target_pairs={{0,32},{8,40},{16,48},{24,56},{32,64},{40,72},{48,80},{56,88},{64,... | collective-permute-start | bytes 399368 | tf_op jit(solution)/shard_map/ppermute | solution.py:29
  23.1 5.0 %collective-permute-start.2 = (bf16[260,256]{1,0:T(8,128)(2,1)S(1)}, bf16[260,256]{1,0:T(8,128)(2,1)S(1)}, u32[]{:S(2)}, u32[]{:S(2)}) collective-permute-start(bf16[260,256]{1,0:T(8,128)(2,1)S(1)} %pad_maximum_fusion.3), channel_id=1, source_target_pairs={{0,48},{8,56},{16,64},{24,72},{32,80},{40,88},{48,96},{56,104},{64... | collective-permute-start | bytes 399368 | tf_op jit(solution)/shard_map/ppermute | solution.py:29
  29.6 3.9 %collective-permute-start = (bf16[260,256]{1,0:T(8,128)(2,1)S(1)}, bf16[260,256]{1,0:T(8,128)(2,1)S(1)}, u32[]{:S(2)}, u32[]{:S(2)}) collective-permute-start(bf16[260,256]{1,0:T(8,128)(2,1)S(1)} %pad_maximum_fusion.3), channel_id=1, source_target_pairs={{0,16},{8,24},{16,32},{24,40},{32,48},{40,56},{48,64},{56,72},{64,... | collective-permute-start | bytes 399368 | tf_op jit(solution)/shard_map/ppermute | solution.py:29
  33.5 2.5 %collective-permute-done.2 = bf16[260,256]{1,0:T(8,128)(2,1)S(1)} collective-permute-done((bf16[260,256]{1,0:T(8,128)(2,1)S(1)}, bf16[260,256]{1,0:T(8,128)(2,1)S(1)}, u32[]{:S(2)}, u32[]{:S(2)}) %collective-permute-start.2) | collective-permute-done | bytes 133152 | tf_op jit(solution)/shard_map/ppermute | solution.py:29
  36.7 1.2 %collective-permute-done = bf16[260,256]{1,0:T(8,128)(2,1)S(1)} collective-permute-done((bf16[260,256]{1,0:T(8,128)(2,1)S(1)}, bf16[260,256]{1,0:T(8,128)(2,1)S(1)}, u32[]{:S(2)}, u32[]{:S(2)}) %collective-permute-start) | collective-permute-done | bytes 133152 | tf_op jit(solution)/shard_map/ppermute | solution.py:29
  38.8 1.9 %collective-permute-start.3 = (bf16[780,256]{1,0:T(8,128)(2,1)S(1)}, bf16[780,256]{1,0:T(8,128)(2,1)S(1)}, u32[]{:S(2)}, u32[]{:S(2)}) collective-permute-start(bf16[780,256]{1,0:T(8,128)(2,1)S(1)} %pad_maximum_fusion.1), channel_id=1, source_target_pairs={{0,8},{8,0},{16,24},{24,16},{32,40},{40,32},{48,56},{56,48},{64,72... | collective-permute-start | bytes 1198088 | tf_op jit(solution)/shard_map/ppermute | solution.py:34
  42.0 1.0 %reshape.96 = bf16[780,128]{1,0:T(8,128)(2,1)S(1)} reshape(bf16[260,384]{1,0:T(8,128)(2,1)} %param.16) | data formatting | bytes 399360 | tf_op jit(solution)/shard_map/reshape | solution.py:53
  43.8 1.0 %fusion.14 = bf16[260,384]{1,0:T(8,128)(2,1)S(1)} fusion(bf16[260,384]{1,0:T(8,128)(2,1)} %param.9, f32[384]{0:T(512)} %param.14, f32[260]{0:T(512)S(1)} %get-tuple-element.11), kind=kLoop, calls=%fused_computation.23 | loop fusion | flops 399360 | bytes 401936 | tf_op jit(solution)/shard_map/convert_element_type | solution.py:115
  45.9 2.5 %concatenate.25 = bf16[1560,256]{1,0:T(8,128)(2,1)S(1)} concatenate(bf16[260,256]{1,0:T(8,128)(2,1)S(1)} %pad_maximum_fusion.2, bf16[260,256]{1,0:T(8,128)(2,1)S(1)} %collective-permute-done, bf16[260,256]{1,0:T(8,128)(2,1)S(1)} %broadcast_select_fusion, bf16[780,256]{1,0:T(8,128)(2,1)S(1)} %collective-permute-done.3), dimensions={0} | concatenate | bytes 1597440 | tf_op jit(solution)/shard_map/concatenate | solution.py:138
  48.4 1.1 %fusion.2 = (f32[780]{0:T(1024)S(1)}, f32[780,1560]{1,0:T(8,128)S(1)}) fusion(pred[1560]{0:T(1024)(128)(4,1)S(1)} %concatenate.21, bf16[780,128]{1,0:T(8,128)(2,1)S(1)} %reshape.94, bf16[1560,256]{1,0:T(8,128)(2,1)S(1)} %concatenate.25), kind=kOutput, calls=%fused_computation.5 | convolution fusion | flops 315150432 | bytes 5472432 | tf_op jit(solution)/shard_map/dot_general | solution.py:55
  49.5 1.2 %fusion.4 = f32[780]{0:T(1024)S(1)} fusion(f32[780,1560]{1,0:T(8,128)S(1)} %get-tuple-element.27, f32[780]{0:T(1024)S(1)} %get-tuple-element.26, pred[1560]{0:T(1024)(128)(4,1)S(1)} %concatenate.21), kind=kLoop, calls=%fused_computation.7 | loop fusion | flops 4866420 | bytes 4875000 | tf_op jit(solution)/shard_map/reduce_sum | solution.py:63
  50.7 1.7 %fusion.3 = f32[780,1560]{1,0:T(8,128)S(1)} fusion(f32[780,1560]{1,0:T(8,128)S(1)} %get-tuple-element.27, f32[780]{0:T(1024)S(1)} %fusion.4, f32[780]{0:T(1024)S(1)} %get-tuple-element.26, pred[1560]{0:T(1024)(128)(4,1)S(1)} %concatenate.21), kind=kLoop, calls=%fused_computation.6 | loop fusion | flops 4867200 | bytes 9742200 | tf_op jit(solution)/shard_map/div | solution.py:63
  52.4 1.6 %multiply_reduce_fusion = (f32[780]{0:T(1024)S(1)}, bf16[780,128]{1,0:T(8,128)(2,1)}) fusion(bf16[780,128]{1,0:T(8,128)(2,1)S(1)} %reshape.96, bf16[1560,256]{1,0:T(8,128)(2,1)S(1)} %concatenate.25, f32[780,1560]{1,0:T(8,128)S(1)} %fusion.3), kind=kOutput, calls=%fused_computation.31 | convolution fusion | flops 313116192 | bytes 6021168 | tf_op jit(solution)/shard_map/dot_general | solution.py:65
  54.0 1.1 %fusion.5 = f32[1560,128]{1,0:T(8,128)S(1)} fusion(bf16[780,128]{1,0:T(8,128)(2,1)S(1)} %reshape.96, f32[780,1560]{1,0:T(8,128)S(1)} %fusion.3), kind=kOutput, calls=%fused_computation.10 | convolution fusion | flops 312717600 | bytes 5865600 | tf_op jit(solution)/shard_map/dot_general | solution.py:80
  56.0 1.1 %fusion.58 = f32[1560,128]{1,0:T(8,128)S(1)} fusion(bf16[780,1560]{1,0:T(8,128)(2,1)S(1)} %fusion.1, bf16[780,128]{1,0:T(8,128)(2,1)S(1)} %reshape.94), kind=kOutput, calls=%fused_computation.100 | convolution fusion | flops 311500800 | bytes 3432000 | tf_op jit(solution)/shard_map/dot_general | solution.py:77
  58.0 2.5 %collective-permute-start.4 = (bf16[780,256]{1,0:T(8,128)(2,1)}, bf16[780,256]{1,0:T(8,128)(2,1)}, u32[]{:S(2)}, u32[]{:S(2)}) collective-permute-start(bf16[780,256]{1,0:T(8,128)(2,1)} %fusion.11), channel_id=1, source_target_pairs={{0,8},{8,0},{16,24},{24,16},{32,40},{40,32},{48,56},{56,48},{64,72... | collective-permute-start | bytes 1198088 | tf_op jit(solution)/shard_map/ppermute | solution.py:34
  62.2 1.1 %fusion.10 = f32[780,256]{1,0:T(8,128)S(1)} fusion(f32[1560,128]{1,0:T(8,128)S(1)} %fusion.58, f32[1560,128]{1,0:T(8,128)S(1)} %fusion.5, bf16[780,256]{1,0:T(8,128)(2,1)} %collective-permute-done.4), kind=kLoop, calls=%fused_computation.15 | loop fusion | flops 599040 | bytes 2795520 | tf_op jit(solution)/shard_map/add | solution.py:142
  63.3 2.0 %select_convert_fusion.1 = (bf16[260,256]{1,0:T(8,128)(2,1)S(1)}, bf16[260,256]{1,0:T(8,128)(2,1)S(1)}, bf16[260,256]{1,0:T(8,128)(2,1)S(1)}) fusion(f32[780,256]{1,0:T(8,128)S(1)} %fusion.10, pred[]{:T(512)} %get-tuple-element.15, pred[]{:T(512)} %get-tuple-element.14, pred[]{:T(512)} %get-tuple-element.16), kind=kLoop, calls=%fused_computation.42 | loop fusion | flops 199680 | bytes 665603 | tf_op jit(solution)/shard_map/convert_element_type | solution.py:146
  65.3 4.2 %collective-permute-start.5 = (bf16[260,256]{1,0:T(8,128)(2,1)S(1)}, bf16[260,256]{1,0:T(8,128)(2,1)S(1)}, u32[]{:S(2)}, u32[]{:S(2)}) collective-permute-start(bf16[260,256]{1,0:T(8,128)(2,1)S(1)} %get-tuple-element.17), channel_id=1, source_target_pairs={{32,0},{40,8},{48,16},{56,24},{64,32},{72,40},{80,48},{88,56},{96,... | collective-permute-start | bytes 399368 | tf_op jit(solution)/shard_map/ppermute | solution.py:29
  69.5 7.6 %collective-permute-start.6 = (bf16[260,256]{1,0:T(8,128)(2,1)S(1)}, bf16[260,256]{1,0:T(8,128)(2,1)S(1)}, u32[]{:S(2)}, u32[]{:S(2)}) collective-permute-start(bf16[260,256]{1,0:T(8,128)(2,1)S(1)} %get-tuple-element.18), channel_id=1, source_target_pairs={{48,0},{56,8},{64,16},{72,24},{80,32},{88,40},{96,48},{104,56},{11... | collective-permute-start | bytes 399368 | tf_op jit(solution)/shard_map/ppermute | solution.py:29
  77.1 1.9 %collective-permute-start.7 = (bf16[260,256]{1,0:T(8,128)(2,1)S(1)}, bf16[260,256]{1,0:T(8,128)(2,1)S(1)}, u32[]{:S(2)}, u32[]{:S(2)}) collective-permute-start(bf16[260,256]{1,0:T(8,128)(2,1)S(1)} %get-tuple-element.19), channel_id=1, source_target_pairs={{16,0},{24,8},{32,16},{40,24},{48,32},{56,40},{64,48},{72,56},{80,... | collective-permute-start | bytes 399368 | tf_op jit(solution)/shard_map/ppermute | solution.py:29
  79.2 6.0 %collective-permute-done.6 = bf16[260,256]{1,0:T(8,128)(2,1)S(1)} collective-permute-done((bf16[260,256]{1,0:T(8,128)(2,1)S(1)}, bf16[260,256]{1,0:T(8,128)(2,1)S(1)}, u32[]{:S(2)}, u32[]{:S(2)}) %collective-permute-start.6) | collective-permute-done | bytes 133152 | tf_op jit(solution)/shard_map/ppermute | solution.py:29
  85.2 1.5 %collective-permute-done.7 = bf16[260,256]{1,0:T(8,128)(2,1)S(1)} collective-permute-done((bf16[260,256]{1,0:T(8,128)(2,1)S(1)}, bf16[260,256]{1,0:T(8,128)(2,1)S(1)}, u32[]{:S(2)}, u32[]{:S(2)}) %collective-permute-start.7) | collective-permute-done | bytes 133152 | tf_op jit(solution)/shard_map/ppermute | solution.py:29
  87.7 7.0 %all-to-all-start.1 = ((f32[8,3,260]{2,1,0:T(4,128)}), f32[8,3,260]{2,1,0:T(4,128)S(1)}, u32[]{:S(2)}, u32[]{:S(2)}) async-start(f32[8,3,260]{2,1,0:T(4,128)} %broadcast_in_dim.77), calls=%async_computation.1 | async-start | bytes 98304 | tf_op jit(solution)/shard_map/all_to_all | solution.py:23
  94.6 1.7 %reshape.95 = bf16[260,384]{1,0:T(8,128)(2,1)} reshape(bf16[780,128]{1,0:T(8,128)(2,1)} %get-tuple-element.21) | data formatting | bytes 399360 | tf_op jit(solution)/shard_map/reshape | solution.py:66
  97.6 3.3 %all-to-all-done.1 = f32[8,3,260]{2,1,0:T(4,128)S(1)} async-done(((f32[8,3,260]{2,1,0:T(4,128)}), f32[8,3,260]{2,1,0:T(4,128)S(1)}, u32[]{:S(2)}, u32[]{:S(2)}) %all-to-all-start.1) | async-done | bytes 24992 | tf_op jit(solution)/shard_map/all_to_all | solution.py:23
  (51 shorter events, 14.0 us)
Async XLA Ops:
  4.4 11.6 %all-to-all-start = ((f32[8,3,260]{2,1,0:T(4,128)}), f32[8,3,260]{2,1,0:T(4,128)S(1)}, u32[]{:S(2)}, u32[]{:S(2)}) async-start(f32[8,3,260]{2,1,0:T(4,128)} %broadcast_in_dim.74), calls=%async_computation | async-start | bytes 98304 | tf_op jit(solution)/shard_map/all_to_all | solution.py:23
  18.1 15.4 %collective-permute-start.1 = (bf16[260,256]{1,0:T(8,128)(2,1)S(1)}, bf16[260,256]{1,0:T(8,128)(2,1)S(1)}, u32[]{:S(2)}, u32[]{:S(2)}) collective-permute-start(bf16[260,256]{1,0:T(8,128)(2,1)S(1)} %pad_maximum_fusion.3), channel_id=1, source_target_pairs={{0,32},{8,40},{16,48},{24,56},{32,64},{40,72},{48,80},{56,88},{64,... | collective-permute-start | bytes 399368 | tf_op jit(solution)/shard_map/ppermute | solution.py:29
  23.1 12.9 %collective-permute-start.2 = (bf16[260,256]{1,0:T(8,128)(2,1)S(1)}, bf16[260,256]{1,0:T(8,128)(2,1)S(1)}, u32[]{:S(2)}, u32[]{:S(2)}) collective-permute-start(bf16[260,256]{1,0:T(8,128)(2,1)S(1)} %pad_maximum_fusion.3), channel_id=1, source_target_pairs={{0,48},{8,56},{16,64},{24,72},{32,80},{40,88},{48,96},{56,104},{64... | collective-permute-start | bytes 399368 | tf_op jit(solution)/shard_map/ppermute | solution.py:29
  29.6 8.3 %collective-permute-start = (bf16[260,256]{1,0:T(8,128)(2,1)S(1)}, bf16[260,256]{1,0:T(8,128)(2,1)S(1)}, u32[]{:S(2)}, u32[]{:S(2)}) collective-permute-start(bf16[260,256]{1,0:T(8,128)(2,1)S(1)} %pad_maximum_fusion.3), channel_id=1, source_target_pairs={{0,16},{8,24},{16,32},{24,40},{32,48},{40,56},{48,64},{56,72},{64,... | collective-permute-start | bytes 399368 | tf_op jit(solution)/shard_map/ppermute | solution.py:29
  38.8 7.1 %collective-permute-start.3 = (bf16[780,256]{1,0:T(8,128)(2,1)S(1)}, bf16[780,256]{1,0:T(8,128)(2,1)S(1)}, u32[]{:S(2)}, u32[]{:S(2)}) collective-permute-start(bf16[780,256]{1,0:T(8,128)(2,1)S(1)} %pad_maximum_fusion.1), channel_id=1, source_target_pairs={{0,8},{8,0},{16,24},{24,16},{32,40},{40,32},{48,56},{56,48},{64,72... | collective-permute-start | bytes 1198088 | tf_op jit(solution)/shard_map/ppermute | solution.py:34
  57.9 21.1 %copy-start = (bf16[260,384]{1,0:T(8,128)(2,1)S(1)}, bf16[260,384]{1,0:T(8,128)(2,1)}, u32[]{:S(2)}) copy-start(bf16[260,384]{1,0:T(8,128)(2,1)} %param.9) | copy-start | bytes 599044
  57.9 21.1 %copy-start.3 = (f32[384]{0:T(512)S(1)}, f32[384]{0:T(512)}, u32[]{:S(2)}) copy-start(f32[384]{0:T(512)} %param.14) | copy-start | bytes 4612
  57.9 28.8 %copy-start.1 = (bf16[260,128]{1,0:T(8,128)(2,1)S(1)}, bf16[260,128]{1,0:T(8,128)(2,1)}, u32[]{:S(2)}) copy-start(bf16[260,128]{1,0:T(8,128)(2,1)} %param.12) | copy-start | bytes 199684
  57.9 28.8 %copy-start.2 = (bf16[260,128]{1,0:T(8,128)(2,1)S(1)}, bf16[260,128]{1,0:T(8,128)(2,1)}, u32[]{:S(2)}) copy-start(bf16[260,128]{1,0:T(8,128)(2,1)} %param.10) | copy-start | bytes 199684
  58.0 28.8 %copy-start.4 = (f32[128]{0:T(128)S(1)}, f32[128]{0:T(128)}, u32[]{:S(2)}) copy-start(f32[128]{0:T(128)} %param.15) | copy-start | bytes 1540
  58.0 4.2 %collective-permute-start.4 = (bf16[780,256]{1,0:T(8,128)(2,1)}, bf16[780,256]{1,0:T(8,128)(2,1)}, u32[]{:S(2)}, u32[]{:S(2)}) collective-permute-start(bf16[780,256]{1,0:T(8,128)(2,1)} %fusion.11), channel_id=1, source_target_pairs={{0,8},{8,0},{16,24},{24,16},{32,40},{40,32},{48,56},{56,48},{64,72... | collective-permute-start | bytes 1198088 | tf_op jit(solution)/shard_map/ppermute | solution.py:34
  65.3 13.9 %collective-permute-start.5 = (bf16[260,256]{1,0:T(8,128)(2,1)S(1)}, bf16[260,256]{1,0:T(8,128)(2,1)S(1)}, u32[]{:S(2)}, u32[]{:S(2)}) collective-permute-start(bf16[260,256]{1,0:T(8,128)(2,1)S(1)} %get-tuple-element.17), channel_id=1, source_target_pairs={{32,0},{40,8},{48,16},{56,24},{64,32},{72,40},{80,48},{88,56},{96,... | collective-permute-start | bytes 399368 | tf_op jit(solution)/shard_map/ppermute | solution.py:29
  69.5 15.7 %collective-permute-start.6 = (bf16[260,256]{1,0:T(8,128)(2,1)S(1)}, bf16[260,256]{1,0:T(8,128)(2,1)S(1)}, u32[]{:S(2)}, u32[]{:S(2)}) collective-permute-start(bf16[260,256]{1,0:T(8,128)(2,1)S(1)} %get-tuple-element.18), channel_id=1, source_target_pairs={{48,0},{56,8},{64,16},{72,24},{80,32},{88,40},{96,48},{104,56},{11... | collective-permute-start | bytes 399368 | tf_op jit(solution)/shard_map/ppermute | solution.py:29
  77.1 9.7 %collective-permute-start.7 = (bf16[260,256]{1,0:T(8,128)(2,1)S(1)}, bf16[260,256]{1,0:T(8,128)(2,1)S(1)}, u32[]{:S(2)}, u32[]{:S(2)}) collective-permute-start(bf16[260,256]{1,0:T(8,128)(2,1)S(1)} %get-tuple-element.19), channel_id=1, source_target_pairs={{16,0},{24,8},{32,16},{40,24},{48,32},{56,40},{64,48},{72,56},{80,... | collective-permute-start | bytes 399368 | tf_op jit(solution)/shard_map/ppermute | solution.py:29
  87.7 13.3 %all-to-all-start.1 = ((f32[8,3,260]{2,1,0:T(4,128)}), f32[8,3,260]{2,1,0:T(4,128)S(1)}, u32[]{:S(2)}, u32[]{:S(2)}) async-start(f32[8,3,260]{2,1,0:T(4,128)} %broadcast_in_dim.77), calls=%async_computation.1 | async-start | bytes 98304 | tf_op jit(solution)/shard_map/all_to_all | solution.py:23

commit v2 on v1

v2 whole, which is shorter than its diff:
```python
import math

import jax
import jax.numpy as jnp
from jax import lax
from jax.experimental import pallas as pl
from jax.experimental.pallas import tpu as pltpu
from jax.sharding import PartitionSpec as P

HEAD_SIZE = 128
KEY_VALUE_HEADS = 8
GROUP = 3
STRETCH = 520
HQ = 24
EPSILON = 1e-06
HIDDEN = -1e30

PAD = 16
LANES = 128
F32 = jnp.float32
BF16 = jnp.bfloat16
SCORE_SCALE = HEAD_SIZE ** (-0.5)
LOG2E = math.log2(math.e)


def up(count, unit):
    return -(-count // unit) * unit


def shape(dims, kind):
    return jax.ShapeDtypeStruct(dims, kind)


def kernel_call(body, outs, flops, scratch=(), smem_first=False, nargs=0):
    specs = [pl.BlockSpec(memory_space=pltpu.VMEM)] * nargs
    if smem_first:
        specs[0] = pl.BlockSpec(memory_space=pltpu.SMEM)
    size = sum(math.prod(o.shape) * o.dtype.itemsize for o in jax.tree.leaves(outs))
    return pl.pallas_call(
        body,
        out_shape=outs,
        in_specs=specs,
        out_specs=jax.tree.map(lambda o: pl.BlockSpec(memory_space=pltpu.VMEM), outs),
        scratch_shapes=list(scratch),
        compiler_params=pltpu.CompilerParams(vmem_limit_bytes=40 * 2**20),
        cost_estimate=pl.CostEstimate(flops=flops, bytes_accessed=2 * size, transcendentals=0),
    )


def dot(a, b, ca, cb):
    return lax.dot_general(a, b, (((ca,), (cb,)), ((), ())), preferred_element_type=F32)


def halves(x):
    high = x.astype(BF16)
    return high, (x - high.astype(F32)).astype(BF16)


def to_lanes(x, row):
    pick = (lax.broadcasted_iota(jnp.int32, (8, x.shape[1]), 0) == row).astype(BF16)
    high, low = halves(x)
    return dot(pick, high, 1, 1) + dot(pick, low, 1, 1)


def to_rows(x):
    row = lax.broadcasted_iota(jnp.int32, (8, 3 * LANES), 0)
    group = lax.broadcasted_iota(jnp.int32, (8, 3 * LANES), 1) // LANES
    pick = (row == group).astype(BF16)
    high, low = halves(x)
    rows = dot(high, pick, 0, 0) + dot(low, pick, 0, 0)
    return [rows[:, i * LANES : (i + 1) * LANES] for i in range(3)]


def added(ref):
    total = ref[0]
    for i in range(1, ref.shape[0]):
        total = total + ref[i]
    return total


def inverses(ref):
    sums = to_rows(added(ref))
    widths = (HQ * HEAD_SIZE, KEY_VALUE_HEADS * HEAD_SIZE, KEY_VALUE_HEADS * HEAD_SIZE)
    return [lax.rsqrt(s / w + EPSILON) for s, w in zip(sums, widths)]


def squares_body(q_ref, k_ref, c_ref, out_ref):
    rows = None
    for i, ref in enumerate((q_ref, k_ref, c_ref)):
        x = ref[...].astype(F32)
        part = to_lanes(x * x, i)
        rows = part if rows is None else rows + part
    for peer in range(out_ref.shape[0]):
        out_ref[peer] = rows


def keys_body(sums_ref, k_ref, v_ref, c_ref, cv_ref, gain_ref, noisy_ref, clean_ref, wide):
    _, k_inv, c_inv = inverses(sums_ref)
    rows = k_ref.shape[0]
    wide[...] = jnp.zeros_like(wide)
    wide[0:rows, 0:LANES] = c_ref[...].astype(F32) * c_inv * gain_ref[...]
    wide[0:rows, LANES:] = cv_ref[...].astype(F32)
    clean_ref[...] = wide[...].astype(BF16)
    wide[0:rows, 0:LANES] = k_ref[...].astype(F32) * k_inv * gain_ref[...]
    wide[0:rows, LANES:] = v_ref[...].astype(F32)
    noisy_ref[...] = wide[...].astype(BF16)


def queries_body(sums_ref, q_ref, g_ref, gain_ref, q_out, gt_out, wide):
    q_inv, _, _ = inverses(sums_ref)
    rows = q_ref.shape[0]
    slot = up(rows, PAD)
    wide[...] = jnp.zeros_like(wide)
    for h in range(GROUP):
        cols = slice(h * HEAD_SIZE, (h + 1) * HEAD_SIZE)
        gain = gain_ref[:, cols] * (SCORE_SCALE * LOG2E)
        wide[h * slot : h * slot + rows, :] = q_ref[:, cols].astype(F32) * q_inv * gain
    q_out[...] = wide[...].astype(BF16)
    for h in range(GROUP):
        cols = slice(h * HEAD_SIZE, (h + 1) * HEAD_SIZE)
        wide[h * slot : h * slot + rows, :] = g_ref[:, cols].astype(F32)
    gt_out[...] = wide[...].T.astype(BF16)


def attend_body(
    hide_ref, q_ref, gt_ref, n0, p0, o0, n1, p1, o1,
    out_ref, dq_ref, own_n, own_c, far_n, far_c, s_ref, e_ref,
):
    rows = out_ref.shape[0]
    slot = n0.shape[0]
    whole = rows // PAD * PAD
    blocks = (n0, p0, o0, n1, p1, o1)
    q = q_ref[...]
    top = None
    for j, ref in enumerate(blocks):
        s = dot(ref[:, :LANES], q, 1, 1)
        if j % 3:
            s = s + hide_ref[j % 3 - 1]
        tail = s[whole:]
        real = lax.broadcasted_iota(jnp.int32, tail.shape, 0) < rows - whole
        tail = jnp.where(real, tail, HIDDEN)
        s_ref[j, 0:whole] = s[:whole]
        s_ref[j, whole:slot] = tail
        here = jnp.maximum(
            jnp.max(s[:whole], axis=0, keepdims=True), jnp.max(tail, axis=0, keepdims=True)
        )
        top = here if top is None else jnp.maximum(top, here)
    total = None
    out_t = None
    for j, ref in enumerate(blocks):
        e = jnp.exp2(s_ref[j] - top)
        part = jnp.sum(e, axis=0, keepdims=True)
        low = e.astype(BF16)
        e_ref[j] = low
        share = dot(ref[:, LANES:], low, 0, 0)
        total = part if total is None else total + part
        out_t = share if out_t is None else out_t + share
    inv = 1.0 / total
    out_t = out_t * inv
    gt = gt_ref[...].astype(F32)
    delta = jnp.sum(gt * out_t, axis=0, keepdims=True) * inv
    gt = gt * inv
    g = gt.T.astype(BF16)
    gt = gt.astype(BF16)
    out = out_t.T
    for h in range(GROUP):
        out_ref[:, h * HEAD_SIZE : (h + 1) * HEAD_SIZE] = out[
            h * slot : h * slot + rows
        ].astype(BF16)
    dq_t = None
    for j, ref in enumerate(blocks):
        low = e_ref[j]
        dp = dot(ref[:, LANES:], gt, 1, 0)
        ds = (low.astype(F32) * (dp - delta)).astype(BF16)
        dv = dot(low, g, 1, 0)[:rows]
        dk = dot(ds, q, 1, 0)[:rows] * (1.0 / LOG2E)
        share = dot(ref[:, :LANES], ds, 0, 0)
        dq_t = share if dq_t is None else dq_t + share
        if j == 0:
            own_n[:, :LANES] = dk
            own_n[:, LANES:] = dv
        elif j < 3:
            own_c[j - 1, :, :LANES] = dk
            own_c[j - 1, :, LANES:] = dv
        elif j == 3:
            far_n[:, :LANES] = dk.astype(BF16)
            far_n[:, LANES:] = dv.astype(BF16)
        else:
            far_c[j - 4, :, :LANES] = dk.astype(BF16)
            far_c[j - 4, :, LANES:] = dv.astype(BF16)
    dq = dq_t.T * SCORE_SCALE
    for h in range(GROUP):
        dq_ref[:, h * HEAD_SIZE : (h + 1) * HEAD_SIZE] = dq[h * slot : h * slot + rows]


def join_body(use_ref, own_ref, far_ref, back1, back2, back3):
    prev = own_ref[0] + far_ref[0].astype(F32)
    other = own_ref[1] + far_ref[1].astype(F32)
    back1[...] = (prev * use_ref[0]).astype(BF16)
    back2[...] = (other * use_ref[1]).astype(BF16)
    back3[...] = (other * use_ref[2]).astype(BF16)


def key_totals(own_n, far_n, r1, r2, r3):
    noisy = own_n[...] + far_n[...].astype(F32)
    clean = r1[...].astype(F32) + r2[...].astype(F32) + r3[...].astype(F32)
    return noisy, clean


def inner_body(
    q_ref, k_ref, c_ref, q_gain, k_gain, dq_ref, own_n, far_n, r1, r2, r3, out_ref
):
    noisy, clean = key_totals(own_n, far_n, r1, r2, r3)
    rows = to_lanes(dq_ref[...] * q_gain[...] * q_ref[...].astype(F32), 0)
    rows = rows + to_lanes(noisy[:, :LANES] * k_gain[...] * k_ref[...].astype(F32), 1)
    rows = rows + to_lanes(clean[:, :LANES] * k_gain[...] * c_ref[...].astype(F32), 2)
    for peer in range(out_ref.shape[0]):
        out_ref[peer] = rows


def finish_body(
    sums_ref, inner_ref, q_ref, k_ref, c_ref, q_gain, k_gain, dq_ref, own_n, far_n, r1, r2, r3,
    grad_q, grad_k, grad_v, grad_ck, grad_cv,
):
    q_inv, k_inv, c_inv = inverses(sums_ref)
    q_sum, k_sum, c_sum = to_rows(added(inner_ref))
    noisy, clean = key_totals(own_n, far_n, r1, r2, r3)
    q_pull = q_inv * q_inv * q_inv * (q_sum / (HQ * HEAD_SIZE))
    for h in range(GROUP):
        cols = slice(h * HEAD_SIZE, (h + 1) * HEAD_SIZE)
        grad_q[:, cols] = (
            q_inv * (dq_ref[:, cols] * q_gain[:, cols]) - q_ref[:, cols].astype(F32) * q_pull
        ).astype(BF16)
    width = KEY_VALUE_HEADS * HEAD_SIZE
    for inv, total, mean, ref, out in (
        (k_inv, noisy, k_sum, k_ref, grad_k),
        (c_inv, clean, c_sum, c_ref, grad_ck),
    ):
        pull = inv * inv * inv * (mean / width)
        out[...] = (
            inv * (total[:, :LANES] * k_gain[...]) - ref[...].astype(F32) * pull
        ).astype(BF16)
    grad_v[...] = noisy[:, LANES:].astype(BF16)
    grad_cv[...] = clean[:, LANES:].astype(BF16)


def head_exchange(value):
    return lax.all_to_all(value, "head", 0, 0)


def stretch_shift(value, steps):
    count = lax.axis_size("seq")
    pairs = [(i, i + 2 * steps) for i in range(count) if 0 <= i + 2 * steps < count]
    return lax.ppermute(value, "seq", pairs)


def core_swap(value):
    count = lax.axis_size("seq")
    return lax.ppermute(value, "seq", [(i, i ^ 1) for i in range(count)])


def on_device(
    noisy_q, noisy_k, noisy_value, clean_k, clean_value, q_gain, key_norm_gain, out_grad, window
):
    rows = noisy_q.shape[0]
    slot = up(rows, PAD)
    stack = up(GROUP * slot, LANES)
    peers = lax.axis_size("head")
    stretch_id = lax.axis_index("seq") // 2
    row_hit = jnp.arange(window.shape[0], dtype=jnp.int32)[:, None] == stretch_id
    listed = jnp.sum(jnp.where(row_hit, window, 0), axis=0)
    back = stretch_id - jnp.arange(1, 4, dtype=jnp.int32)
    use = jnp.any((listed[None, :] == back[:, None]) & (back[:, None] >= 0), axis=1)
    use_f = use.astype(F32)
    hide = jnp.where(jnp.stack([use[0], use[1] | use[2]]), 0.0, HIDDEN).astype(F32)
    q_gain = q_gain[None, :]
    k_gain = key_norm_gain[None, :]

    sums = kernel_call(squares_body, shape((peers, 8, rows), F32), 10**6, nargs=3)(
        noisy_q, noisy_k, clean_k
    )
    sums = head_exchange(sums)
    pack = shape((slot, 2 * LANES), BF16)
    noisy_kv, clean_kv = kernel_call(
        keys_body, (pack, pack), 10**6, [pltpu.VMEM((slot, 2 * LANES), F32)], nargs=6
    )(sums, noisy_k, noisy_value, clean_k, clean_value, k_gain)
    got = [stretch_shift(clean_kv, steps) for steps in (1, 2, 3)]
    q_norm, g_turned = kernel_call(
        queries_body,
        (shape((stack, LANES), BF16), shape((LANES, stack), BF16)),
        10**6,
        [pltpu.VMEM((stack, LANES), F32)],
        nargs=4,
    )(sums, noisy_q, out_grad, q_gain)
    noisy_far = core_swap(noisy_kv)
    prev_far = core_swap(got[0])
    other = jnp.where(use[1], got[1], got[2])
    other_far = core_swap(other)
    grad_low = shape((rows, 2 * LANES), BF16)
    attn_out, dq, own_n, own_c, far_n, far_c = kernel_call(
        attend_body,
        (
            shape((rows, GROUP * LANES), BF16),
            shape((rows, GROUP * LANES), F32),
            shape((rows, 2 * LANES), F32),
            shape((2, rows, 2 * LANES), F32),
            grad_low,
            shape((2, rows, 2 * LANES), BF16),
        ),
        12 * rows * GROUP * 6 * slot * LANES,
        [pltpu.VMEM((6, slot, stack), F32), pltpu.VMEM((6, slot, stack), BF16)],
        smem_first=True,
        nargs=9,
    )(hide, q_norm, g_turned, noisy_kv, got[0], other, noisy_far, prev_far, other_far)
    clean_far = core_swap(far_c)
    back1, back2, back3 = kernel_call(
        join_body, (grad_low, grad_low, grad_low), 10**6, smem_first=True, nargs=3
    )(use_f, own_c, clean_far)
    r2 = stretch_shift(back2, -2)
    r3 = stretch_shift(back3, -3)
    r1 = stretch_shift(back1, -1)
    far_n = core_swap(far_n)
    inner = kernel_call(inner_body, shape((peers, 8, rows), F32), 10**6, nargs=11)(
        noisy_q, noisy_k, clean_k, q_gain, k_gain, dq, own_n, far_n, r1, r2, r3
    )
    inner = head_exchange(inner)
    key_grad = shape((rows, LANES), BF16)
    grad_q, grad_k, grad_v, grad_ck, grad_cv = kernel_call(
        finish_body,
        (shape((rows, GROUP * LANES), BF16), key_grad, key_grad, key_grad, key_grad),
        10**6,
        nargs=13,
    )(sums, inner, noisy_q, noisy_k, clean_k, q_gain, k_gain, dq, own_n, far_n, r1, r2, r3)
    return (attn_out, grad_q, grad_k, grad_v, grad_ck, grad_cv)


def solution(mesh):
    tokens = P("seq", "head")
    return jax.shard_map(
        on_device,
        mesh=mesh,
        in_specs=(tokens,) * 5 + (P("head"), P("head"), tokens, P()),
        out_specs=(tokens,) * 6,
        check_vma=False,
    )
```

time: 104 us -> 94.7 us (0.911)
  the two profiles are of different devices: /device:TPU:336 before, /device:TPU:192 now
where the time goes in v2:
time: 94.7 us; the launch traced here: 94 us
  starting transfers between devices  40.3 us (43%)
  waiting for transfers between devices  24.7 us (26%)
  Pallas kernels  11.6 us (12%)
  blocking collectives  9.35 us (10%)
  local copies, waits for them, and re-layouts  3.98 us (4%)
  between operations  2.22 us (2%)
  other arithmetic  1.76 us (2%)
    ppermute x6, starting transfers between devices, stretch_shift(): return lax.ppermute(value, 'seq', pairs)  24.3 us
    ppermute x6, waiting for transfers between devices, stretch_shift(): return lax.ppermute(value, 'seq', pairs)  19.1 us
    ppermute x5, starting transfers between devices, core_swap(): return lax.ppermute(value, 'seq', [(i, i ^ 1) for i in range(count)])  10.6 us
    all_to_all x1, blocking collectives, head_exchange(): return lax.all_to_all(value, 'head', 0, 0)  9.35 us
    pallas_call x1, Pallas kernels, on_device(): kernel_call(attend_body, (shape((rows, GROUP * LANES), BF16), shape((rows...  7.54 us
    all_to_all x1, waiting for transfers between devices, head_exchange(): return lax.all_to_all(value, 'head', 0, 0)  5.61 us
    all_to_all x1, starting transfers between devices, head_exchange(): return lax.all_to_all(value, 'head', 0, 0)  5.44 us
    unnamed x24, local copies, waits for them, and re-layouts  3.39 us
  transfers between devices with their start and end apart: 12, of which 4 were waited for; matrix products, arithmetic and copies ran while one was open for 3% of the time, Pallas kernels for 1%

profile of v2, /device:TPU:192, one launch (start us, length us, event | category | flops | bytes accessed | tf_op | source)
XLA Modules:
  0.0 94.0 jit_solution(10403223494532172490)
XLA Ops:
  0.6 0.9 copy-done
  1.6 0.9 copy-done.2
  2.4 0.9 copy-done.4
  3.3 1.0 %shard_map.136 = f32[8,8,260]{2,1,0:T(8,128)} custom-call(bf16[260,384]{1,0:T(8,128)(2,1)S(1)} %copy-done, bf16[260,128]{1,0:T(8,128)(2,1)S(1)} %copy-done.2, bf16[260,128]{1,0:T(8,128)(2,1)S(1)} %copy-done.4), custom_call_target="tpu_custom_call" | custom-call | flops 1000000 | bytes 133120 | tf_op jit(solution)/shard_map/pallas_call | solution.py:279
  4.3 5.4 %all-to-all-start = ((f32[8,8,260]{2,1,0:T(8,128)}), f32[8,8,260]{2,1,0:T(8,128)S(1)}, u32[]{:S(2)}, u32[]{:S(2)}) async-start(f32[8,8,260]{2,1,0:T(8,128)} %shard_map.136), calls=%async_computation | async-start | bytes 196608 | tf_op jit(solution)/shard_map/all_to_all | solution.py:248
  9.8 0.7 copy-done.11
  10.6 5.6 %all-to-all-done.sums_ref = f32[8,8,260]{2,1,0:T(8,128)S(1)} async-done(((f32[8,8,260]{2,1,0:T(8,128)}), f32[8,8,260]{2,1,0:T(8,128)S(1)}, u32[]{:S(2)}, u32[]{:S(2)}) %all-to-all-start) | async-done | bytes 66592 | tf_op jit(solution)/shard_map/all_to_all | solution.py:248
  16.2 0.4 shard_map.138
  16.6 5.3 %collective-permute-start.2 = (bf16[272,256]{1,0:T(8,128)(2,1)S(1)}, bf16[272,256]{1,0:T(8,128)(2,1)S(1)}, u32[]{:S(2)}, u32[]{:S(2)}) collective-permute-start(bf16[272,256]{1,0:T(8,128)(2,1)S(1)} %get-tuple-element.27), channel_id=1, source_target_pairs={{0,48},{8,56},{16,64},{24,72},{32,80},{40,88},{48,96},{56,104},{64... | collective-permute-start | bytes 417800 | tf_op jit(solution)/shard_map/ppermute | solution.py:254
  21.9 7.7 %collective-permute-start.1 = (bf16[272,256]{1,0:T(8,128)(2,1)S(1)}, bf16[272,256]{1,0:T(8,128)(2,1)S(1)}, u32[]{:S(2)}, u32[]{:S(2)}) collective-permute-start(bf16[272,256]{1,0:T(8,128)(2,1)S(1)} %get-tuple-element.27), channel_id=1, source_target_pairs={{0,32},{8,40},{16,48},{24,56},{32,64},{40,72},{48,80},{56,88},{64,... | collective-permute-start | bytes 417800 | tf_op jit(solution)/shard_map/ppermute | solution.py:254
  29.6 0.2 and_reduce_fusion
  29.8 0.6 fusion
  30.4 3.6 %collective-permute-start = (bf16[272,256]{1,0:T(8,128)(2,1)S(1)}, bf16[272,256]{1,0:T(8,128)(2,1)S(1)}, u32[]{:S(2)}, u32[]{:S(2)}) collective-permute-start(bf16[272,256]{1,0:T(8,128)(2,1)S(1)} %get-tuple-element.27), channel_id=1, source_target_pairs={{0,16},{8,24},{16,32},{24,40},{32,48},{40,56},{48,64},{56,72},{64,... | collective-permute-start | bytes 417800 | tf_op jit(solution)/shard_map/ppermute | solution.py:254
  34.0 1.9 %collective-permute-start.3 = (bf16[272,256]{1,0:T(8,128)(2,1)S(1)}, bf16[272,256]{1,0:T(8,128)(2,1)S(1)}, u32[]{:S(2)}, u32[]{:S(2)}) collective-permute-start(bf16[272,256]{1,0:T(8,128)(2,1)S(1)} %get-tuple-element.26.n0), channel_id=1, source_target_pairs={{0,8},{8,0},{16,24},{24,16},{32,40},{40,32},{48,56},{56,48},{64,72... | collective-permute-start | bytes 417800 | tf_op jit(solution)/shard_map/ppermute | solution.py:259
  36.0 0.7 broadcast_select_fusion.o0
  36.7 2.4 %collective-permute-start.5 = (bf16[272,256]{1,0:T(8,128)(2,1)S(1)}, bf16[272,256]{1,0:T(8,128)(2,1)S(1)}, u32[]{:S(2)}, u32[]{:S(2)}) collective-permute-start(bf16[272,256]{1,0:T(8,128)(2,1)S(1)} %broadcast_select_fusion.o0), channel_id=1, source_target_pairs={{0,8},{8,0},{16,24},{24,16},{32,40},{40,32},{48,56},{56,48},{64,72... | collective-permute-start | bytes 417800 | tf_op jit(solution)/shard_map/ppermute | solution.py:259
  39.1 4.1 %collective-permute-done.p0 = bf16[272,256]{1,0:T(8,128)(2,1)S(1)} collective-permute-done((bf16[272,256]{1,0:T(8,128)(2,1)S(1)}, bf16[272,256]{1,0:T(8,128)(2,1)S(1)}, u32[]{:S(2)}, u32[]{:S(2)}) %collective-permute-start) | collective-permute-done | bytes 139296 | tf_op jit(solution)/shard_map/ppermute | solution.py:254
  43.2 1.9 %collective-permute-start.4 = (bf16[272,256]{1,0:T(8,128)(2,1)S(1)}, bf16[272,256]{1,0:T(8,128)(2,1)S(1)}, u32[]{:S(2)}, u32[]{:S(2)}) collective-permute-start(bf16[272,256]{1,0:T(8,128)(2,1)S(1)} %collective-permute-done.p0), channel_id=1, source_target_pairs={{0,8},{8,0},{16,24},{24,16},{32,40},{40,32},{48,56},{56,48},{64,72... | collective-permute-start | bytes 417800 | tf_op jit(solution)/shard_map/ppermute | solution.py:259
  46.4 0.7 add_select_fusion.hide_ref
  47.2 0.4 shard_map.137
  47.6 7.5 %shard_map.139 = (bf16[260,384]{1,0:T(8,128)(2,1)}, f32[260,384]{1,0:T(8,128)S(1)}, f32[260,256]{1,0:T(8,128)S(1)}, f32[2,260,256]{2,1,0:T(8,128)S(1)}, bf16[260...) custom-call(f32[2]{0:T(128)S(1)} %add_select_fusion.hide_ref, bf16[896,128]{1,0:T(8,128)(2,1)S(1)} %get-tuple-element.24.q_ref, ...), custom_call_target="tpu_custom_call" | custom-call | flops 1955266560 | bytes 3594240 | tf_op jit(solution)/shard_map/pallas_call | solution.py:300
  55.2 2.4 %collective-permute-start.7 = (bf16[2,260,256]{2,1,0:T(8,128)(2,1)S(1)}, bf16[2,260,256]{2,1,0:T(8,128)(2,1)S(1)}, u32[]{:S(2)}, u32[]{:S(2)}) collective-permute-start(bf16[2,260,256]{2,1,0:T(8,128)(2,1)S(1)} %get-tuple-element.33), channel_id=1, source_target_pairs={{0,8},{8,0},{16,24},{24,16},{32,40},{40,32},{48,56},{56,48},{64,72... | collective-permute-start | bytes 798728 | tf_op jit(solution)/shard_map/ppermute | solution.py:259
  57.6 1.9 %collective-permute-start.6 = (bf16[260,256]{1,0:T(8,128)(2,1)S(1)}, bf16[260,256]{1,0:T(8,128)(2,1)S(1)}, u32[]{:S(2)}, u32[]{:S(2)}) collective-permute-start(bf16[260,256]{1,0:T(8,128)(2,1)S(1)} %get-tuple-element.31), channel_id=1, source_target_pairs={{0,8},{8,0},{16,24},{24,16},{32,40},{40,32},{48,56},{56,48},{64,72... | collective-permute-start | bytes 399368 | tf_op jit(solution)/shard_map/ppermute | solution.py:259
  59.5 0.6 shard_map.140
  60.2 1.9 %collective-permute-start.8 = (bf16[260,256]{1,0:T(8,128)(2,1)S(1)}, bf16[260,256]{1,0:T(8,128)(2,1)S(1)}, u32[]{:S(2)}, u32[]{:S(2)}) collective-permute-start(bf16[260,256]{1,0:T(8,128)(2,1)S(1)} %get-tuple-element.34), channel_id=1, source_target_pairs={{16,0},{24,8},{32,16},{40,24},{48,32},{56,40},{64,48},{72,56},{80,... | collective-permute-start | bytes 399368 | tf_op jit(solution)/shard_map/ppermute | solution.py:254
  62.1 3.9 %collective-permute-start.9 = (bf16[260,256]{1,0:T(8,128)(2,1)S(1)}, bf16[260,256]{1,0:T(8,128)(2,1)S(1)}, u32[]{:S(2)}, u32[]{:S(2)}) collective-permute-start(bf16[260,256]{1,0:T(8,128)(2,1)S(1)} %get-tuple-element.35), channel_id=1, source_target_pairs={{32,0},{40,8},{48,16},{56,24},{64,32},{72,40},{80,48},{88,56},{96,... | collective-permute-start | bytes 399368 | tf_op jit(solution)/shard_map/ppermute | solution.py:254
  66.0 1.9 %collective-permute-start.10 = (bf16[260,256]{1,0:T(8,128)(2,1)S(1)}, bf16[260,256]{1,0:T(8,128)(2,1)S(1)}, u32[]{:S(2)}, u32[]{:S(2)}) collective-permute-start(bf16[260,256]{1,0:T(8,128)(2,1)S(1)} %get-tuple-element.36), channel_id=1, source_target_pairs={{48,0},{56,8},{64,16},{72,24},{80,32},{88,40},{96,48},{104,56},{11... | collective-permute-start | bytes 399368 | tf_op jit(solution)/shard_map/ppermute | solution.py:254
  68.0 9.4 %collective-permute-done.8.r1 = bf16[260,256]{1,0:T(8,128)(2,1)S(1)} collective-permute-done((bf16[260,256]{1,0:T(8,128)(2,1)S(1)}, bf16[260,256]{1,0:T(8,128)(2,1)S(1)}, u32[]{:S(2)}, u32[]{:S(2)}) %collective-permute-start.8) | collective-permute-done | bytes 133152 | tf_op jit(solution)/shard_map/ppermute | solution.py:254
  77.3 5.6 %collective-permute-done.10.r3 = bf16[260,256]{1,0:T(8,128)(2,1)S(1)} collective-permute-done((bf16[260,256]{1,0:T(8,128)(2,1)S(1)}, bf16[260,256]{1,0:T(8,128)(2,1)S(1)}, u32[]{:S(2)}, u32[]{:S(2)}) %collective-permute-start.10) | collective-permute-done | bytes 133152 | tf_op jit(solution)/shard_map/ppermute | solution.py:254
  82.9 0.3 shard_map.141
  83.3 9.3 %all_to_all.10.inner_ref = f32[8,8,260]{2,1,0:T(8,128)S(1)} all-to-all(f32[8,8,260]{2,1,0:T(8,128)S(1)} %shard_map.141), channel_id=1, replica_groups=mesh['seq'=64,'head'=8] {'head'}, dimensions={0} | all-to-all | bytes 133120 | tf_op jit(solution)/shard_map/all_to_all | solution.py:248
  92.6 1.3 %shard_map.142 = (bf16[260,384]{1,0:T(8,128)(2,1)}, bf16[260,128]{1,0:T(8,128)(2,1)}, bf16[260,128]{1,0:T(8,128)(2,1)}, bf16[260,128]{1,0:T(8,128)(2,1)}, bf16[260,128]{1,0:T(8,128)(2,1)}) custom-call(f32[8,8,260]{2,1,0:T(8,128)S(1)} %all-to-all-done.sums_ref, f32[8,8,260]{2,1,0:T(8,128)S(1)} %all_to_all.10.inner_ref, bf16[260,384]{1,0:T(8,128)(2,1)S(1)} %copy-done.1, ...), custom_call_target="tpu_custom_call" | custom-call | flops 1000000 | bytes 931840 | tf_op jit(solution)/shard_map/pallas_call | solution.py:328
  (34 shorter events, 0.2 us)
Async XLA Ops:
  0.6 0.9 copy-start
  1.6 0.9 copy-start.2
  2.4 0.9 copy-start.4
  3.3 12.9 %copy-start.8 = (bf16[260,128]{1,0:T(8,128)(2,1)S(1)}, bf16[260,128]{1,0:T(8,128)(2,1)}, u32[]{:S(2)}) copy-start(bf16[260,128]{1,0:T(8,128)(2,1)} %cv_ref.1) | copy-start | bytes 199684
  4.3 11.9 %copy-start.3 = (bf16[260,128]{1,0:T(8,128)(2,1)S(1)}, bf16[260,128]{1,0:T(8,128)(2,1)}, u32[]{:S(2)}) copy-start(bf16[260,128]{1,0:T(8,128)(2,1)} %k_ref.7) | copy-start | bytes 199684
  4.3 11.9 %copy-start.5 = (bf16[260,128]{1,0:T(8,128)(2,1)S(1)}, bf16[260,128]{1,0:T(8,128)(2,1)}, u32[]{:S(2)}) copy-start(bf16[260,128]{1,0:T(8,128)(2,1)} %c_ref.7) | copy-start | bytes 199684
  4.3 11.9 %copy-start.7 = (bf16[260,128]{1,0:T(8,128)(2,1)S(1)}, bf16[260,128]{1,0:T(8,128)(2,1)}, u32[]{:S(2)}) copy-start(bf16[260,128]{1,0:T(8,128)(2,1)} %v_ref.1) | copy-start | bytes 199684
  4.3 11.9 %all-to-all-start = ((f32[8,8,260]{2,1,0:T(8,128)}), f32[8,8,260]{2,1,0:T(8,128)S(1)}, u32[]{:S(2)}, u32[]{:S(2)}) async-start(f32[8,8,260]{2,1,0:T(8,128)} %shard_map.136), calls=%async_computation | async-start | bytes 196608 | tf_op jit(solution)/shard_map/all_to_all | solution.py:248
  9.8 0.7 copy-start.11
  10.6 5.6 %copy-start.9 = (f32[128]{0:T(128)S(1)}, f32[128]{0:T(128)}, u32[]{:S(2)}) copy-start(f32[128]{0:T(128)} %param.15) | copy-start | bytes 1540
  16.6 19.3 %collective-permute-start.2 = (bf16[272,256]{1,0:T(8,128)(2,1)S(1)}, bf16[272,256]{1,0:T(8,128)(2,1)S(1)}, u32[]{:S(2)}, u32[]{:S(2)}) collective-permute-start(bf16[272,256]{1,0:T(8,128)(2,1)S(1)} %get-tuple-element.27), channel_id=1, source_target_pairs={{0,48},{8,56},{16,64},{24,72},{32,80},{40,88},{48,96},{56,104},{64... | collective-permute-start | bytes 417800 | tf_op jit(solution)/shard_map/ppermute | solution.py:254
  21.9 14.1 %collective-permute-start.1 = (bf16[272,256]{1,0:T(8,128)(2,1)S(1)}, bf16[272,256]{1,0:T(8,128)(2,1)S(1)}, u32[]{:S(2)}, u32[]{:S(2)}) collective-permute-start(bf16[272,256]{1,0:T(8,128)(2,1)S(1)} %get-tuple-element.27), channel_id=1, source_target_pairs={{0,32},{8,40},{16,48},{24,56},{32,64},{40,72},{48,80},{56,88},{64,... | collective-permute-start | bytes 417800 | tf_op jit(solution)/shard_map/ppermute | solution.py:254
  30.4 12.8 %collective-permute-start = (bf16[272,256]{1,0:T(8,128)(2,1)S(1)}, bf16[272,256]{1,0:T(8,128)(2,1)S(1)}, u32[]{:S(2)}, u32[]{:S(2)}) collective-permute-start(bf16[272,256]{1,0:T(8,128)(2,1)S(1)} %get-tuple-element.27), channel_id=1, source_target_pairs={{0,16},{8,24},{16,32},{24,40},{32,48},{40,56},{48,64},{56,72},{64,... | collective-permute-start | bytes 417800 | tf_op jit(solution)/shard_map/ppermute | solution.py:254
  34.0 13.6 %collective-permute-start.3 = (bf16[272,256]{1,0:T(8,128)(2,1)S(1)}, bf16[272,256]{1,0:T(8,128)(2,1)S(1)}, u32[]{:S(2)}, u32[]{:S(2)}) collective-permute-start(bf16[272,256]{1,0:T(8,128)(2,1)S(1)} %get-tuple-element.26.n0), channel_id=1, source_target_pairs={{0,8},{8,0},{16,24},{24,16},{32,40},{40,32},{48,56},{56,48},{64,72... | collective-permute-start | bytes 417800 | tf_op jit(solution)/shard_map/ppermute | solution.py:259
  35.9 11.2 %copy-start.1 = (bf16[260,384]{1,0:T(8,128)(2,1)S(1)}, bf16[260,384]{1,0:T(8,128)(2,1)}, u32[]{:S(2)}) copy-start(bf16[260,384]{1,0:T(8,128)(2,1)} %q_ref.7) | copy-start | bytes 599044
  35.9 11.2 %copy-start.6 = (bf16[260,384]{1,0:T(8,128)(2,1)S(1)}, bf16[260,384]{1,0:T(8,128)(2,1)}, u32[]{:S(2)}) copy-start(bf16[260,384]{1,0:T(8,128)(2,1)} %g_ref.1) | copy-start | bytes 599044
  36.7 10.9 %collective-permute-start.5 = (bf16[272,256]{1,0:T(8,128)(2,1)S(1)}, bf16[272,256]{1,0:T(8,128)(2,1)S(1)}, u32[]{:S(2)}, u32[]{:S(2)}) collective-permute-start(bf16[272,256]{1,0:T(8,128)(2,1)S(1)} %broadcast_select_fusion.o0), channel_id=1, source_target_pairs={{0,8},{8,0},{16,24},{24,16},{32,40},{40,32},{48,56},{56,48},{64,72... | collective-permute-start | bytes 417800 | tf_op jit(solution)/shard_map/ppermute | solution.py:259
  43.2 4.4 %collective-permute-start.4 = (bf16[272,256]{1,0:T(8,128)(2,1)S(1)}, bf16[272,256]{1,0:T(8,128)(2,1)S(1)}, u32[]{:S(2)}, u32[]{:S(2)}) collective-permute-start(bf16[272,256]{1,0:T(8,128)(2,1)S(1)} %collective-permute-done.p0), channel_id=1, source_target_pairs={{0,8},{8,0},{16,24},{24,16},{32,40},{40,32},{48,56},{56,48},{64,72... | collective-permute-start | bytes 417800 | tf_op jit(solution)/shard_map/ppermute | solution.py:259
  45.1 1.3 %copy-start.10 = (f32[384]{0:T(512)S(1)}, f32[384]{0:T(512)}, u32[]{:S(2)}) copy-start(f32[384]{0:T(512)} %param.14) | copy-start | bytes 4612
  55.2 4.3 %collective-permute-start.7 = (bf16[2,260,256]{2,1,0:T(8,128)(2,1)S(1)}, bf16[2,260,256]{2,1,0:T(8,128)(2,1)S(1)}, u32[]{:S(2)}, u32[]{:S(2)}) collective-permute-start(bf16[2,260,256]{2,1,0:T(8,128)(2,1)S(1)} %get-tuple-element.33), channel_id=1, source_target_pairs={{0,8},{8,0},{16,24},{24,16},{32,40},{40,32},{48,56},{56,48},{64,72... | collective-permute-start | bytes 798728 | tf_op jit(solution)/shard_map/ppermute | solution.py:259
  57.6 10.3 %collective-permute-start.6 = (bf16[260,256]{1,0:T(8,128)(2,1)S(1)}, bf16[260,256]{1,0:T(8,128)(2,1)S(1)}, u32[]{:S(2)}, u32[]{:S(2)}) collective-permute-start(bf16[260,256]{1,0:T(8,128)(2,1)S(1)} %get-tuple-element.31), channel_id=1, source_target_pairs={{0,8},{8,0},{16,24},{24,16},{32,40},{40,32},{48,56},{56,48},{64,72... | collective-permute-start | bytes 399368 | tf_op jit(solution)/shard_map/ppermute | solution.py:259
  60.2 17.1 %collective-permute-start.8 = (bf16[260,256]{1,0:T(8,128)(2,1)S(1)}, bf16[260,256]{1,0:T(8,128)(2,1)S(1)}, u32[]{:S(2)}, u32[]{:S(2)}) collective-permute-start(bf16[260,256]{1,0:T(8,128)(2,1)S(1)} %get-tuple-element.34), channel_id=1, source_target_pairs={{16,0},{24,8},{32,16},{40,24},{48,32},{56,40},{64,48},{72,56},{80,... | collective-permute-start | bytes 399368 | tf_op jit(solution)/shard_map/ppermute | solution.py:254
  62.1 15.2 %collective-permute-start.9 = (bf16[260,256]{1,0:T(8,128)(2,1)S(1)}, bf16[260,256]{1,0:T(8,128)(2,1)S(1)}, u32[]{:S(2)}, u32[]{:S(2)}) collective-permute-start(bf16[260,256]{1,0:T(8,128)(2,1)S(1)} %get-tuple-element.35), channel_id=1, source_target_pairs={{32,0},{40,8},{48,16},{56,24},{64,32},{72,40},{80,48},{88,56},{96,... | collective-permute-start | bytes 399368 | tf_op jit(solution)/shard_map/ppermute | solution.py:254
  66.0 16.9 %collective-permute-start.10 = (bf16[260,256]{1,0:T(8,128)(2,1)S(1)}, bf16[260,256]{1,0:T(8,128)(2,1)S(1)}, u32[]{:S(2)}, u32[]{:S(2)}) collective-permute-start(bf16[260,256]{1,0:T(8,128)(2,1)S(1)} %get-tuple-element.36), channel_id=1, source_target_pairs={{48,0},{56,8},{64,16},{72,24},{80,32},{88,40},{96,48},{104,56},{11... | collective-permute-start | bytes 399368 | tf_op jit(solution)/shard_map/ppermute | solution.py:254

commit v3 on v2

v3 whole, which is shorter than its diff:
```python
import math

import jax
import jax.numpy as jnp
from jax import lax
from jax.experimental import pallas as pl
from jax.experimental.pallas import tpu as pltpu
from jax.sharding import PartitionSpec as P

HEAD_SIZE = 128
KEY_VALUE_HEADS = 8
GROUP = 3
STRETCH = 520
HQ = 24
TOKENS = STRETCH // 2
EPSILON = 1e-06
HIDDEN = -1e30

PAD = 16
LANES = 128
F32 = jnp.float32
BF16 = jnp.bfloat16
SCORE_SCALE = HEAD_SIZE ** (-0.5)
LOG2E = math.log2(math.e)


def up(count, unit):
    return -(-count // unit) * unit


def shape(dims, kind):
    return jax.ShapeDtypeStruct(dims, kind)


def kernel_call(body, outs, flops, scratch=(), smem=(), nargs=0):
    specs = [pl.BlockSpec(memory_space=pltpu.SMEM if i in smem else pltpu.VMEM) for i in range(nargs)]
    size = sum(math.prod(o.shape) * o.dtype.itemsize for o in jax.tree.leaves(outs))
    return pl.pallas_call(
        body,
        out_shape=outs,
        in_specs=specs,
        out_specs=jax.tree.map(lambda o: pl.BlockSpec(memory_space=pltpu.VMEM), outs),
        scratch_shapes=list(scratch),
        compiler_params=pltpu.CompilerParams(vmem_limit_bytes=32 * 2**20),
        cost_estimate=pl.CostEstimate(flops=flops, bytes_accessed=size, transcendentals=0),
    )


def dot(a, b, ca, cb):
    return lax.dot_general(a, b, (((ca,), (cb,)), ((), ())), preferred_element_type=F32)


def halves(x):
    high = x.astype(BF16)
    return high, (x - high.astype(F32)).astype(BF16)


def to_lanes(x, row):
    pick = (lax.broadcasted_iota(jnp.int32, (8, x.shape[1]), 0) == row).astype(BF16)
    high, low = halves(x)
    return dot(pick, high, 1, 1) + dot(pick, low, 1, 1)


def to_rows(x):
    row = lax.broadcasted_iota(jnp.int32, (8, 3 * LANES), 0)
    group = lax.broadcasted_iota(jnp.int32, (8, 3 * LANES), 1) // LANES
    pick = (row == group).astype(BF16)
    high, low = halves(x)
    rows = dot(high, pick, 0, 0) + dot(low, pick, 0, 0)
    return [rows[:, i * LANES : (i + 1) * LANES] for i in range(3)]


def added(ref):
    total = ref[0]
    for i in range(1, ref.shape[0]):
        total = total + ref[i]
    return total


def inverses(ref):
    sums = to_rows(added(ref))
    widths = (HQ * HEAD_SIZE, KEY_VALUE_HEADS * HEAD_SIZE, KEY_VALUE_HEADS * HEAD_SIZE)
    return [lax.rsqrt(s / w + EPSILON) for s, w in zip(sums, widths)]


def squares_body(q_ref, k_ref, c_ref, out_ref):
    rows = None
    for i, ref in enumerate((q_ref, k_ref, c_ref)):
        x = ref[...].astype(F32)
        part = to_lanes(x * x, i)
        rows = part if rows is None else rows + part
    for peer in range(out_ref.shape[0]):
        out_ref[peer] = rows


def norms_body(
    sums_ref, q_ref, k_ref, c_ref, v_ref, cv_ref, g_ref, q_gain, k_gain,
    noisy_ref, clean_ref, out, wide, tall,
):
    q_inv, k_inv, c_inv = inverses(sums_ref)
    rows = k_ref.shape[0]
    slot = up(rows, PAD)
    wide[rows:] = jnp.zeros((slot - rows, 2 * LANES), F32)
    wide[0:rows, 0:LANES] = c_ref[...].astype(F32) * c_inv * k_gain[...]
    wide[0:rows, LANES:] = cv_ref[...].astype(F32)
    clean_ref[...] = wide[...].astype(BF16)
    wide[0:rows, 0:LANES] = k_ref[...].astype(F32) * k_inv * k_gain[...]
    wide[0:rows, LANES:] = v_ref[...].astype(F32)
    noisy_ref[...] = wide[...].astype(BF16)
    for h in range(2 * GROUP):
        tall[h * slot + rows : (h + 1) * slot] = jnp.zeros((slot - rows, LANES), F32)
    for h in range(GROUP):
        cols = slice(h * HEAD_SIZE, (h + 1) * HEAD_SIZE)
        gain = q_gain[:, cols] * (SCORE_SCALE * LOG2E)
        tall[h * slot : h * slot + rows, :] = q_ref[:, cols].astype(F32) * q_inv * gain
        at = (GROUP + h) * slot
        tall[at : at + rows, :] = g_ref[:, cols].astype(F32)
    out[...] = tall[...].astype(BF16)


def both(out, own, far, first, span):
    core = lax.axis_index("seq") % 2

    @pl.when(core == 0)
    def _():
        out[0:span] = own[first : first + span]
        out[span : 2 * span] = far[first : first + span]

    @pl.when(core == 1)
    def _():
        out[0:span] = far[first : first + span]
        out[span : 2 * span] = own[first : first + span]

    out[2 * span :] = jnp.zeros((out.shape[0] - 2 * span, out.shape[1]), out.dtype)


def listed(window_ref):
    here = lax.axis_index("seq") // 2
    found = []
    for steps in (1, 2, 3):
        at = here - steps
        hit = window_ref[here, 0] == at
        for j in range(1, window_ref.shape[1]):
            hit = hit | (window_ref[here, j] == at)
        found.append(hit & (at >= 0))
    return found


def scores(key_ref, q, rows):
    whole = rows // PAD * PAD
    s = dot(key_ref[:, :LANES], q, 1, 1)
    tail = s[whole:]
    real = lax.broadcasted_iota(jnp.int32, tail.shape, 0) < rows - whole
    return s[:whole], jnp.where(real, tail, HIDDEN)


def noisy_body(own, far, keys, q_out, gt_out, e_out, sum_out, stats, g_rows):
    span = own.shape[0] // 2
    both(q_out, own, far, 0, span)
    both(g_rows, own, far, span, span)
    gt = g_rows[...].astype(F32).T
    gt_out[...] = gt.astype(BF16)
    body, tail = scores(keys, q_out[...], TOKENS)
    whole = body.shape[0]
    top = jnp.maximum(
        jnp.max(body, axis=0, keepdims=True), jnp.max(tail, axis=0, keepdims=True)
    )
    body = jnp.exp2(body - top)
    tail = jnp.exp2(tail - top)
    total = jnp.sum(body, axis=0, keepdims=True) + jnp.sum(tail, axis=0, keepdims=True)
    e_out[0:whole] = body.astype(BF16)
    e_out[whole:] = tail.astype(BF16)
    sums = dot(keys[:, LANES:], e_out[...], 0, 0)
    sum_out[...] = sums
    stats[...] = jnp.zeros_like(stats)
    stats[0:1] = top
    stats[1:2] = total
    stats[2:3] = jnp.sum(gt * sums, axis=0, keepdims=True)


def clean_body(
    window_ref, got1, got2, got3, q_ref, gt_ref, noisy_stats, other, e_out, sum_out, stats, s_ref
):
    use1, use2, use3 = listed(window_ref)

    @pl.when(use2)
    def _():
        other[...] = got2[...]

    @pl.when(jnp.logical_not(use2))
    def _():
        other[...] = got3[...]

    q = q_ref[...]
    top = None
    for j, (ref, use) in enumerate(((got1, use1), (other, use2 | use3))):
        hide = jnp.where(use, 0.0, HIDDEN)
        body, tail = scores(ref, q, TOKENS)
        whole = body.shape[0]
        body = body + hide
        s_ref[j, 0:whole] = body
        s_ref[j, whole:] = tail
        here = jnp.maximum(
            jnp.max(body, axis=0, keepdims=True),
            jnp.max(tail + hide, axis=0, keepdims=True),
        )
        top = here if top is None else jnp.maximum(top, here)
        s_ref[j, whole:] = tail + hide
    total = None
    sums = None
    for j, ref in enumerate((got1, other)):
        e = jnp.exp2(s_ref[j] - top)
        part = jnp.sum(e, axis=0, keepdims=True)
        low = e.astype(BF16)
        e_out[j] = low
        share = dot(ref[:, LANES:], low, 0, 0)
        total = part if total is None else total + part
        sums = share if sums is None else sums + share
    sum_out[...] = sums
    stats[...] = noisy_stats[...]
    stats[3:4] = top
    stats[4:5] = total
    stats[5:6] = jnp.sum(gt_ref[...].astype(F32) * sums, axis=0, keepdims=True)


def key_grads(key_ref, e, gt, g, delta, q):
    dp = dot(key_ref[:, LANES:], gt, 1, 0)
    ds = (e.astype(F32) * (dp - delta)).astype(BF16)
    dv = dot(e, g, 1, 0)
    dk = dot(ds, q, 1, 0) * (1.0 / LOG2E)
    return ds, dk, dv


def clean_grad_body(
    window_ref, own, far, q_ref, gt_ref, got1, other, e_ref, back1, back2, back3, ds_out, merged
):
    use1, use2, use3 = listed(window_ref)
    groups = [(ref[i : i + 1], ref[i + 1 : i + 2], ref[i + 2 : i + 3])
              for ref in (own, far) for i in (0, 3)]
    top = groups[0][0]
    for group in groups[1:]:
        top = jnp.maximum(top, group[0])
    weights = [jnp.exp2(group[0] - top) for group in groups]
    inv = 1.0 / sum(w * group[1] for w, group in zip(weights, groups))
    delta = sum(w * group[2] for w, group in zip(weights, groups)) * inv
    noisy, clean = weights[0] * inv, weights[1] * inv
    merged[...] = jnp.zeros_like(merged)
    merged[0:1] = noisy
    merged[1:2] = clean
    merged[2:3] = delta * noisy
    gt = gt_ref[...].astype(F32) * clean
    g = gt.T.astype(BF16)
    gt = gt.astype(BF16)
    q = q_ref[...]
    rows = back1.shape[0]
    for j, (ref, outs) in enumerate(
        ((other, ((back2, use2), (back3, use3))), (got1, ((back1, use1),)))
    ):
        at = 1 - j
        ds, dk, dv = key_grads(ref, e_ref[at], gt, g, delta * clean, q)
        ds_out[at] = ds
        for out, use in outs:
            keep = jnp.where(use, 1.0, 0.0)
            out[:, :LANES] = (dk[:rows] * keep).astype(BF16)
            out[:, LANES:] = (dv[:rows] * keep).astype(BF16)


def noisy_grad_body(
    merged, q_ref, gt_ref, keys, got1, other, e_ref, ds_ref, noisy_sum, clean_sum,
    grads, own, far, wide,
):
    core = lax.axis_index("seq") % 2
    span = own.shape[0] // 2
    mine = pl.ds(pl.multiple_of(core * span, 8), span)
    theirs = pl.ds(pl.multiple_of((1 - core) * span, 8), span)
    noisy = merged[0:1]
    gt = gt_ref[...].astype(F32) * noisy
    g = gt.T.astype(BF16)
    ds, dk, dv = key_grads(keys, e_ref[...], gt.astype(BF16), g, merged[2:3], q_ref[...])
    rows = grads.shape[0]
    grads[:, :LANES] = dk[:rows]
    grads[:, LANES:] = dv[:rows]
    dq = dot(keys[:, :LANES], ds, 0, 0)
    dq = dq + dot(got1[:, :LANES], ds_ref[0], 0, 0)
    dq = dq + dot(other[:, :LANES], ds_ref[1], 0, 0)
    wide[0] = (noisy_sum[...] * noisy + clean_sum[...] * merged[1:2]).T
    wide[1] = (dq * SCORE_SCALE).T
    for i in range(2):
        own[i * span : (i + 1) * span] = wide[i, mine]
        far[i * span : (i + 1) * span] = wide[i, theirs].astype(BF16)


def clean_total_body(c_ref, k_ref, k_gain, grads, r1, r2, r3, sums, total_ref, grad_v, grad_cv):
    clean = r1[...].astype(F32) + r2[...].astype(F32) + r3[...].astype(F32)
    total_ref[...] = clean
    rows = to_lanes(clean[:, :LANES] * k_gain[...] * c_ref[...].astype(F32), 2)
    sums[...] = rows + to_lanes(grads[:, :LANES] * k_gain[...] * k_ref[...].astype(F32), 1)
    grad_v[...] = grads[:, LANES:].astype(BF16)
    grad_cv[...] = clean[:, LANES:].astype(BF16)


def inner_body(own, far, q_ref, q_gain, sums, attn_out, dq_out, out_ref):
    span = own.shape[0] // 2
    slot = span // GROUP
    rows = attn_out.shape[0]
    total = own[...] + far[...].astype(F32)
    for h in range(GROUP):
        cols = slice(h * HEAD_SIZE, (h + 1) * HEAD_SIZE)
        attn_out[:, cols] = total[h * slot : h * slot + rows].astype(BF16)
        at = span + h * slot
        dq_out[:, cols] = total[at : at + rows]
    part = sums[...] + to_lanes(dq_out[...] * q_gain[...] * q_ref[...].astype(F32), 0)
    for peer in range(out_ref.shape[0]):
        out_ref[peer] = part


def finish_body(
    sums_ref, inner_ref, q_ref, k_ref, c_ref, q_gain, k_gain, dq_ref, noisy_ref, clean_ref,
    grad_q, grad_k, grad_ck,
):
    q_inv, k_inv, c_inv = inverses(sums_ref)
    q_sum, k_sum, c_sum = to_rows(added(inner_ref))
    q_pull = q_inv * q_inv * q_inv * (q_sum / (HQ * HEAD_SIZE))
    for h in range(GROUP):
        cols = slice(h * HEAD_SIZE, (h + 1) * HEAD_SIZE)
        grad_q[:, cols] = (
            q_inv * (dq_ref[:, cols] * q_gain[:, cols]) - q_ref[:, cols].astype(F32) * q_pull
        ).astype(BF16)
    width = KEY_VALUE_HEADS * HEAD_SIZE
    for inv, total, mean, ref, out in (
        (k_inv, noisy_ref, k_sum, k_ref, grad_k),
        (c_inv, clean_ref, c_sum, c_ref, grad_ck),
    ):
        pull = inv * inv * inv * (mean / width)
        out[...] = (
            inv * (total[:, :LANES] * k_gain[...]) - ref[...].astype(F32) * pull
        ).astype(BF16)


def head_exchange(value):
    return lax.all_to_all(value, "head", 0, 0)


def stretch_shift(value, steps):
    count = lax.axis_size("seq")
    pairs = [(i, i + 2 * steps) for i in range(count) if 0 <= i + 2 * steps < count]
    return lax.ppermute(value, "seq", pairs)


def core_swap(value):
    count = lax.axis_size("seq")
    return lax.ppermute(value, "seq", [(i, i ^ 1) for i in range(count)])


def on_device(
    noisy_q, noisy_k, noisy_value, clean_k, clean_value, q_gain, key_norm_gain, out_grad, window
):
    rows = noisy_q.shape[0]
    slot = up(rows, PAD)
    span = GROUP * slot
    queries = up(2 * span, LANES)
    peers = lax.axis_size("head")
    q_gain = q_gain[None, :]
    k_gain = key_norm_gain[None, :]
    product = 2 * slot * queries * LANES
    stats = shape((8, queries), F32)
    turned = shape((LANES, queries), F32)

    fetched = (noisy_q, noisy_k, clean_k)
    sums = pl.pallas_call(
        squares_body,
        grid=(1,),
        out_shape=shape((peers, 8, rows), F32),
        in_specs=[pl.BlockSpec(a.shape, lambda i: (0, 0)) for a in fetched],
        out_specs=pl.BlockSpec((peers, 8, rows), lambda i: (0, 0, 0)),
        compiler_params=pltpu.CompilerParams(vmem_limit_bytes=60 * 2**20),
        cost_estimate=pl.CostEstimate(flops=10**10, bytes_accessed=10**6, transcendentals=0),
    )(*fetched)
    sums = head_exchange(sums)
    pack = shape((slot, 2 * LANES), BF16)
    noisy_kv, clean_kv, own = kernel_call(
        norms_body,
        (pack, pack, shape((2 * span, LANES), BF16)),
        10**6,
        [pltpu.VMEM((slot, 2 * LANES), F32), pltpu.VMEM((2 * span, LANES), F32)],
        nargs=9,
    )(sums, noisy_q, noisy_k, clean_k, noisy_value, clean_value, out_grad, q_gain, k_gain)
    got = [stretch_shift(clean_kv, steps) for steps in (1, 2, 3)]
    far = core_swap(own)
    q_all, g_turned, noisy_e, noisy_sum, noisy_stats = kernel_call(
        noisy_body,
        (
            shape((queries, LANES), BF16),
            shape((LANES, queries), BF16),
            shape((slot, queries), BF16),
            turned,
            stats,
        ),
        4 * product,
        [pltpu.VMEM((queries, LANES), BF16)],
        nargs=3,
    )(own, far, noisy_kv)
    pair = shape((2, slot, queries), BF16)
    other, clean_e, clean_sum, own_stats = kernel_call(
        clean_body,
        (pack, pair, turned, stats),
        8 * product,
        [pltpu.VMEM((2, slot, queries), F32)],
        smem=(0,),
        nargs=7,
    )(window, *got, q_all, g_turned, noisy_stats)
    far_stats = core_swap(own_stats)
    grad_low = shape((rows, 2 * LANES), BF16)
    back1, back2, back3, clean_ds, merged = kernel_call(
        clean_grad_body,
        (grad_low, grad_low, grad_low, pair, stats),
        8 * product,
        smem=(0,),
        nargs=8,
    )(window, own_stats, far_stats, q_all, g_turned, got[0], other, clean_e)
    r2 = stretch_shift(back2, -2)
    r3 = stretch_shift(back3, -3)
    r1 = stretch_shift(back1, -1)
    noisy_grads, own, far = kernel_call(
        noisy_grad_body,
        (
            shape((rows, 2 * LANES), F32),
            shape((2 * span, LANES), F32),
            shape((2 * span, LANES), BF16),
        ),
        8 * product,
        [pltpu.VMEM((2, queries, LANES), F32)],
        nargs=10,
    )(
        merged, q_all, g_turned, noisy_kv, got[0], other, noisy_e, clean_ds, noisy_sum, clean_sum
    )
    far = core_swap(far)
    key_grad = shape((rows, LANES), BF16)
    query_grad = shape((rows, GROUP * LANES), BF16)
    inner, clean_grads, grad_v, grad_cv = kernel_call(
        clean_total_body,
        (shape((8, rows), F32), shape((rows, 2 * LANES), F32), key_grad, key_grad),
        10**10,
        nargs=7,
    )(clean_k, noisy_k, k_gain, noisy_grads, r1, r2, r3)
    attn_out, dq, inner = kernel_call(
        inner_body,
        (query_grad, shape((rows, GROUP * LANES), F32), shape((peers, 8, rows), F32)),
        10**6,
        nargs=5,
    )(own, far, noisy_q, q_gain, inner)
    inner = head_exchange(inner)
    grad_q, grad_k, grad_ck = kernel_call(
        finish_body, (query_grad, key_grad, key_grad), 10**6, nargs=10
    )(sums, inner, noisy_q, noisy_k, clean_k, q_gain, k_gain, dq, noisy_grads, clean_grads)
    return (attn_out, grad_q, grad_k, grad_v, grad_ck, grad_cv)


def solution(mesh):
    tokens = P("seq", "head")
    return jax.shard_map(
        on_device,
        mesh=mesh,
        in_specs=(tokens,) * 5 + (P("head"), P("head"), tokens, P()),
        out_specs=(tokens,) * 6,
        check_vma=False,
    )
```

time: 94.7 us -> 87.1 us (0.920)
  the two profiles are of different devices: /device:TPU:192 before, /device:TPU:208 now
where the time goes in v3:
time: 87.1 us; the launch traced here: 86.6 us
  starting transfers between devices  35.9 us (41%)
  waiting for transfers between devices  23.8 us (27%)
  Pallas kernels  13.8 us (16%)
  blocking collectives  12.1 us (14%)
  between operations  0.88 us (1%)
    ppermute x6, starting transfers between devices, stretch_shift(): return lax.ppermute(value, 'seq', pairs)  24.8 us
    ppermute x6, waiting for transfers between devices, stretch_shift(): return lax.ppermute(value, 'seq', pairs)  16.2 us
    all_to_all x1, blocking collectives, head_exchange(): return lax.all_to_all(value, 'head', 0, 0)  12.1 us
    all_to_all x1, waiting for transfers between devices, head_exchange(): return lax.all_to_all(value, 'head', 0, 0)  6.42 us
    ppermute x3, starting transfers between devices, core_swap(): return lax.ppermute(value, 'seq', [(i, i ^ 1) for i in range(count)])  5.76 us
    all_to_all x1, starting transfers between devices, head_exchange(): return lax.all_to_all(value, 'head', 0, 0)  5.31 us
    pallas_call x1, Pallas kernels, on_device(): kernel_call(clean_grad_body, (grad_low, grad_low, grad_low, pair, stats),...  2.65 us
    pallas_call x1, Pallas kernels, on_device(): kernel_call(clean_body, (pack, pair, turned, stats), 8 * product, [pltpu....  2.58 us
  transfers between devices with their start and end apart: 10, of which 6 were waited for; matrix products, arithmetic and copies ran while one was open for 0% of the time, Pallas kernels for 4%

profile of v3, /device:TPU:208, one launch (start us, length us, event | category | flops | bytes accessed | tf_op | source)
XLA Modules:
  0.0 86.6 jit_solution(16053571318203197011)
XLA Ops:
  0.7 2.1 %shard_map.136 = f32[8,8,260]{2,1,0:T(8,128)} custom-call(bf16[260,384]{1,0:T(8,128)(2,1)} %q_ref.7, bf16[260,128]{1,0:T(8,128)(2,1)} %k_ref.7, bf16[260,128]{1,0:T(8,128)(2,1)} %c_ref.7), custom_call_target="tpu_custom_call" | custom-call | flops 10000000000 | bytes 1000000 | tf_op jit(solution)/shard_map/pallas_call | solution.py:370
  2.9 5.3 %all-to-all-start = ((f32[8,8,260]{2,1,0:T(8,128)}), f32[8,8,260]{2,1,0:T(8,128)S(1)}, u32[]{:S(2)}, u32[]{:S(2)}) async-start(f32[8,8,260]{2,1,0:T(8,128)} %shard_map.136), calls=%async_computation | async-start | bytes 196608 | tf_op jit(solution)/shard_map/all_to_all | solution.py:341
  8.2 6.4 %all-to-all-done.sums_ref = f32[8,8,260]{2,1,0:T(8,128)S(1)} async-done(((f32[8,8,260]{2,1,0:T(8,128)}), f32[8,8,260]{2,1,0:T(8,128)S(1)}, u32[]{:S(2)}, u32[]{:S(2)}) %all-to-all-start) | async-done | bytes 66592 | tf_op jit(solution)/shard_map/all_to_all | solution.py:341
  14.6 0.0 copy-done.2
  14.7 0.4 shard_map.137
  15.1 1.9 %collective-permute-start.3 = (bf16[1632,128]{1,0:T(8,128)(2,1)S(1)}, bf16[1632,128]{1,0:T(8,128)(2,1)S(1)}, u32[]{:S(2)}, u32[]{:S(2)}) collective-permute-start(bf16[1632,128]{1,0:T(8,128)(2,1)S(1)} %get-tuple-element.37.own), channel_id=1, source_target_pairs={{0,8},{8,0},{16,24},{24,16},{32,40},{40,32},{48,56},{56,48},{64,72... | collective-permute-start | bytes 1253384 | tf_op jit(solution)/shard_map/ppermute | solution.py:352
  17.0 5.3 %collective-permute-start.2 = (bf16[272,256]{1,0:T(8,128)(2,1)S(1)}, bf16[272,256]{1,0:T(8,128)(2,1)S(1)}, u32[]{:S(2)}, u32[]{:S(2)}) collective-permute-start(bf16[272,256]{1,0:T(8,128)(2,1)S(1)} %get-tuple-element.36), channel_id=1, source_target_pairs={{0,48},{8,56},{16,64},{24,72},{32,80},{40,88},{48,96},{56,104},{64... | collective-permute-start | bytes 417800 | tf_op jit(solution)/shard_map/ppermute | solution.py:347
  22.3 6.8 %collective-permute-start.1 = (bf16[272,256]{1,0:T(8,128)(2,1)S(1)}, bf16[272,256]{1,0:T(8,128)(2,1)S(1)}, u32[]{:S(2)}, u32[]{:S(2)}) collective-permute-start(bf16[272,256]{1,0:T(8,128)(2,1)S(1)} %get-tuple-element.36), channel_id=1, source_target_pairs={{0,32},{8,40},{16,48},{24,56},{32,64},{40,72},{48,80},{56,88},{64,... | collective-permute-start | bytes 417800 | tf_op jit(solution)/shard_map/ppermute | solution.py:347
  29.1 3.9 %collective-permute-start = (bf16[272,256]{1,0:T(8,128)(2,1)S(1)}, bf16[272,256]{1,0:T(8,128)(2,1)S(1)}, u32[]{:S(2)}, u32[]{:S(2)}) collective-permute-start(bf16[272,256]{1,0:T(8,128)(2,1)S(1)} %get-tuple-element.36), channel_id=1, source_target_pairs={{0,16},{8,24},{16,32},{24,40},{32,48},{40,56},{48,64},{56,72},{64,... | collective-permute-start | bytes 417800 | tf_op jit(solution)/shard_map/ppermute | solution.py:347
  33.1 0.1 copy.16.window_ref
  33.1 0.0 collective-permute-done.3.far
  33.2 1.0 %shard_map.138 = (bf16[1664,128]{1,0:T(8,128)(2,1)S(1)}, bf16[128,1664]{1,0:T(8,128)(2,1)S(1)}, bf16[272,1664]{1,0:T(8,128)(2,1)S(1)}, f32[128,1664]{1,0:T(8,128)S(1)}, f32[8,1664]{1,0:T(8,128)S(1)}) custom-call(bf16[1632,128]{1,0:T(8,128)(2,1)S(1)} %get-tuple-element.37.own, bf16[1632,128]{1,0:T(8,128)(2,1)S(1)} %collective-permute-done.3.far, ...), custom_call_target="tpu_custom_call" | custom-call | flops 463470592 | bytes 2662400 | tf_op jit(solution)/shard_map/pallas_call | solution.py:390
  34.1 0.0 collective-permute-done.2.got3
  34.1 4.1 %collective-permute-done.1.got2 = bf16[272,256]{1,0:T(8,128)(2,1)S(1)} collective-permute-done((bf16[272,256]{1,0:T(8,128)(2,1)S(1)}, bf16[272,256]{1,0:T(8,128)(2,1)S(1)}, u32[]{:S(2)}, u32[]{:S(2)}) %collective-permute-start.1) | collective-permute-done | bytes 139296 | tf_op jit(solution)/shard_map/ppermute | solution.py:347
  38.3 3.2 %collective-permute-done.got1 = bf16[272,256]{1,0:T(8,128)(2,1)S(1)} collective-permute-done((bf16[272,256]{1,0:T(8,128)(2,1)S(1)}, bf16[272,256]{1,0:T(8,128)(2,1)S(1)}, u32[]{:S(2)}, u32[]{:S(2)}) %collective-permute-start) | collective-permute-done | bytes 139296 | tf_op jit(solution)/shard_map/ppermute | solution.py:347
  41.4 2.6 %shard_map.139 = (bf16[272,256]{1,0:T(8,128)(2,1)S(1)}, bf16[2,272,1664]{2,1,0:T(8,128)(2,1)S(1)}, f32[128,1664]{1,0:T(8,128)S(1)}, f32[8,1664]{1,0:T(8,128)S(1)}) custom-call(s32[32,2]{1,0:T(8,128)S(1)} %copy.16.window_ref, bf16[272,256]{1,0:T(8,128)(2,1)S(1)} %collective-permute-done.got1, bf16[272,256]{1,0:T(8,128)(2,1)S(1)} %collective-permute-done.1.got2, ...), custom_call_target="tpu_custom_call" | custom-call | flops 926941184 | bytes 2854912 | tf_op jit(solution)/shard_map/pallas_call | solution.py:404
  44.0 1.9 %collective-permute-start.4 = (f32[8,1664]{1,0:T(8,128)S(1)}, f32[8,1664]{1,0:T(8,128)S(1)}, u32[]{:S(2)}, u32[]{:S(2)}) collective-permute-start(f32[8,1664]{1,0:T(8,128)S(1)} %get-tuple-element.42.own), channel_id=1, source_target_pairs={{0,8},{8,0},{16,24},{24,16},{32,40},{40,32},{48,56},{56,48},{64,72... | collective-permute-start | bytes 159752 | tf_op jit(solution)/shard_map/ppermute | solution.py:352
  46.0 1.2 %collective-permute-done.4.far = f32[8,1664]{1,0:T(8,128)S(1)} collective-permute-done((f32[8,1664]{1,0:T(8,128)S(1)}, f32[8,1664]{1,0:T(8,128)S(1)}, u32[]{:S(2)}, u32[]{:S(2)}) %collective-permute-start.4) | collective-permute-done | bytes 53280 | tf_op jit(solution)/shard_map/ppermute | solution.py:352
  47.2 2.6 %shard_map.140 = (bf16[260,256]{1,0:T(8,128)(2,1)S(1)}, bf16[260,256]{1,0:T(8,128)(2,1)S(1)}, bf16[260,256]{1,0:T(8,128)(2,1)S(1)}, bf16[2,272,1664]{2,1,0:T(8,128)(2,1)S(1)}, f32[8,1664]{1,0:T(8,128)S(1)}) custom-call(s32[32,2]{1,0:T(8,128)S(1)} %copy.16.window_ref, f32[8,1664]{1,0:T(8,128)S(1)} %get-tuple-element.42.own, ...), custom_call_target="tpu_custom_call" | custom-call | flops 926941184 | bytes 2263040 | tf_op jit(solution)/shard_map/pallas_call | solution.py:414
  49.8 2.2 %collective-permute-start.6 = (bf16[260,256]{1,0:T(8,128)(2,1)S(1)}, bf16[260,256]{1,0:T(8,128)(2,1)S(1)}, u32[]{:S(2)}, u32[]{:S(2)}) collective-permute-start(bf16[260,256]{1,0:T(8,128)(2,1)S(1)} %get-tuple-element.53), channel_id=1, source_target_pairs={{16,0},{24,8},{32,16},{40,24},{48,32},{56,40},{64,48},{72,56},{80,... | collective-permute-start | bytes 399368 | tf_op jit(solution)/shard_map/ppermute | solution.py:347
  52.1 3.8 %collective-permute-start.7 = (bf16[260,256]{1,0:T(8,128)(2,1)S(1)}, bf16[260,256]{1,0:T(8,128)(2,1)S(1)}, u32[]{:S(2)}, u32[]{:S(2)}) collective-permute-start(bf16[260,256]{1,0:T(8,128)(2,1)S(1)} %get-tuple-element.54), channel_id=1, source_target_pairs={{32,0},{40,8},{48,16},{56,24},{64,32},{72,40},{80,48},{88,56},{96,... | collective-permute-start | bytes 399368 | tf_op jit(solution)/shard_map/ppermute | solution.py:347
  55.9 2.7 %collective-permute-start.8 = (bf16[260,256]{1,0:T(8,128)(2,1)S(1)}, bf16[260,256]{1,0:T(8,128)(2,1)S(1)}, u32[]{:S(2)}, u32[]{:S(2)}) collective-permute-start(bf16[260,256]{1,0:T(8,128)(2,1)S(1)} %get-tuple-element.55), channel_id=1, source_target_pairs={{48,0},{56,8},{64,16},{72,24},{80,32},{88,40},{96,48},{104,56},{11... | collective-permute-start | bytes 399368 | tf_op jit(solution)/shard_map/ppermute | solution.py:347
  58.6 2.0 %shard_map.141 = (f32[260,256]{1,0:T(8,128)S(1)}, f32[1632,128]{1,0:T(8,128)S(1)}, bf16[1632,128]{1,0:T(8,128)(2,1)S(1)}) custom-call(f32[8,1664]{1,0:T(8,128)S(1)} %get-tuple-element.45.merged, bf16[1664,128]{1,0:T(8,128)(2,1)S(1)} %get-tuple-element.39.q_ref, bf16[128,1664]{1,0:T(8,128)(2,1)S(1)} %get-tuple-element.40.gt_ref, ...), custom_call_target="tpu_custom_call" | custom-call | flops 926941184 | bytes 1519616 | tf_op jit(solution)/shard_map/pallas_call | solution.py:424
  60.6 1.9 %collective-permute-start.5 = (bf16[1632,128]{1,0:T(8,128)(2,1)S(1)}, bf16[1632,128]{1,0:T(8,128)(2,1)S(1)}, u32[]{:S(2)}, u32[]{:S(2)}) collective-permute-start(bf16[1632,128]{1,0:T(8,128)(2,1)S(1)} %get-tuple-element.51), channel_id=1, source_target_pairs={{0,8},{8,0},{16,24},{24,16},{32,40},{40,32},{48,56},{56,48},{64,72... | collective-permute-start | bytes 1253384 | tf_op jit(solution)/shard_map/ppermute | solution.py:352
  62.6 0.0 collective-permute-done.6.r1
  62.6 3.8 %collective-permute-done.7.r2 = bf16[260,256]{1,0:T(8,128)(2,1)S(1)} collective-permute-done((bf16[260,256]{1,0:T(8,128)(2,1)S(1)}, bf16[260,256]{1,0:T(8,128)(2,1)S(1)}, u32[]{:S(2)}, u32[]{:S(2)}) %collective-permute-start.7) | collective-permute-done | bytes 133152 | tf_op jit(solution)/shard_map/ppermute | solution.py:347
  66.4 5.0 %collective-permute-done.8.r3 = bf16[260,256]{1,0:T(8,128)(2,1)S(1)} collective-permute-done((bf16[260,256]{1,0:T(8,128)(2,1)S(1)}, bf16[260,256]{1,0:T(8,128)(2,1)S(1)}, u32[]{:S(2)}, u32[]{:S(2)}) %collective-permute-start.8) | collective-permute-done | bytes 133152 | tf_op jit(solution)/shard_map/ppermute | solution.py:347
  71.4 0.8 shard_map.142
  72.2 0.0 collective-permute-done.5.far
  72.2 1.0 %shard_map.143 = (bf16[260,384]{1,0:T(8,128)(2,1)}, f32[260,384]{1,0:T(8,128)S(1)}, f32[8,8,260]{2,1,0:T(8,128)S(1)}) custom-call(f32[1632,128]{1,0:T(8,128)S(1)} %get-tuple-element.50.own, bf16[1632,128]{1,0:T(8,128)(2,1)S(1)} %collective-permute-done.5.far, bf16[260,384]{1,0:T(8,128)(2,1)S(1)} %copy-done, f32[1,384]{1,0:T(1,128)S(1)} %broadcast_in_dim.6.q_gain, ...), custom_call_target="tpu_custom_call" | custom-call | flops 1000000 | bytes 665600 | tf_op jit(solution)/shard_map/pallas_call | solution.py:446
  73.2 12.1 %all_to_all.10.inner_ref = f32[8,8,260]{2,1,0:T(8,128)S(1)} all-to-all(f32[8,8,260]{2,1,0:T(8,128)S(1)} %get-tuple-element.58), channel_id=1, replica_groups=mesh['seq'=64,'head'=8] {'head'}, dimensions={0} | all-to-all | bytes 133120 | tf_op jit(solution)/shard_map/all_to_all | solution.py:341
  85.3 1.3 %shard_map.144 = (bf16[260,384]{1,0:T(8,128)(2,1)}, bf16[260,128]{1,0:T(8,128)(2,1)}, bf16[260,128]{1,0:T(8,128)(2,1)}) custom-call(f32[8,8,260]{2,1,0:T(8,128)S(1)} %all-to-all-done.sums_ref, f32[8,8,260]{2,1,0:T(8,128)S(1)} %all_to_all.10.inner_ref, bf16[260,384]{1,0:T(8,128)(2,1)S(1)} %copy-done, bf16[260,128]{1,0:T(8,128)(2,1)S(1)} %copy-done.1, ...), custom_call_target="tpu_custom_call" | custom-call | flops 1000000 | bytes 332800 | tf_op jit(solution)/shard_map/pallas_call | solution.py:453
  (18 shorter events, 0.0 us)
Async XLA Ops:
  0.6 14.0 %copy-start.2 = (bf16[260,128]{1,0:T(8,128)(2,1)S(1)}, bf16[260,128]{1,0:T(8,128)(2,1)}, u32[]{:S(2)}) copy-start(bf16[260,128]{1,0:T(8,128)(2,1)} %c_ref.7) | copy-start | bytes 199684
  0.6 14.0 %copy-start.1 = (bf16[260,128]{1,0:T(8,128)(2,1)S(1)}, bf16[260,128]{1,0:T(8,128)(2,1)}, u32[]{:S(2)}) copy-start(bf16[260,128]{1,0:T(8,128)(2,1)} %k_ref.7) | copy-start | bytes 199684
  0.7 14.0 %copy-start = (bf16[260,384]{1,0:T(8,128)(2,1)S(1)}, bf16[260,384]{1,0:T(8,128)(2,1)}, u32[]{:S(2)}) copy-start(bf16[260,384]{1,0:T(8,128)(2,1)} %q_ref.7) | copy-start | bytes 599044
  0.7 7.5 %copy-start.7 = (f32[384]{0:T(512)S(1)}, f32[384]{0:T(512)}, u32[]{:S(2)}) copy-start(f32[384]{0:T(512)} %param.14) | copy-start | bytes 4612
  0.7 13.9 %copy-start.3 = (bf16[260,384]{1,0:T(8,128)(2,1)S(1)}, bf16[260,384]{1,0:T(8,128)(2,1)}, u32[]{:S(2)}) copy-start(bf16[260,384]{1,0:T(8,128)(2,1)} %g_ref.1) | copy-start | bytes 599044
  0.7 13.9 %copy-start.6 = (f32[128]{0:T(128)S(1)}, f32[128]{0:T(128)}, u32[]{:S(2)}) copy-start(f32[128]{0:T(128)} %param.15) | copy-start | bytes 1540
  0.7 13.9 %copy-start.5 = (bf16[260,128]{1,0:T(8,128)(2,1)S(1)}, bf16[260,128]{1,0:T(8,128)(2,1)}, u32[]{:S(2)}) copy-start(bf16[260,128]{1,0:T(8,128)(2,1)} %cv_ref.1) | copy-start | bytes 199684
  0.7 13.9 %copy-start.4 = (bf16[260,128]{1,0:T(8,128)(2,1)S(1)}, bf16[260,128]{1,0:T(8,128)(2,1)}, u32[]{:S(2)}) copy-start(bf16[260,128]{1,0:T(8,128)(2,1)} %v_ref.1) | copy-start | bytes 199684
  0.7 32.3 %copy-start.8 = (s32[32,2]{0,1:T(2,128)S(1)}, s32[32,2]{0,1:T(2,128)}, u32[]{:S(2)}) copy-start(s32[32,2]{0,1:T(2,128)} %param.17) | copy-start | bytes 772
  2.9 11.7 %all-to-all-start = ((f32[8,8,260]{2,1,0:T(8,128)}), f32[8,8,260]{2,1,0:T(8,128)S(1)}, u32[]{:S(2)}, u32[]{:S(2)}) async-start(f32[8,8,260]{2,1,0:T(8,128)} %shard_map.136), calls=%async_computation | async-start | bytes 196608 | tf_op jit(solution)/shard_map/all_to_all | solution.py:341
  15.1 18.1 %collective-permute-start.3 = (bf16[1632,128]{1,0:T(8,128)(2,1)S(1)}, bf16[1632,128]{1,0:T(8,128)(2,1)S(1)}, u32[]{:S(2)}, u32[]{:S(2)}) collective-permute-start(bf16[1632,128]{1,0:T(8,128)(2,1)S(1)} %get-tuple-element.37.own), channel_id=1, source_target_pairs={{0,8},{8,0},{16,24},{24,16},{32,40},{40,32},{48,56},{56,48},{64,72... | collective-permute-start | bytes 1253384 | tf_op jit(solution)/shard_map/ppermute | solution.py:352
  17.0 17.1 %collective-permute-start.2 = (bf16[272,256]{1,0:T(8,128)(2,1)S(1)}, bf16[272,256]{1,0:T(8,128)(2,1)S(1)}, u32[]{:S(2)}, u32[]{:S(2)}) collective-permute-start(bf16[272,256]{1,0:T(8,128)(2,1)S(1)} %get-tuple-element.36), channel_id=1, source_target_pairs={{0,48},{8,56},{16,64},{24,72},{32,80},{40,88},{48,96},{56,104},{64... | collective-permute-start | bytes 417800 | tf_op jit(solution)/shard_map/ppermute | solution.py:347
  22.3 16.0 %collective-permute-start.1 = (bf16[272,256]{1,0:T(8,128)(2,1)S(1)}, bf16[272,256]{1,0:T(8,128)(2,1)S(1)}, u32[]{:S(2)}, u32[]{:S(2)}) collective-permute-start(bf16[272,256]{1,0:T(8,128)(2,1)S(1)} %get-tuple-element.36), channel_id=1, source_target_pairs={{0,32},{8,40},{16,48},{24,56},{32,64},{40,72},{48,80},{56,88},{64,... | collective-permute-start | bytes 417800 | tf_op jit(solution)/shard_map/ppermute | solution.py:347
  29.1 12.3 %collective-permute-start = (bf16[272,256]{1,0:T(8,128)(2,1)S(1)}, bf16[272,256]{1,0:T(8,128)(2,1)S(1)}, u32[]{:S(2)}, u32[]{:S(2)}) collective-permute-start(bf16[272,256]{1,0:T(8,128)(2,1)S(1)} %get-tuple-element.36), channel_id=1, source_target_pairs={{0,16},{8,24},{16,32},{24,40},{32,48},{40,56},{48,64},{56,72},{64,... | collective-permute-start | bytes 417800 | tf_op jit(solution)/shard_map/ppermute | solution.py:347
  44.0 3.1 %collective-permute-start.4 = (f32[8,1664]{1,0:T(8,128)S(1)}, f32[8,1664]{1,0:T(8,128)S(1)}, u32[]{:S(2)}, u32[]{:S(2)}) collective-permute-start(f32[8,1664]{1,0:T(8,128)S(1)} %get-tuple-element.42.own), channel_id=1, source_target_pairs={{0,8},{8,0},{16,24},{24,16},{32,40},{40,32},{48,56},{56,48},{64,72... | collective-permute-start | bytes 159752 | tf_op jit(solution)/shard_map/ppermute | solution.py:352
  49.8 12.8 %collective-permute-start.6 = (bf16[260,256]{1,0:T(8,128)(2,1)S(1)}, bf16[260,256]{1,0:T(8,128)(2,1)S(1)}, u32[]{:S(2)}, u32[]{:S(2)}) collective-permute-start(bf16[260,256]{1,0:T(8,128)(2,1)S(1)} %get-tuple-element.53), channel_id=1, source_target_pairs={{16,0},{24,8},{32,16},{40,24},{48,32},{56,40},{64,48},{72,56},{80,... | collective-permute-start | bytes 399368 | tf_op jit(solution)/shard_map/ppermute | solution.py:347
  52.1 14.4 %collective-permute-start.7 = (bf16[260,256]{1,0:T(8,128)(2,1)S(1)}, bf16[260,256]{1,0:T(8,128)(2,1)S(1)}, u32[]{:S(2)}, u32[]{:S(2)}) collective-permute-start(bf16[260,256]{1,0:T(8,128)(2,1)S(1)} %get-tuple-element.54), channel_id=1, source_target_pairs={{32,0},{40,8},{48,16},{56,24},{64,32},{72,40},{80,48},{88,56},{96,... | collective-permute-start | bytes 399368 | tf_op jit(solution)/shard_map/ppermute | solution.py:347
  55.9 15.6 %collective-permute-start.8 = (bf16[260,256]{1,0:T(8,128)(2,1)S(1)}, bf16[260,256]{1,0:T(8,128)(2,1)S(1)}, u32[]{:S(2)}, u32[]{:S(2)}) collective-permute-start(bf16[260,256]{1,0:T(8,128)(2,1)S(1)} %get-tuple-element.55), channel_id=1, source_target_pairs={{48,0},{56,8},{64,16},{72,24},{80,32},{88,40},{96,48},{104,56},{11... | collective-permute-start | bytes 399368 | tf_op jit(solution)/shard_map/ppermute | solution.py:347
  60.6 11.6 %collective-permute-start.5 = (bf16[1632,128]{1,0:T(8,128)(2,1)S(1)}, bf16[1632,128]{1,0:T(8,128)(2,1)S(1)}, u32[]{:S(2)}, u32[]{:S(2)}) collective-permute-start(bf16[1632,128]{1,0:T(8,128)(2,1)S(1)} %get-tuple-element.51), channel_id=1, source_target_pairs={{0,8},{8,0},{16,24},{24,16},{32,40},{40,32},{48,56},{56,48},{64,72... | collective-permute-start | bytes 1253384 | tf_op jit(solution)/shard_map/ppermute | solution.py:352

commit v4 on v3

--- a/solution.py
+++ b/solution.py
@@ -62,8 +62,8 @@
 
 
 def to_rows(x):
-    row = lax.broadcasted_iota(jnp.int32, (8, 3 * LANES), 0)
-    group = lax.broadcasted_iota(jnp.int32, (8, 3 * LANES), 1) // LANES
+    row = lax.broadcasted_iota(jnp.int32, (3, 3 * LANES), 0)
+    group = lax.broadcasted_iota(jnp.int32, (3, 3 * LANES), 1) // LANES
     pick = (row == group).astype(BF16)
     high, low = halves(x)
     rows = dot(high, pick, 0, 0) + dot(low, pick, 0, 0)
@@ -90,7 +90,7 @@
         part = to_lanes(x * x, i)
         rows = part if rows is None else rows + part
     for peer in range(out_ref.shape[0]):
-        out_ref[peer] = rows
+        out_ref[peer] = rows[:3]
 
 
 def norms_body(
@@ -178,42 +178,48 @@
     stats[2:3] = jnp.sum(gt * sums, axis=0, keepdims=True)
 
 
+def pair_body(own, far, out):
+    out[0] = own[...]
+    out[1] = far[...]
+
+
 def clean_body(
-    window_ref, got1, got2, got3, q_ref, gt_ref, noisy_stats, other, e_out, sum_out, stats, s_ref
+    window_ref, near, far, q_ref, gt_ref, noisy_stats, keys, e_out, sum_out, stats, s_ref
 ):
     use1, use2, use3 = listed(window_ref)
-
-    @pl.when(use2)
+    first = lax.axis_index("seq") % 2 == 0
+    from_far = jnp.logical_not(first) & use2
+
+    @pl.when(from_far)
     def _():
-        other[...] = got2[...]
-
-    @pl.when(jnp.logical_not(use2))
+        keys[...] = far[...]
+
+    @pl.when(jnp.logical_not(from_far))
     def _():
-        other[...] = got3[...]
-
+        keys[...] = near[...]
+
+    hide = jnp.where(jnp.where(first, use1, use2 | use3), 0.0, HIDDEN)
     q = q_ref[...]
     top = None
-    for j, (ref, use) in enumerate(((got1, use1), (other, use2 | use3))):
-        hide = jnp.where(use, 0.0, HIDDEN)
-        body, tail = scores(ref, q, TOKENS)
+    for j in range(2):
+        body, tail = scores(keys.at[j], q, TOKENS)
         whole = body.shape[0]
         body = body + hide
+        tail = tail + hide
         s_ref[j, 0:whole] = body
         s_ref[j, whole:] = tail
         here = jnp.maximum(
-            jnp.max(body, axis=0, keepdims=True),
-            jnp.max(tail + hide, axis=0, keepdims=True),
+            jnp.max(body, axis=0, keepdims=True), jnp.max(tail, axis=0, keepdims=True)
         )
         top = here if top is None else jnp.maximum(top, here)
-        s_ref[j, whole:] = tail + hide
     total = None
     sums = None
-    for j, ref in enumerate((got1, other)):
+    for j in range(2):
         e = jnp.exp2(s_ref[j] - top)
         part = jnp.sum(e, axis=0, keepdims=True)
         low = e.astype(BF16)
         e_out[j] = low
-        share = dot(ref[:, LANES:], low, 0, 0)
+        share = dot(keys[j, :, LANES:], low, 0, 0)
         total = part if total is None else total + part
         sums = share if sums is None else sums + share
     sum_out[...] = sums
@@ -232,9 +238,10 @@
 
 
 def clean_grad_body(
-    window_ref, own, far, q_ref, gt_ref, got1, other, e_ref, back1, back2, back3, ds_out, merged
+    window_ref, own, far, q_ref, gt_ref, keys, e_ref, near_out, far_out, ds_out, merged
 ):
     use1, use2, use3 = listed(window_ref)
+    first = lax.axis_index("seq") % 2 == 0
     groups = [(ref[i : i + 1], ref[i + 1 : i + 2], ref[i + 2 : i + 3])
               for ref in (own, far) for i in (0, 3)]
     top = groups[0][0]
@@ -252,21 +259,19 @@
     g = gt.T.astype(BF16)
     gt = gt.astype(BF16)
     q = q_ref[...]
-    rows = back1.shape[0]
-    for j, (ref, outs) in enumerate(
-        ((other, ((back2, use2), (back3, use3))), (got1, ((back1, use1),)))
-    ):
-        at = 1 - j
-        ds, dk, dv = key_grads(ref, e_ref[at], gt, g, delta * clean, q)
-        ds_out[at] = ds
-        for out, use in outs:
-            keep = jnp.where(use, 1.0, 0.0)
-            out[:, :LANES] = (dk[:rows] * keep).astype(BF16)
-            out[:, LANES:] = (dv[:rows] * keep).astype(BF16)
+    rows = near_out.shape[1]
+    keep_near = jnp.where(jnp.where(first, use1, use3), 1.0, 0.0)
+    keep_far = jnp.where(use2, 1.0, 0.0)
+    for j in range(2):
+        ds, dk, dv = key_grads(keys.at[j], e_ref[j], gt, g, delta * clean, q)
+        ds_out[j] = ds
+        for out, keep in ((near_out, keep_near), (far_out, keep_far)):
+            out[j, :, :LANES] = (dk[:rows] * keep).astype(BF16)
+            out[j, :, LANES:] = (dv[:rows] * keep).astype(BF16)
 
 
 def noisy_grad_body(
-    merged, q_ref, gt_ref, keys, got1, other, e_ref, ds_ref, noisy_sum, clean_sum,
+    merged, q_ref, gt_ref, keys, clean_keys, e_ref, ds_ref, noisy_sum, clean_sum,
     grads, own, far, wide,
 ):
     core = lax.axis_index("seq") % 2
@@ -281,8 +286,8 @@
     grads[:, :LANES] = dk[:rows]
     grads[:, LANES:] = dv[:rows]
     dq = dot(keys[:, :LANES], ds, 0, 0)
-    dq = dq + dot(got1[:, :LANES], ds_ref[0], 0, 0)
-    dq = dq + dot(other[:, :LANES], ds_ref[1], 0, 0)
+    for j in range(2):
+        dq = dq + dot(clean_keys[j, :, :LANES], ds_ref[j], 0, 0)
     wide[0] = (noisy_sum[...] * noisy + clean_sum[...] * merged[1:2]).T
     wide[1] = (dq * SCORE_SCALE).T
     for i in range(2):
@@ -290,16 +295,21 @@
         far[i * span : (i + 1) * span] = wide[i, theirs].astype(BF16)
 
 
-def clean_total_body(c_ref, k_ref, k_gain, grads, r1, r2, r3, sums, total_ref, grad_v, grad_cv):
-    clean = r1[...].astype(F32) + r2[...].astype(F32) + r3[...].astype(F32)
-    total_ref[...] = clean
-    rows = to_lanes(clean[:, :LANES] * k_gain[...] * c_ref[...].astype(F32), 2)
-    sums[...] = rows + to_lanes(grads[:, :LANES] * k_gain[...] * k_ref[...].astype(F32), 1)
+def join_body(far, near, own_out, far_out):
+    own_out[...] = near[0].astype(F32) + far[0].astype(F32)
+    far_out[...] = (near[1].astype(F32) + far[1].astype(F32)).astype(BF16)
+
+
+def inner_body(
+    own, far, own_clean, far_clean, grads, q_ref, k_ref, c_ref, q_gain, k_gain,
+    attn_out, dq_out, clean_out, grad_v, grad_cv, out_ref,
+):
+    clean = own_clean[...] + far_clean[...].astype(F32)
+    clean_out[...] = clean
+    grad_cv[...] = clean[:, LANES:].astype(BF16)
     grad_v[...] = grads[:, LANES:].astype(BF16)
-    grad_cv[...] = clean[:, LANES:].astype(BF16)
-
-
-def inner_body(own, far, q_ref, q_gain, sums, attn_out, dq_out, out_ref):
+    part = to_lanes(clean[:, :LANES] * k_gain[...] * c_ref[...].astype(F32), 2)
+    part = part + to_lanes(grads[:, :LANES] * k_gain[...] * k_ref[...].astype(F32), 1)
     span = own.shape[0] // 2
     slot = span // GROUP
     rows = attn_out.shape[0]
@@ -309,9 +319,9 @@
         attn_out[:, cols] = total[h * slot : h * slot + rows].astype(BF16)
         at = span + h * slot
         dq_out[:, cols] = total[at : at + rows]
-    part = sums[...] + to_lanes(dq_out[...] * q_gain[...] * q_ref[...].astype(F32), 0)
+    part = part + to_lanes(dq_out[...] * q_gain[...] * q_ref[...].astype(F32), 0)
     for peer in range(out_ref.shape[0]):
-        out_ref[peer] = part
+        out_ref[peer] = part[:3]
 
 
 def finish_body(
@@ -341,9 +351,16 @@
     return lax.all_to_all(value, "head", 0, 0)
 
 
-def stretch_shift(value, steps):
+def stretch_shift(value, steps, far):
     count = lax.axis_size("seq")
-    pairs = [(i, i + 2 * steps) for i in range(count) if 0 <= i + 2 * steps < count]
+    pairs = []
+    for i in range(count):
+        if far and i % 2 == 0:
+            continue
+        length = 2 if far else (1, 3)[i % 2]
+        target = i + 2 * length * steps
+        if 0 <= target < count:
+            pairs.append((i, target))
     return lax.ppermute(value, "seq", pairs)
 
 
@@ -370,9 +387,9 @@
     sums = pl.pallas_call(
         squares_body,
         grid=(1,),
-        out_shape=shape((peers, 8, rows), F32),
+        out_shape=shape((peers, 3, rows), F32),
         in_specs=[pl.BlockSpec(a.shape, lambda i: (0, 0)) for a in fetched],
-        out_specs=pl.BlockSpec((peers, 8, rows), lambda i: (0, 0, 0)),
+        out_specs=pl.BlockSpec((peers, 3, rows), lambda i: (0, 0, 0)),
         compiler_params=pltpu.CompilerParams(vmem_limit_bytes=60 * 2**20),
         cost_estimate=pl.CostEstimate(flops=10**10, bytes_accessed=10**6, transcendentals=0),
     )(*fetched)
@@ -385,7 +402,10 @@
         [pltpu.VMEM((slot, 2 * LANES), F32), pltpu.VMEM((2 * span, LANES), F32)],
         nargs=9,
     )(sums, noisy_q, noisy_k, clean_k, noisy_value, clean_value, out_grad, q_gain, k_gain)
-    got = [stretch_shift(clean_kv, steps) for steps in (1, 2, 3)]
+    pair_kv = shape((2, slot, 2 * LANES), BF16)
+    clean_kv = kernel_call(pair_body, pair_kv, 10**6, nargs=2)(clean_kv, core_swap(clean_kv))
+    near_kv = stretch_shift(clean_kv, 1, False)
+    far_kv = stretch_shift(clean_kv, 1, True)
     far = core_swap(own)
     q_all, g_turned, noisy_e, noisy_sum, noisy_stats = kernel_call(
         noisy_body,
@@ -401,26 +421,25 @@
         nargs=3,
     )(own, far, noisy_kv)
     pair = shape((2, slot, queries), BF16)
-    other, clean_e, clean_sum, own_stats = kernel_call(
+    keys, clean_e, clean_sum, own_stats = kernel_call(
         clean_body,
-        (pack, pair, turned, stats),
+        (pair_kv, pair, turned, stats),
         8 * product,
         [pltpu.VMEM((2, slot, queries), F32)],
         smem=(0,),
-        nargs=7,
-    )(window, *got, q_all, g_turned, noisy_stats)
+        nargs=6,
+    )(window, near_kv, far_kv, q_all, g_turned, noisy_stats)
     far_stats = core_swap(own_stats)
-    grad_low = shape((rows, 2 * LANES), BF16)
-    back1, back2, back3, clean_ds, merged = kernel_call(
+    pair_grad = shape((2, rows, 2 * LANES), BF16)
+    near_back, far_back, clean_ds, merged = kernel_call(
         clean_grad_body,
-        (grad_low, grad_low, grad_low, pair, stats),
+        (pair_grad, pair_grad, pair, stats),
         8 * product,
         smem=(0,),
-        nargs=8,
-    )(window, own_stats, far_stats, q_all, g_turned, got[0], other, clean_e)
-    r2 = stretch_shift(back2, -2)
-    r3 = stretch_shift(back3, -3)
-    r1 = stretch_shift(back1, -1)
+        nargs=7,
+    )(window, own_stats, far_stats, q_all, g_turned, keys, clean_e)
+    far_back = stretch_shift(far_back, -1, True)
+    near_back = stretch_shift(near_back, -1, False)
     noisy_grads, own, far = kernel_call(
         noisy_grad_body,
         (
@@ -430,25 +449,33 @@
         ),
         8 * product,
         [pltpu.VMEM((2, queries, LANES), F32)],
-        nargs=10,
-    )(
-        merged, q_all, g_turned, noisy_kv, got[0], other, noisy_e, clean_ds, noisy_sum, clean_sum
-    )
+        nargs=9,
+    )(merged, q_all, g_turned, noisy_kv, keys, noisy_e, clean_ds, noisy_sum, clean_sum)
     far = core_swap(far)
     key_grad = shape((rows, LANES), BF16)
     query_grad = shape((rows, GROUP * LANES), BF16)
-    inner, clean_grads, grad_v, grad_cv = kernel_call(
-        clean_total_body,
-        (shape((8, rows), F32), shape((rows, 2 * LANES), F32), key_grad, key_grad),
+    own_clean, far_clean = kernel_call(
+        join_body,
+        (shape((rows, 2 * LANES), F32), shape((rows, 2 * LANES), BF16)),
         10**10,
-        nargs=7,
-    )(clean_k, noisy_k, k_gain, noisy_grads, r1, r2, r3)
-    attn_out, dq, inner = kernel_call(
+        nargs=2,
+    )(far_back, near_back)
+    far_clean = core_swap(far_clean)
+    attn_out, dq, clean_grads, grad_v, grad_cv, inner = kernel_call(
         inner_body,
-        (query_grad, shape((rows, GROUP * LANES), F32), shape((peers, 8, rows), F32)),
+        (
+            query_grad,
+            shape((rows, GROUP * LANES), F32),
+            shape((rows, 2 * LANES), F32),
+            key_grad,
+            key_grad,
+            shape((peers, 3, rows), F32),
+        ),
         10**6,
-        nargs=5,
-    )(own, far, noisy_q, q_gain, inner)
+        nargs=10,
+    )(
+        own, far, own_clean, far_clean, noisy_grads, noisy_q, noisy_k, clean_k, q_gain, k_gain
+    )
     inner = head_exchange(inner)
     grad_q, grad_k, grad_ck = kernel_call(
         finish_body, (query_grad, key_grad, key_grad), 10**6, nargs=10

time: 87.1 us -> 85.5 us (0.982)
  the two profiles are of different devices: /device:TPU:208 before, /device:TPU:256 now
where the time goes in v4:
time: 85.5 us; the launch traced here: 85 us
  waiting for transfers between devices  31.1 us (36%)
  starting transfers between devices  29.9 us (35%)
  Pallas kernels  13.1 us (15%)
  blocking collectives  9.88 us (12%)
  between operations  0.88 us (1%)
    ppermute x4, waiting for transfers between devices, stretch_shift(): return lax.ppermute(value, 'seq', pairs)  22 us
    ppermute x5, starting transfers between devices, core_swap(): return lax.ppermute(value, 'seq', [(i, i ^ 1) for i in range(count)])  15.9 us
    all_to_all x1, blocking collectives, head_exchange(): return lax.all_to_all(value, 'head', 0, 0)  9.88 us
    ppermute x4, starting transfers between devices, stretch_shift(): return lax.ppermute(value, 'seq', pairs)  8.68 us
    all_to_all x1, waiting for transfers between devices, head_exchange(): return lax.all_to_all(value, 'head', 0, 0)  6.29 us
    all_to_all x1, starting transfers between devices, head_exchange(): return lax.all_to_all(value, 'head', 0, 0)  5.31 us
    ppermute x5, waiting for transfers between devices, core_swap(): return lax.ppermute(value, 'seq', [(i, i ^ 1) for i in range(count)])  2.81 us
    pallas_call x1, Pallas kernels, on_device(): kernel_call(clean_grad_body, (pair_grad, pair_grad, pair, stats), 8 * pro...  2.68 us
  transfers between devices with their start and end apart: 10, of which 6 were waited for; matrix products, arithmetic and copies ran while one was open for 0% of the time, Pallas kernels for 4%

profile of v4, /device:TPU:256, one launch (start us, length us, event | category | flops | bytes accessed | tf_op | source)
XLA Modules:
  0.0 85.0 jit_solution(6539801661523879608)
XLA Ops:
  0.6 0.0 copy-start.2
  0.7 2.1 %shard_map.136 = f32[8,3,260]{2,1,0:T(4,128)} custom-call(bf16[260,384]{1,0:T(8,128)(2,1)} %q_ref.7, bf16[260,128]{1,0:T(8,128)(2,1)} %k_ref.7, bf16[260,128]{1,0:T(8,128)(2,1)} %c_ref.7), custom_call_target="tpu_custom_call" | custom-call | flops 10000000000 | bytes 1000000 | tf_op jit(solution)/shard_map/pallas_call | solution.py:387
  2.8 5.3 %all-to-all-start = ((f32[8,3,260]{2,1,0:T(4,128)}), f32[8,3,260]{2,1,0:T(4,128)S(1)}, u32[]{:S(2)}, u32[]{:S(2)}) async-start(f32[8,3,260]{2,1,0:T(4,128)} %shard_map.136), calls=%async_computation | async-start | bytes 98304 | tf_op jit(solution)/shard_map/all_to_all | solution.py:351
  8.2 6.3 %all-to-all-done.sums_ref = f32[8,3,260]{2,1,0:T(4,128)S(1)} async-done(((f32[8,3,260]{2,1,0:T(4,128)}), f32[8,3,260]{2,1,0:T(4,128)S(1)}, u32[]{:S(2)}, u32[]{:S(2)}) %all-to-all-start) | async-done | bytes 24992 | tf_op jit(solution)/shard_map/all_to_all | solution.py:351
  14.5 0.4 shard_map.137
  14.9 1.9 %collective-permute-start.3 = (bf16[1632,128]{1,0:T(8,128)(2,1)S(1)}, bf16[1632,128]{1,0:T(8,128)(2,1)S(1)}, u32[]{:S(2)}, u32[]{:S(2)}) collective-permute-start(bf16[1632,128]{1,0:T(8,128)(2,1)S(1)} %get-tuple-element.37.own), channel_id=1, source_target_pairs={{0,8},{8,0},{16,24},{24,16},{32,40},{40,32},{48,56},{56,48},{64,72... | collective-permute-start | bytes 1253384 | tf_op jit(solution)/shard_map/ppermute | solution.py:369
  16.9 2.4 %collective-permute-start = (bf16[272,256]{1,0:T(8,128)(2,1)S(1)}, bf16[272,256]{1,0:T(8,128)(2,1)S(1)}, u32[]{:S(2)}, u32[]{:S(2)}) collective-permute-start(bf16[272,256]{1,0:T(8,128)(2,1)S(1)} %get-tuple-element.36.own), channel_id=1, source_target_pairs={{0,8},{8,0},{16,24},{24,16},{32,40},{40,32},{48,56},{56,48},{64,72... | collective-permute-start | bytes 417800 | tf_op jit(solution)/shard_map/ppermute | solution.py:369
  19.3 1.0 %collective-permute-done.far = bf16[272,256]{1,0:T(8,128)(2,1)S(1)} collective-permute-done((bf16[272,256]{1,0:T(8,128)(2,1)S(1)}, bf16[272,256]{1,0:T(8,128)(2,1)S(1)}, u32[]{:S(2)}, u32[]{:S(2)}) %collective-permute-start) | collective-permute-done | bytes 139296 | tf_op jit(solution)/shard_map/ppermute | solution.py:369
  20.3 0.7 collective-permute-start.2
  21.0 4.5 %collective-permute-start.1 = (bf16[2,272,256]{2,1,0:T(8,128)(2,1)S(1)}, bf16[2,272,256]{2,1,0:T(8,128)(2,1)S(1)}, u32[]{:S(2)}, u32[]{:S(2)}) collective-permute-start(bf16[2,272,256]{2,1,0:T(8,128)(2,1)S(1)} %shard_map.138), channel_id=1, source_target_pairs={{0,16},{8,56},{16,32},{24,72},{32,48},{40,88},{48,64},{56,104},{64... | collective-permute-start | bytes 835592 | tf_op jit(solution)/shard_map/ppermute | solution.py:364
  25.5 0.1 copy.16.window_ref
  25.6 0.0 collective-permute-done.3.far
  25.6 1.0 %shard_map.139 = (bf16[1664,128]{1,0:T(8,128)(2,1)S(1)}, bf16[128,1664]{1,0:T(8,128)(2,1)S(1)}, bf16[272,1664]{1,0:T(8,128)(2,1)S(1)}, f32[128,1664]{1,0:T(8,128)S(1)}, f32[8,1664]{1,0:T(8,128)S(1)}) custom-call(bf16[1632,128]{1,0:T(8,128)(2,1)S(1)} %get-tuple-element.37.own, bf16[1632,128]{1,0:T(8,128)(2,1)S(1)} %collective-permute-done.3.far, ...), custom_call_target="tpu_custom_call" | custom-call | flops 463470592 | bytes 2662400 | tf_op jit(solution)/shard_map/pallas_call | solution.py:410
  26.5 0.0 collective-permute-done.2.far
  26.5 15.2 %collective-permute-done.1.near = bf16[2,272,256]{2,1,0:T(8,128)(2,1)S(1)} collective-permute-done((bf16[2,272,256]{2,1,0:T(8,128)(2,1)S(1)}, bf16[2,272,256]{2,1,0:T(8,128)(2,1)S(1)}, u32[]{:S(2)}, u32[]{:S(2)}) %collective-permute-start.1) | collective-permute-done | bytes 278560 | tf_op jit(solution)/shard_map/ppermute | solution.py:364
  41.8 2.5 %shard_map.140 = (bf16[2,272,256]{2,1,0:T(8,128)(2,1)S(1)}, bf16[2,272,1664]{2,1,0:T(8,128)(2,1)S(1)}, f32[128,1664]{1,0:T(8,128)S(1)}, f32[8,1664]{1,0:T(8,128)S(1)}) custom-call(s32[32,2]{1,0:T(8,128)S(1)} %copy.16.window_ref, bf16[2,272,256]{2,1,0:T(8,128)(2,1)S(1)} %collective-permute-done.1.near, bf16[2,272,256]{2,1,0:T(8,128)(2,1)S(1)} %collective-permute-done.2.far, ...), custom_call_target="tpu_custom_call" | custom-call | flops 926941184 | bytes 2994176 | tf_op jit(solution)/shard_map/pallas_call | solution.py:424
  44.3 2.5 %collective-permute-start.4 = (f32[8,1664]{1,0:T(8,128)S(1)}, f32[8,1664]{1,0:T(8,128)S(1)}, u32[]{:S(2)}, u32[]{:S(2)}) collective-permute-start(f32[8,1664]{1,0:T(8,128)S(1)} %get-tuple-element.42.own), channel_id=1, source_target_pairs={{0,8},{8,0},{16,24},{24,16},{32,40},{40,32},{48,56},{56,48},{64,72... | collective-permute-start | bytes 159752 | tf_op jit(solution)/shard_map/ppermute | solution.py:369
  46.8 0.9 %collective-permute-done.4.far = f32[8,1664]{1,0:T(8,128)S(1)} collective-permute-done((f32[8,1664]{1,0:T(8,128)S(1)}, f32[8,1664]{1,0:T(8,128)S(1)}, u32[]{:S(2)}, u32[]{:S(2)}) %collective-permute-start.4) | collective-permute-done | bytes 53280 | tf_op jit(solution)/shard_map/ppermute | solution.py:369
  47.6 2.7 %shard_map.141 = (bf16[2,260,256]{2,1,0:T(8,128)(2,1)S(1)}, bf16[2,260,256]{2,1,0:T(8,128)(2,1)S(1)}, bf16[2,272,1664]{2,1,0:T(8,128)(2,1)S(1)}, f32[8,1664]{1,0:T(8,128)S(1)}) custom-call(s32[32,2]{1,0:T(8,128)S(1)} %copy.16.window_ref, f32[8,1664]{1,0:T(8,128)S(1)} %get-tuple-element.42.own, f32[8,1664]{1,0:T(8,128)S(1)} %collective-permute-done.4.far, ...), custom_call_target="tpu_custom_call" | custom-call | flops 926941184 | bytes 2396160 | tf_op jit(solution)/shard_map/pallas_call | solution.py:434
  50.3 0.7 collective-permute-start.6
  51.0 2.8 %collective-permute-start.7 = (bf16[2,260,256]{2,1,0:T(8,128)(2,1)S(1)}, bf16[2,260,256]{2,1,0:T(8,128)(2,1)S(1)}, u32[]{:S(2)}, u32[]{:S(2)}) collective-permute-start(bf16[2,260,256]{2,1,0:T(8,128)(2,1)S(1)} %get-tuple-element.53), channel_id=1, source_target_pairs={{16,0},{32,16},{48,32},{56,8},{64,48},{72,24},{80,64},{88,40},{96,... | collective-permute-start | bytes 798728 | tf_op jit(solution)/shard_map/ppermute | solution.py:364
  53.8 1.9 %shard_map.142 = (f32[260,256]{1,0:T(8,128)S(1)}, f32[1632,128]{1,0:T(8,128)S(1)}, bf16[1632,128]{1,0:T(8,128)(2,1)S(1)}) custom-call(f32[8,1664]{1,0:T(8,128)S(1)} %get-tuple-element.45.merged, bf16[1664,128]{1,0:T(8,128)(2,1)S(1)} %get-tuple-element.39.q_ref, bf16[128,1664]{1,0:T(8,128)(2,1)S(1)} %get-tuple-element.40.gt_ref, ...), custom_call_target="tpu_custom_call" | custom-call | flops 926941184 | bytes 1519616 | tf_op jit(solution)/shard_map/pallas_call | solution.py:443
  55.8 4.3 %collective-permute-start.5 = (bf16[1632,128]{1,0:T(8,128)(2,1)S(1)}, bf16[1632,128]{1,0:T(8,128)(2,1)S(1)}, u32[]{:S(2)}, u32[]{:S(2)}) collective-permute-start(bf16[1632,128]{1,0:T(8,128)(2,1)S(1)} %get-tuple-element.51), channel_id=1, source_target_pairs={{0,8},{8,0},{16,24},{24,16},{32,40},{40,32},{48,56},{56,48},{64,72... | collective-permute-start | bytes 1253384 | tf_op jit(solution)/shard_map/ppermute | solution.py:369
  60.1 0.0 collective-permute-done.6.far
  60.1 6.8 %collective-permute-done.7.near = bf16[2,260,256]{2,1,0:T(8,128)(2,1)S(1)} collective-permute-done((bf16[2,260,256]{2,1,0:T(8,128)(2,1)S(1)}, bf16[2,260,256]{2,1,0:T(8,128)(2,1)S(1)}, u32[]{:S(2)}, u32[]{:S(2)}) %collective-permute-start.7) | collective-permute-done | bytes 266272 | tf_op jit(solution)/shard_map/ppermute | solution.py:364
  66.9 0.1 shard_map.143
  66.9 4.9 %collective-permute-start.8 = (bf16[260,256]{1,0:T(8,128)(2,1)S(1)}, bf16[260,256]{1,0:T(8,128)(2,1)S(1)}, u32[]{:S(2)}, u32[]{:S(2)}) collective-permute-start(bf16[260,256]{1,0:T(8,128)(2,1)S(1)} %get-tuple-element.55), channel_id=1, source_target_pairs={{0,8},{8,0},{16,24},{24,16},{32,40},{40,32},{48,56},{56,48},{64,72... | collective-permute-start | bytes 399368 | tf_op jit(solution)/shard_map/ppermute | solution.py:369
  71.8 1.0 %collective-permute-done.8.far_clean = bf16[260,256]{1,0:T(8,128)(2,1)S(1)} collective-permute-done((bf16[260,256]{1,0:T(8,128)(2,1)S(1)}, bf16[260,256]{1,0:T(8,128)(2,1)S(1)}, u32[]{:S(2)}, u32[]{:S(2)}) %collective-permute-start.8) | collective-permute-done | bytes 133152 | tf_op jit(solution)/shard_map/ppermute | solution.py:369
  72.8 0.0 collective-permute-done.5.far
  72.8 1.1 %shard_map.144 = (bf16[260,384]{1,0:T(8,128)(2,1)}, f32[260,384]{1,0:T(8,128)S(1)}, f32[260,256]{1,0:T(8,128)S(1)}, bf16[260,128]{1,0:T(8,128)(2,1)}, bf16[260,1...) custom-call(f32[1632,128]{1,0:T(8,128)S(1)} %get-tuple-element.50.own, bf16[1632,128]{1,0:T(8,128)(2,1)S(1)} %collective-permute-done.5.far, ...), custom_call_target="tpu_custom_call" | custom-call | flops 1000000 | bytes 1023360 | tf_op jit(solution)/shard_map/pallas_call | solution.py:464
  73.9 9.9 %all_to_all.10.inner_ref = f32[8,3,260]{2,1,0:T(4,128)S(1)} all-to-all(f32[8,3,260]{2,1,0:T(4,128)S(1)} %get-tuple-element.58), channel_id=1, replica_groups=mesh['seq'=64,'head'=8] {'head'}, dimensions={0} | all-to-all | bytes 49920 | tf_op jit(solution)/shard_map/all_to_all | solution.py:351
  83.8 1.3 %shard_map.145 = (bf16[260,384]{1,0:T(8,128)(2,1)}, bf16[260,128]{1,0:T(8,128)(2,1)}, bf16[260,128]{1,0:T(8,128)(2,1)}) custom-call(f32[8,3,260]{2,1,0:T(4,128)S(1)} %all-to-all-done.sums_ref, f32[8,3,260]{2,1,0:T(4,128)S(1)} %all_to_all.10.inner_ref, bf16[260,384]{1,0:T(8,128)(2,1)S(1)} %copy-done, bf16[260,128]{1,0:T(8,128)(2,1)S(1)} %copy-done.1, ...), custom_call_target="tpu_custom_call" | custom-call | flops 1000000 | bytes 332800 | tf_op jit(solution)/shard_map/pallas_call | solution.py:480
  (19 shorter events, 0.1 us)
Async XLA Ops:
  0.6 13.8 %copy-start.2 = (bf16[260,128]{1,0:T(8,128)(2,1)S(1)}, bf16[260,128]{1,0:T(8,128)(2,1)}, u32[]{:S(2)}) copy-start(bf16[260,128]{1,0:T(8,128)(2,1)} %c_ref.7) | copy-start | bytes 199684
  0.6 13.8 %copy-start.1 = (bf16[260,128]{1,0:T(8,128)(2,1)S(1)}, bf16[260,128]{1,0:T(8,128)(2,1)}, u32[]{:S(2)}) copy-start(bf16[260,128]{1,0:T(8,128)(2,1)} %k_ref.7) | copy-start | bytes 199684
  0.7 13.8 %copy-start = (bf16[260,384]{1,0:T(8,128)(2,1)S(1)}, bf16[260,384]{1,0:T(8,128)(2,1)}, u32[]{:S(2)}) copy-start(bf16[260,384]{1,0:T(8,128)(2,1)} %q_ref.7) | copy-start | bytes 599044
  0.7 7.5 %copy-start.7 = (f32[384]{0:T(512)S(1)}, f32[384]{0:T(512)}, u32[]{:S(2)}) copy-start(f32[384]{0:T(512)} %param.14) | copy-start | bytes 4612
  0.7 13.8 %copy-start.3 = (bf16[260,384]{1,0:T(8,128)(2,1)S(1)}, bf16[260,384]{1,0:T(8,128)(2,1)}, u32[]{:S(2)}) copy-start(bf16[260,384]{1,0:T(8,128)(2,1)} %g_ref.1) | copy-start | bytes 599044
  0.7 13.8 %copy-start.6 = (f32[128]{0:T(128)S(1)}, f32[128]{0:T(128)}, u32[]{:S(2)}) copy-start(f32[128]{0:T(128)} %param.15) | copy-start | bytes 1540
  0.7 13.8 %copy-start.5 = (bf16[260,128]{1,0:T(8,128)(2,1)S(1)}, bf16[260,128]{1,0:T(8,128)(2,1)}, u32[]{:S(2)}) copy-start(bf16[260,128]{1,0:T(8,128)(2,1)} %cv_ref.1) | copy-start | bytes 199684
  0.7 13.8 %copy-start.4 = (bf16[260,128]{1,0:T(8,128)(2,1)S(1)}, bf16[260,128]{1,0:T(8,128)(2,1)}, u32[]{:S(2)}) copy-start(bf16[260,128]{1,0:T(8,128)(2,1)} %v_ref.1) | copy-start | bytes 199684
  0.7 24.8 %copy-start.8 = (s32[32,2]{0,1:T(2,128)S(1)}, s32[32,2]{0,1:T(2,128)}, u32[]{:S(2)}) copy-start(s32[32,2]{0,1:T(2,128)} %param.17) | copy-start | bytes 772
  2.8 11.6 %all-to-all-start = ((f32[8,3,260]{2,1,0:T(4,128)}), f32[8,3,260]{2,1,0:T(4,128)S(1)}, u32[]{:S(2)}, u32[]{:S(2)}) async-start(f32[8,3,260]{2,1,0:T(4,128)} %shard_map.136), calls=%async_computation | async-start | bytes 98304 | tf_op jit(solution)/shard_map/all_to_all | solution.py:351
  14.9 10.6 %collective-permute-start.3 = (bf16[1632,128]{1,0:T(8,128)(2,1)S(1)}, bf16[1632,128]{1,0:T(8,128)(2,1)S(1)}, u32[]{:S(2)}, u32[]{:S(2)}) collective-permute-start(bf16[1632,128]{1,0:T(8,128)(2,1)S(1)} %get-tuple-element.37.own), channel_id=1, source_target_pairs={{0,8},{8,0},{16,24},{24,16},{32,40},{40,32},{48,56},{56,48},{64,72... | collective-permute-start | bytes 1253384 | tf_op jit(solution)/shard_map/ppermute | solution.py:369
  16.9 3.4 %collective-permute-start = (bf16[272,256]{1,0:T(8,128)(2,1)S(1)}, bf16[272,256]{1,0:T(8,128)(2,1)S(1)}, u32[]{:S(2)}, u32[]{:S(2)}) collective-permute-start(bf16[272,256]{1,0:T(8,128)(2,1)S(1)} %get-tuple-element.36.own), channel_id=1, source_target_pairs={{0,8},{8,0},{16,24},{24,16},{32,40},{40,32},{48,56},{56,48},{64,72... | collective-permute-start | bytes 417800 | tf_op jit(solution)/shard_map/ppermute | solution.py:369
  20.3 6.3 %collective-permute-start.2 = (bf16[2,272,256]{2,1,0:T(8,128)(2,1)S(1)}, bf16[2,272,256]{2,1,0:T(8,128)(2,1)S(1)}, u32[]{:S(2)}, u32[]{:S(2)}) collective-permute-start(bf16[2,272,256]{2,1,0:T(8,128)(2,1)S(1)} %shard_map.138), channel_id=1, source_target_pairs={{8,40},{24,56},{40,72},{56,88},{72,104},{88,120},{104,136},{120,15... | collective-permute-start | bytes 835592 | tf_op jit(solution)/shard_map/ppermute | solution.py:364
  21.0 20.8 %collective-permute-start.1 = (bf16[2,272,256]{2,1,0:T(8,128)(2,1)S(1)}, bf16[2,272,256]{2,1,0:T(8,128)(2,1)S(1)}, u32[]{:S(2)}, u32[]{:S(2)}) collective-permute-start(bf16[2,272,256]{2,1,0:T(8,128)(2,1)S(1)} %shard_map.138), channel_id=1, source_target_pairs={{0,16},{8,56},{16,32},{24,72},{32,48},{40,88},{48,64},{56,104},{64... | collective-permute-start | bytes 835592 | tf_op jit(solution)/shard_map/ppermute | solution.py:364
  44.3 3.3 %collective-permute-start.4 = (f32[8,1664]{1,0:T(8,128)S(1)}, f32[8,1664]{1,0:T(8,128)S(1)}, u32[]{:S(2)}, u32[]{:S(2)}) collective-permute-start(f32[8,1664]{1,0:T(8,128)S(1)} %get-tuple-element.42.own), channel_id=1, source_target_pairs={{0,8},{8,0},{16,24},{24,16},{32,40},{40,32},{48,56},{56,48},{64,72... | collective-permute-start | bytes 159752 | tf_op jit(solution)/shard_map/ppermute | solution.py:369
  50.3 9.8 %collective-permute-start.6 = (bf16[2,260,256]{2,1,0:T(8,128)(2,1)S(1)}, bf16[2,260,256]{2,1,0:T(8,128)(2,1)S(1)}, u32[]{:S(2)}, u32[]{:S(2)}) collective-permute-start(bf16[2,260,256]{2,1,0:T(8,128)(2,1)S(1)} %get-tuple-element.52), channel_id=1, source_target_pairs={{40,8},{56,24},{72,40},{88,56},{104,72},{120,88},{136,104},{152,12... | collective-permute-start | bytes 798728 | tf_op jit(solution)/shard_map/ppermute | solution.py:364
  51.0 15.9 %collective-permute-start.7 = (bf16[2,260,256]{2,1,0:T(8,128)(2,1)S(1)}, bf16[2,260,256]{2,1,0:T(8,128)(2,1)S(1)}, u32[]{:S(2)}, u32[]{:S(2)}) collective-permute-start(bf16[2,260,256]{2,1,0:T(8,128)(2,1)S(1)} %get-tuple-element.53), channel_id=1, source_target_pairs={{16,0},{32,16},{48,32},{56,8},{64,48},{72,24},{80,64},{88,40},{96,... | collective-permute-start | bytes 798728 | tf_op jit(solution)/shard_map/ppermute | solution.py:364
  55.8 17.0 %collective-permute-start.5 = (bf16[1632,128]{1,0:T(8,128)(2,1)S(1)}, bf16[1632,128]{1,0:T(8,128)(2,1)S(1)}, u32[]{:S(2)}, u32[]{:S(2)}) collective-permute-start(bf16[1632,128]{1,0:T(8,128)(2,1)S(1)} %get-tuple-element.51), channel_id=1, source_target_pairs={{0,8},{8,0},{16,24},{24,16},{32,40},{40,32},{48,56},{56,48},{64,72... | collective-permute-start | bytes 1253384 | tf_op jit(solution)/shard_map/ppermute | solution.py:369
  66.9 5.8 %collective-permute-start.8 = (bf16[260,256]{1,0:T(8,128)(2,1)S(1)}, bf16[260,256]{1,0:T(8,128)(2,1)S(1)}, u32[]{:S(2)}, u32[]{:S(2)}) collective-permute-start(bf16[260,256]{1,0:T(8,128)(2,1)S(1)} %get-tuple-element.55), channel_id=1, source_target_pairs={{0,8},{8,0},{16,24},{24,16},{32,40},{40,32},{48,56},{56,48},{64,72... | collective-permute-start | bytes 399368 | tf_op jit(solution)/shard_map/ppermute | solution.py:369

commit v5 on v4

--- a/solution.py
+++ b/solution.py
@@ -62,12 +62,13 @@
 
 
 def to_rows(x):
-    row = lax.broadcasted_iota(jnp.int32, (3, 3 * LANES), 0)
-    group = lax.broadcasted_iota(jnp.int32, (3, 3 * LANES), 1) // LANES
+    count = x.shape[0]
+    row = lax.broadcasted_iota(jnp.int32, (count, count * LANES), 0)
+    group = lax.broadcasted_iota(jnp.int32, (count, count * LANES), 1) // LANES
     pick = (row == group).astype(BF16)
     high, low = halves(x)
     rows = dot(high, pick, 0, 0) + dot(low, pick, 0, 0)
-    return [rows[:, i * LANES : (i + 1) * LANES] for i in range(3)]
+    return [rows[:, i * LANES : (i + 1) * LANES] for i in range(count)]
 
 
 def added(ref):
@@ -77,61 +78,51 @@
     return total
 
 
-def inverses(ref):
-    sums = to_rows(added(ref))
-    widths = (HQ * HEAD_SIZE, KEY_VALUE_HEADS * HEAD_SIZE, KEY_VALUE_HEADS * HEAD_SIZE)
-    return [lax.rsqrt(s / w + EPSILON) for s, w in zip(sums, widths)]
-
-
-def squares_body(q_ref, k_ref, c_ref, out_ref):
-    rows = None
-    for i, ref in enumerate((q_ref, k_ref, c_ref)):
-        x = ref[...].astype(F32)
-        part = to_lanes(x * x, i)
-        rows = part if rows is None else rows + part
-    for peer in range(out_ref.shape[0]):
-        out_ref[peer] = rows[:3]
-
-
-def norms_body(
-    sums_ref, q_ref, k_ref, c_ref, v_ref, cv_ref, g_ref, q_gain, k_gain,
-    noisy_ref, clean_ref, out, wide, tall,
-):
-    q_inv, k_inv, c_inv = inverses(sums_ref)
+def inverse(sums, heads):
+    return lax.rsqrt(sums / (heads * HEAD_SIZE) + EPSILON)
+
+
+def pack_body(q_ref, g_ref, c_ref, v_ref, out, wide):
+    rows = c_ref.shape[0]
+    slot = up(rows, PAD)
+    wide[0:rows, :LANES] = c_ref[...].astype(F32)
+    wide[0:rows, LANES:] = v_ref[...].astype(F32)
+    wide[rows:slot] = jnp.zeros((slot - rows, 2 * LANES), F32)
+    for h in range(GROUP):
+        cols = slice(h * HEAD_SIZE, (h + 1) * HEAD_SIZE)
+        at = (1 + h) * slot
+        wide[at : at + rows, :LANES] = q_ref[:, cols].astype(F32)
+        wide[at : at + rows, LANES:] = g_ref[:, cols].astype(F32)
+        wide[at + rows : at + slot] = jnp.zeros((slot - rows, 2 * LANES), F32)
+    out[...] = wide[...].astype(BF16)
+
+
+def pair_body(own, far, out):
+    out[0] = own[...]
+    out[1] = far[...]
+
+
+def squares_body(own, far, k_ref, out_ref):
     rows = k_ref.shape[0]
     slot = up(rows, PAD)
-    wide[rows:] = jnp.zeros((slot - rows, 2 * LANES), F32)
-    wide[0:rows, 0:LANES] = c_ref[...].astype(F32) * c_inv * k_gain[...]
-    wide[0:rows, LANES:] = cv_ref[...].astype(F32)
-    clean_ref[...] = wide[...].astype(BF16)
-    wide[0:rows, 0:LANES] = k_ref[...].astype(F32) * k_inv * k_gain[...]
-    wide[0:rows, LANES:] = v_ref[...].astype(F32)
-    noisy_ref[...] = wide[...].astype(BF16)
-    for h in range(2 * GROUP):
-        tall[h * slot + rows : (h + 1) * slot] = jnp.zeros((slot - rows, LANES), F32)
-    for h in range(GROUP):
-        cols = slice(h * HEAD_SIZE, (h + 1) * HEAD_SIZE)
-        gain = q_gain[:, cols] * (SCORE_SCALE * LOG2E)
-        tall[h * slot : h * slot + rows, :] = q_ref[:, cols].astype(F32) * q_inv * gain
-        at = (GROUP + h) * slot
-        tall[at : at + rows, :] = g_ref[:, cols].astype(F32)
-    out[...] = tall[...].astype(BF16)
-
-
-def both(out, own, far, first, span):
-    core = lax.axis_index("seq") % 2
-
-    @pl.when(core == 0)
-    def _():
-        out[0:span] = own[first : first + span]
-        out[span : 2 * span] = far[first : first + span]
-
-    @pl.when(core == 1)
-    def _():
-        out[0:span] = far[first : first + span]
-        out[span : 2 * span] = own[first : first + span]
-
-    out[2 * span :] = jnp.zeros((out.shape[0] - 2 * span, out.shape[1]), out.dtype)
+    part = None
+    for i, ref in enumerate((own, far)):
+        x = ref[:, :LANES].astype(F32)
+        x = x * x
+        total = x[slot : 2 * slot]
+        for h in range(1, GROUP):
+            total = total + x[(1 + h) * slot : (2 + h) * slot]
+        add = to_lanes(total, i) + to_lanes(x[0:slot], 2 + i)
+        part = add if part is None else part + add
+    x = k_ref[...].astype(F32)
+    last = to_lanes(x * x, 4)
+    for peer in range(out_ref.shape[0]):
+        out_ref[peer, :, 0:rows] = part[:, :rows] + last
+        out_ref[peer, :, rows:] = jnp.zeros((8, slot - rows), F32)
+
+
+def clean_sums_body(sums_ref, out):
+    out[...] = added(sums_ref)[2:4]
 
 
 def listed(window_ref):
@@ -154,13 +145,32 @@
     return s[:whole], jnp.where(real, tail, HIDDEN)
 
 
-def noisy_body(own, far, keys, q_out, gt_out, e_out, sum_out, stats, g_rows):
-    span = own.shape[0] // 2
-    both(q_out, own, far, 0, span)
-    both(g_rows, own, far, span, span)
-    gt = g_rows[...].astype(F32).T
+def noisy_body(
+    sums_ref, own, far, k_ref, v_ref, q_gain, k_gain,
+    q_out, gt_out, keys, e_out, sum_out, stats, tall, wide,
+):
+    rows = k_ref.shape[0]
+    slot = up(rows, PAD)
+    span = GROUP * slot
+    own_sum, far_sum, _, _, k_sum = to_rows(added(sums_ref)[:5])
+    first = lax.axis_index("seq") % 2
+    tall[...] = jnp.zeros_like(tall)
+    for ref, sums, core in ((own, own_sum, first), (far, far_sum, 1 - first)):
+        inv = inverse(sums, HQ)
+        for h in range(GROUP):
+            gain = q_gain[:, h * HEAD_SIZE : (h + 1) * HEAD_SIZE] * (SCORE_SCALE * LOG2E)
+            x = ref[(1 + h) * slot : (2 + h) * slot].astype(F32)
+            at = pl.ds(pl.multiple_of(core * span + h * slot, 8), slot)
+            tall[at, :LANES] = x[:, :LANES] * inv * gain
+            tall[at, LANES:] = x[:, LANES:]
+    q_out[...] = tall[:, :LANES].astype(BF16)
+    gt = tall[:, LANES:].T
     gt_out[...] = gt.astype(BF16)
-    body, tail = scores(keys, q_out[...], TOKENS)
+    wide[rows:] = jnp.zeros((slot - rows, 2 * LANES), F32)
+    wide[0:rows, :LANES] = k_ref[...].astype(F32) * inverse(k_sum, KEY_VALUE_HEADS)[:rows] * k_gain[...]
+    wide[0:rows, LANES:] = v_ref[...].astype(F32)
+    keys[...] = wide[...].astype(BF16)
+    body, tail = scores(keys, q_out[...], rows)
     whole = body.shape[0]
     top = jnp.maximum(
         jnp.max(body, axis=0, keepdims=True), jnp.max(tail, axis=0, keepdims=True)
@@ -178,25 +188,28 @@
     stats[2:3] = jnp.sum(gt * sums, axis=0, keepdims=True)
 
 
-def pair_body(own, far, out):
-    out[0] = own[...]
-    out[1] = far[...]
-
-
 def clean_body(
-    window_ref, near, far, q_ref, gt_ref, noisy_stats, keys, e_out, sum_out, stats, s_ref
+    window_ref, near, far, near_sums, far_sums, k_gain, q_ref, gt_ref, noisy_stats,
+    keys, e_out, sum_out, stats, s_ref,
 ):
     use1, use2, use3 = listed(window_ref)
     first = lax.axis_index("seq") % 2 == 0
     from_far = jnp.logical_not(first) & use2
 
+    def norm(ref, sums_ref):
+        for j, sums in enumerate(to_rows(sums_ref[...])):
+            inv = inverse(sums, KEY_VALUE_HEADS)
+            raw = ref[j, :, :LANES].astype(F32)
+            keys[j, :, :LANES] = (raw * inv * k_gain[...]).astype(BF16)
+            keys[j, :, LANES:] = ref[j, :, LANES:]
+
     @pl.when(from_far)
     def _():
-        keys[...] = far[...]
+        norm(far, far_sums)
 
     @pl.when(jnp.logical_not(from_far))
     def _():
-        keys[...] = near[...]
+        norm(near, near_sums)
 
     hide = jnp.where(jnp.where(first, use1, use2 | use3), 0.0, HIDDEN)
     q = q_ref[...]
@@ -328,7 +341,11 @@
     sums_ref, inner_ref, q_ref, k_ref, c_ref, q_gain, k_gain, dq_ref, noisy_ref, clean_ref,
     grad_q, grad_k, grad_ck,
 ):
-    q_inv, k_inv, c_inv = inverses(sums_ref)
+    rows = q_ref.shape[0]
+    q_inv, _, c_inv, _, k_inv = [x[:rows] for x in to_rows(added(sums_ref)[:5])]
+    q_inv = inverse(q_inv, HQ)
+    k_inv = inverse(k_inv, KEY_VALUE_HEADS)
+    c_inv = inverse(c_inv, KEY_VALUE_HEADS)
     q_sum, k_sum, c_sum = to_rows(added(inner_ref))
     q_pull = q_inv * q_inv * q_inv * (q_sum / (HQ * HEAD_SIZE))
     for h in range(GROUP):
@@ -383,43 +400,52 @@
     stats = shape((8, queries), F32)
     turned = shape((LANES, queries), F32)
 
-    fetched = (noisy_q, noisy_k, clean_k)
-    sums = pl.pallas_call(
-        squares_body,
+    fetched = (noisy_q, out_grad, clean_k, clean_value)
+    packed = ((1 + GROUP) * slot, 2 * LANES)
+    own = pl.pallas_call(
+        pack_body,
         grid=(1,),
-        out_shape=shape((peers, 3, rows), F32),
+        out_shape=shape(packed, BF16),
         in_specs=[pl.BlockSpec(a.shape, lambda i: (0, 0)) for a in fetched],
-        out_specs=pl.BlockSpec((peers, 3, rows), lambda i: (0, 0, 0)),
-        compiler_params=pltpu.CompilerParams(vmem_limit_bytes=60 * 2**20),
+        out_specs=pl.BlockSpec(packed, lambda i: (0, 0)),
+        scratch_shapes=[pltpu.VMEM(packed, F32)],
+        compiler_params=pltpu.CompilerParams(vmem_limit_bytes=58 * 2**20),
         cost_estimate=pl.CostEstimate(flops=10**10, bytes_accessed=10**6, transcendentals=0),
     )(*fetched)
+    far = core_swap(own)
+    pair_kv = shape((2, slot, 2 * LANES), BF16)
+    clean_kv = pl.pallas_call(
+        pair_body,
+        grid=(1,),
+        out_shape=pair_kv,
+        in_specs=[pl.BlockSpec((slot, 2 * LANES), lambda i: (0, 0))] * 2,
+        out_specs=pl.BlockSpec(pair_kv.shape, lambda i: (0, 0, 0)),
+        compiler_params=pltpu.CompilerParams(vmem_limit_bytes=32 * 2**20),
+    )(own, far)
+    far_kv = stretch_shift(clean_kv, 1, True)
+    near_kv = stretch_shift(clean_kv, 1, False)
+    sums = kernel_call(squares_body, shape((peers, 8, slot), F32), 10**6, nargs=3)(
+        own, far, noisy_k
+    )
     sums = head_exchange(sums)
+    clean_sums = kernel_call(clean_sums_body, shape((2, slot), F32), 10**6, nargs=1)(sums)
+    far_sums = stretch_shift(clean_sums, 1, True)
+    near_sums = stretch_shift(clean_sums, 1, False)
     pack = shape((slot, 2 * LANES), BF16)
-    noisy_kv, clean_kv, own = kernel_call(
-        norms_body,
-        (pack, pack, shape((2 * span, LANES), BF16)),
-        10**6,
-        [pltpu.VMEM((slot, 2 * LANES), F32), pltpu.VMEM((2 * span, LANES), F32)],
-        nargs=9,
-    )(sums, noisy_q, noisy_k, clean_k, noisy_value, clean_value, out_grad, q_gain, k_gain)
-    pair_kv = shape((2, slot, 2 * LANES), BF16)
-    clean_kv = kernel_call(pair_body, pair_kv, 10**6, nargs=2)(clean_kv, core_swap(clean_kv))
-    near_kv = stretch_shift(clean_kv, 1, False)
-    far_kv = stretch_shift(clean_kv, 1, True)
-    far = core_swap(own)
-    q_all, g_turned, noisy_e, noisy_sum, noisy_stats = kernel_call(
+    q_all, g_turned, noisy_kv, noisy_e, noisy_sum, noisy_stats = kernel_call(
         noisy_body,
         (
             shape((queries, LANES), BF16),
             shape((LANES, queries), BF16),
+            pack,
             shape((slot, queries), BF16),
             turned,
             stats,
         ),
         4 * product,
-        [pltpu.VMEM((queries, LANES), BF16)],
-        nargs=3,
-    )(own, far, noisy_kv)
+        [pltpu.VMEM((queries, 2 * LANES), F32), pltpu.VMEM((slot, 2 * LANES), F32)],
+        nargs=7,
+    )(sums, own, far, noisy_k, noisy_value, q_gain, k_gain)
     pair = shape((2, slot, queries), BF16)
     keys, clean_e, clean_sum, own_stats = kernel_call(
         clean_body,
@@ -427,8 +453,8 @@
         8 * product,
         [pltpu.VMEM((2, slot, queries), F32)],
         smem=(0,),
-        nargs=6,
-    )(window, near_kv, far_kv, q_all, g_turned, noisy_stats)
+        nargs=9,
+    )(window, near_kv, far_kv, near_sums, far_sums, k_gain, q_all, g_turned, noisy_stats)
     far_stats = core_swap(own_stats)
     pair_grad = shape((2, rows, 2 * LANES), BF16)
     near_back, far_back, clean_ds, merged = kernel_call(

time: 85.5 us -> 89.3 us (1.044)
  the two profiles are of different devices: /device:TPU:256 before, /device:TPU:208 now
where the time goes in v5:
time: 89.3 us; the launch traced here: 88.7 us
  starting transfers between devices  38.2 us (43%)
  waiting for transfers between devices  22.4 us (25%)
  Pallas kernels  14.5 us (16%)
  blocking collectives  11.5 us (13%)
  local copies, waits for them, and re-layouts  1.18 us (1%)
    ppermute x4, starting transfers between devices, core_swap(): return lax.ppermute(value, 'seq', [(i, i ^ 1) for i in range(count)])  21.9 us
    ppermute x6, starting transfers between devices, stretch_shift(): return lax.ppermute(value, 'seq', pairs)  11.9 us
    all_to_all x1, blocking collectives, head_exchange(): return lax.all_to_all(value, 'head', 0, 0)  11.5 us
    ppermute x6, waiting for transfers between devices, stretch_shift(): return lax.ppermute(value, 'seq', pairs)  10.4 us
    all_to_all x1, waiting for transfers between devices, head_exchange(): return lax.all_to_all(value, 'head', 0, 0)  8.02 us
    all_to_all x1, starting transfers between devices, head_exchange(): return lax.all_to_all(value, 'head', 0, 0)  4.41 us
    ppermute x4, waiting for transfers between devices, core_swap(): return lax.ppermute(value, 'seq', [(i, i ^ 1) for i in range(count)])  3.97 us
    pallas_call x1, Pallas kernels, on_device(): kernel_call(clean_body, (pair_kv, pair, turned, stats), 8 * product, [plt...  2.83 us
  transfers between devices with their start and end apart: 11, of which 6 were waited for; matrix products, arithmetic and copies ran while one was open for 0% of the time, Pallas kernels for 5%

profile of v5, /device:TPU:208, one launch (start us, length us, event | category | flops | bytes accessed | tf_op | source)
XLA Modules:
  0.0 88.7 jit_solution(1196900447884332064)
XLA Ops:
  0.7 2.1 %shard_map.136.own = bf16[1088,256]{1,0:T(8,128)(2,1)} custom-call(bf16[260,384]{1,0:T(8,128)(2,1)} %q_ref.5, bf16[260,384]{1,0:T(8,128)(2,1)} %g_ref.1, bf16[260,128]{1,0:T(8,128)(2,1)} %c_ref.5, bf16[260,128]{1,0:T(8,128)(2,1)} %v_ref.2), custom_call_target="tpu_custom_call" | custom-call | flops 10000000000 | bytes 1000000 | tf_op jit(solution)/shard_map/pallas_call | solution.py:405
  2.8 1.9 %collective-permute-start = (bf16[1088,256]{1,0:T(8,128)(2,1)}, bf16[1088,256]{1,0:T(8,128)(2,1)S(1)}, u32[]{:S(2)}, u32[]{:S(2)}) collective-permute-start(bf16[1088,256]{1,0:T(8,128)(2,1)} %shard_map.136.own), channel_id=1, source_target_pairs={{0,8},{8,0},{16,24},{24,16},{32,40},{40,32},{48,56},{56,48},{64,72... | collective-permute-start | bytes 1671176 | tf_op jit(solution)/shard_map/ppermute | solution.py:386
  4.7 2.1 %collective-permute-done.far = bf16[1088,256]{1,0:T(8,128)(2,1)S(1)} collective-permute-done((bf16[1088,256]{1,0:T(8,128)(2,1)}, bf16[1088,256]{1,0:T(8,128)(2,1)S(1)}, u32[]{:S(2)}, u32[]{:S(2)}) %collective-permute-start) | collective-permute-done | bytes 557088 | tf_op jit(solution)/shard_map/ppermute | solution.py:386
  6.8 1.1 %copy-done = bf16[1088,256]{1,0:T(8,128)(2,1)S(1)} copy-done((bf16[1088,256]{1,0:T(8,128)(2,1)S(1)}, bf16[1088,256]{1,0:T(8,128)(2,1)}, u32[]{:S(2)}) %copy-start) | copy-done | bytes 557080
  7.9 0.8 collective-permute-start.2
  8.7 5.7 %collective-permute-start.1 = (bf16[2,272,256]{2,1,0:T(8,128)(2,1)S(1)}, bf16[2,272,256]{2,1,0:T(8,128)(2,1)S(1)}, u32[]{:S(2)}, u32[]{:S(2)}) collective-permute-start(bf16[2,272,256]{2,1,0:T(8,128)(2,1)S(1)} %shard_map.137), channel_id=1, source_target_pairs={{0,16},{8,56},{16,32},{24,72},{32,48},{40,88},{48,64},{56,104},{64... | collective-permute-start | bytes 835592 | tf_op jit(solution)/shard_map/ppermute | solution.py:381
  14.5 1.0 %shard_map.138 = f32[8,8,272]{2,1,0:T(8,128)} custom-call(bf16[1088,256]{1,0:T(8,128)(2,1)S(1)} %copy-done, bf16[1088,256]{1,0:T(8,128)(2,1)S(1)} %collective-permute-done.far, bf16[260,128]{1,0:T(8,128)(2,1)S(1)} %copy-done.3), custom_call_target="tpu_custom_call" | custom-call | flops 1000000 | bytes 69632 | tf_op jit(solution)/shard_map/pallas_call | solution.py:427
  15.5 4.4 %all-to-all-start = ((f32[8,8,272]{2,1,0:T(8,128)}), f32[8,8,272]{2,1,0:T(8,128)S(1)}, u32[]{:S(2)}, u32[]{:S(2)}) async-start(f32[8,8,272]{2,1,0:T(8,128)} %shard_map.138), calls=%async_computation | async-start | bytes 196608 | tf_op jit(solution)/shard_map/all_to_all | solution.py:368
  19.9 0.1 copy.16.window_ref
  20.0 8.0 %all-to-all-done.sums_ref = f32[8,8,272]{2,1,0:T(8,128)S(1)} async-done(((f32[8,8,272]{2,1,0:T(8,128)}), f32[8,8,272]{2,1,0:T(8,128)S(1)}, u32[]{:S(2)}, u32[]{:S(2)}) %all-to-all-start) | async-done | bytes 69664 | tf_op jit(solution)/shard_map/all_to_all | solution.py:368
  28.1 0.7 collective-permute-start.4
  28.7 1.9 %collective-permute-start.3 = (f32[2,272]{1,0:T(2,128)S(1)}, f32[2,272]{1,0:T(2,128)S(1)}, u32[]{:S(2)}, u32[]{:S(2)}) collective-permute-start(f32[2,272]{1,0:T(2,128)S(1)} %shard_map.139), channel_id=1, source_target_pairs={{0,16},{8,56},{16,32},{24,72},{32,48},{40,88},{48,64},{56,104},{64... | collective-permute-start | bytes 6536 | tf_op jit(solution)/shard_map/ppermute | solution.py:381
  30.7 1.5 %shard_map.140 = (bf16[1664,128]{1,0:T(8,128)(2,1)S(1)}, bf16[128,1664]{1,0:T(8,128)(2,1)S(1)}, bf16[272,256]{1,0:T(8,128)(2,1)S(1)}, bf16[272,1664]{1,0:T(8,128...) custom-call(f32[8,8,272]{2,1,0:T(8,128)S(1)} %all-to-all-done.sums_ref, bf16[1088,256]{1,0:T(8,128)(2,1)S(1)} %copy-done.1, ...), custom_call_target="tpu_custom_call" | custom-call | flops 463470592 | bytes 2801664 | tf_op jit(solution)/shard_map/pallas_call | solution.py:435
  32.1 0.0 collective-permute-done.4.far_sums
  32.2 3.0 %collective-permute-done.3.near_sums = f32[2,272]{1,0:T(2,128)S(1)} collective-permute-done((f32[2,272]{1,0:T(2,128)S(1)}, f32[2,272]{1,0:T(2,128)S(1)}, u32[]{:S(2)}, u32[]{:S(2)}) %collective-permute-start.3) | collective-permute-done | bytes 2208 | tf_op jit(solution)/shard_map/ppermute | solution.py:381
  35.1 2.8 %shard_map.141 = (bf16[2,272,256]{2,1,0:T(8,128)(2,1)S(1)}, bf16[2,272,1664]{2,1,0:T(8,128)(2,1)S(1)}, f32[128,1664]{1,0:T(8,128)S(1)}, f32[8,1664]{1,0:T(8,128)S(1)}) custom-call(s32[32,2]{1,0:T(8,128)S(1)} %copy.16.window_ref, bf16[2,272,256]{2,1,0:T(8,128)(2,1)S(1)} %collective-permute-done.1.near, bf16[2,272,256]{2,1,0:T(8,128)(2,1)S(1)} %collective-permute-done.2.far, ...), custom_call_target="tpu_custom_call" | custom-call | flops 926941184 | bytes 2994176 | tf_op jit(solution)/shard_map/pallas_call | solution.py:450
  38.0 11.7 %collective-permute-start.5 = (f32[8,1664]{1,0:T(8,128)S(1)}, f32[8,1664]{1,0:T(8,128)S(1)}, u32[]{:S(2)}, u32[]{:S(2)}) collective-permute-start(f32[8,1664]{1,0:T(8,128)S(1)} %get-tuple-element.37.own), channel_id=1, source_target_pairs={{0,8},{8,0},{16,24},{24,16},{32,40},{40,32},{48,56},{56,48},{64,72... | collective-permute-start | bytes 159752 | tf_op jit(solution)/shard_map/ppermute | solution.py:386
  49.7 0.9 collective-permute-done.5.far
  50.6 2.7 %shard_map.142 = (bf16[2,260,256]{2,1,0:T(8,128)(2,1)S(1)}, bf16[2,260,256]{2,1,0:T(8,128)(2,1)S(1)}, bf16[2,272,1664]{2,1,0:T(8,128)(2,1)S(1)}, f32[8,1664]{1,0:T(8,128)S(1)}) custom-call(s32[32,2]{1,0:T(8,128)S(1)} %copy.16.window_ref, f32[8,1664]{1,0:T(8,128)S(1)} %get-tuple-element.37.own, f32[8,1664]{1,0:T(8,128)S(1)} %collective-permute-done.5.far, ...), custom_call_target="tpu_custom_call" | custom-call | flops 926941184 | bytes 2396160 | tf_op jit(solution)/shard_map/pallas_call | solution.py:460
  53.2 0.7 collective-permute-start.7
  53.9 2.1 %collective-permute-start.8 = (bf16[2,260,256]{2,1,0:T(8,128)(2,1)S(1)}, bf16[2,260,256]{2,1,0:T(8,128)(2,1)S(1)}, u32[]{:S(2)}, u32[]{:S(2)}) collective-permute-start(bf16[2,260,256]{2,1,0:T(8,128)(2,1)S(1)} %get-tuple-element.49), channel_id=1, source_target_pairs={{16,0},{32,16},{48,32},{56,8},{64,48},{72,24},{80,64},{88,40},{96,... | collective-permute-start | bytes 798728 | tf_op jit(solution)/shard_map/ppermute | solution.py:381
  56.0 2.0 %shard_map.143 = (f32[260,256]{1,0:T(8,128)S(1)}, f32[1632,128]{1,0:T(8,128)S(1)}, bf16[1632,128]{1,0:T(8,128)(2,1)S(1)}) custom-call(f32[8,1664]{1,0:T(8,128)S(1)} %get-tuple-element.40.merged, bf16[1664,128]{1,0:T(8,128)(2,1)S(1)} %get-tuple-element.34.q_ref, bf16[128,1664]{1,0:T(8,128)(2,1)S(1)} %get-tuple-element.35.gt_ref, ...), custom_call_target="tpu_custom_call" | custom-call | flops 926941184 | bytes 1519616 | tf_op jit(solution)/shard_map/pallas_call | solution.py:469
  58.0 0.0 copy-start.2
  58.0 0.0 copy-start.4
  58.0 5.5 %collective-permute-start.6 = (bf16[1632,128]{1,0:T(8,128)(2,1)S(1)}, bf16[1632,128]{1,0:T(8,128)(2,1)S(1)}, u32[]{:S(2)}, u32[]{:S(2)}) collective-permute-start(bf16[1632,128]{1,0:T(8,128)(2,1)S(1)} %get-tuple-element.47), channel_id=1, source_target_pairs={{0,8},{8,0},{16,24},{24,16},{32,40},{40,32},{48,56},{56,48},{64,72... | collective-permute-start | bytes 1253384 | tf_op jit(solution)/shard_map/ppermute | solution.py:386
  63.5 7.4 %collective-permute-done.8.near = bf16[2,260,256]{2,1,0:T(8,128)(2,1)S(1)} collective-permute-done((bf16[2,260,256]{2,1,0:T(8,128)(2,1)S(1)}, bf16[2,260,256]{2,1,0:T(8,128)(2,1)S(1)}, u32[]{:S(2)}, u32[]{:S(2)}) %collective-permute-start.8) | collective-permute-done | bytes 266272 | tf_op jit(solution)/shard_map/ppermute | solution.py:381
  71.0 0.1 shard_map.144
  71.0 2.8 %collective-permute-start.9 = (bf16[260,256]{1,0:T(8,128)(2,1)S(1)}, bf16[260,256]{1,0:T(8,128)(2,1)S(1)}, u32[]{:S(2)}, u32[]{:S(2)}) collective-permute-start(bf16[260,256]{1,0:T(8,128)(2,1)S(1)} %get-tuple-element.51), channel_id=1, source_target_pairs={{0,8},{8,0},{16,24},{24,16},{32,40},{40,32},{48,56},{56,48},{64,72... | collective-permute-start | bytes 399368 | tf_op jit(solution)/shard_map/ppermute | solution.py:386
  73.8 1.0 %collective-permute-done.9.far_clean = bf16[260,256]{1,0:T(8,128)(2,1)S(1)} collective-permute-done((bf16[260,256]{1,0:T(8,128)(2,1)S(1)}, bf16[260,256]{1,0:T(8,128)(2,1)S(1)}, u32[]{:S(2)}, u32[]{:S(2)}) %collective-permute-start.9) | collective-permute-done | bytes 133152 | tf_op jit(solution)/shard_map/ppermute | solution.py:386
  74.8 1.1 %shard_map.145 = (bf16[260,384]{1,0:T(8,128)(2,1)}, f32[260,384]{1,0:T(8,128)S(1)}, f32[260,256]{1,0:T(8,128)S(1)}, bf16[260,128]{1,0:T(8,128)(2,1)}, bf16[260,1...) custom-call(f32[1632,128]{1,0:T(8,128)S(1)} %get-tuple-element.46.own, bf16[1632,128]{1,0:T(8,128)(2,1)S(1)} %collective-permute-done.6.far, ...), custom_call_target="tpu_custom_call" | custom-call | flops 1000000 | bytes 1023360 | tf_op jit(solution)/shard_map/pallas_call | solution.py:490
  75.9 11.5 %all_to_all.10.inner_ref = f32[8,3,260]{2,1,0:T(4,128)S(1)} all-to-all(f32[8,3,260]{2,1,0:T(4,128)S(1)} %get-tuple-element.54), channel_id=1, replica_groups=mesh['seq'=64,'head'=8] {'head'}, dimensions={0} | all-to-all | bytes 49920 | tf_op jit(solution)/shard_map/all_to_all | solution.py:368
  87.4 1.3 %shard_map.146 = (bf16[260,384]{1,0:T(8,128)(2,1)}, bf16[260,128]{1,0:T(8,128)(2,1)}, bf16[260,128]{1,0:T(8,128)(2,1)}) custom-call(f32[8,8,272]{2,1,0:T(8,128)S(1)} %all-to-all-done.sums_ref, f32[8,3,260]{2,1,0:T(4,128)S(1)} %all_to_all.10.inner_ref, bf16[260,384]{1,0:T(8,128)(2,1)S(1)} %copy-done.2, bf16[260,128]{1,0:T(8,128)(2,1)S(1)} %copy-done.3, ...), custom_call_target="tpu_custom_call" | custom-call | flops 1000000 | bytes 332800 | tf_op jit(solution)/shard_map/pallas_call | solution.py:506
  (22 shorter events, 0.1 us)
Async XLA Ops:
  0.6 13.8 %copy-start.3 = (bf16[260,128]{1,0:T(8,128)(2,1)S(1)}, bf16[260,128]{1,0:T(8,128)(2,1)}, u32[]{:S(2)}) copy-start(bf16[260,128]{1,0:T(8,128)(2,1)} %k_ref.7) | copy-start | bytes 199684
  0.6 19.3 %copy-start.7 = (f32[384]{0:T(512)S(1)}, f32[384]{0:T(512)}, u32[]{:S(2)}) copy-start(f32[384]{0:T(512)} %param.14) | copy-start | bytes 4612
  0.7 19.3 %copy-start.8 = (s32[32,2]{0,1:T(2,128)S(1)}, s32[32,2]{0,1:T(2,128)}, u32[]{:S(2)}) copy-start(s32[32,2]{0,1:T(2,128)} %param.17) | copy-start | bytes 772
  0.7 30.0 %copy-start.5 = (f32[128]{0:T(128)S(1)}, f32[128]{0:T(128)}, u32[]{:S(2)}) copy-start(f32[128]{0:T(128)} %param.15) | copy-start | bytes 1540
  0.7 30.0 %copy-start.6 = (bf16[260,128]{1,0:T(8,128)(2,1)S(1)}, bf16[260,128]{1,0:T(8,128)(2,1)}, u32[]{:S(2)}) copy-start(bf16[260,128]{1,0:T(8,128)(2,1)} %v_ref.3) | copy-start | bytes 199684
  2.8 4.0 %collective-permute-start = (bf16[1088,256]{1,0:T(8,128)(2,1)}, bf16[1088,256]{1,0:T(8,128)(2,1)S(1)}, u32[]{:S(2)}, u32[]{:S(2)}) collective-permute-start(bf16[1088,256]{1,0:T(8,128)(2,1)} %shard_map.136.own), channel_id=1, source_target_pairs={{0,8},{8,0},{16,24},{24,16},{32,40},{40,32},{48,56},{56,48},{64,72... | collective-permute-start | bytes 1671176 | tf_op jit(solution)/shard_map/ppermute | solution.py:386
  6.8 1.1 %copy-start = (bf16[1088,256]{1,0:T(8,128)(2,1)S(1)}, bf16[1088,256]{1,0:T(8,128)(2,1)}, u32[]{:S(2)}) copy-start(bf16[1088,256]{1,0:T(8,128)(2,1)} %shard_map.136.own) | copy-start | bytes 1671172
  7.9 22.8 %copy-start.1 = (bf16[1088,256]{1,0:T(8,128)(2,1)S(1)}, bf16[1088,256]{1,0:T(8,128)(2,1)}, u32[]{:S(2)}) copy-start(bf16[1088,256]{1,0:T(8,128)(2,1)} %shard_map.136.own) | copy-start | bytes 1671172
  7.9 27.2 %collective-permute-start.2 = (bf16[2,272,256]{2,1,0:T(8,128)(2,1)S(1)}, bf16[2,272,256]{2,1,0:T(8,128)(2,1)S(1)}, u32[]{:S(2)}, u32[]{:S(2)}) collective-permute-start(bf16[2,272,256]{2,1,0:T(8,128)(2,1)S(1)} %shard_map.137), channel_id=1, source_target_pairs={{8,40},{24,56},{40,72},{56,88},{72,104},{88,120},{104,136},{120,15... | collective-permute-start | bytes 835592 | tf_op jit(solution)/shard_map/ppermute | solution.py:381
  8.7 26.4 %collective-permute-start.1 = (bf16[2,272,256]{2,1,0:T(8,128)(2,1)S(1)}, bf16[2,272,256]{2,1,0:T(8,128)(2,1)S(1)}, u32[]{:S(2)}, u32[]{:S(2)}) collective-permute-start(bf16[2,272,256]{2,1,0:T(8,128)(2,1)S(1)} %shard_map.137), channel_id=1, source_target_pairs={{0,16},{8,56},{16,32},{24,72},{32,48},{40,88},{48,64},{56,104},{64... | collective-permute-start | bytes 835592 | tf_op jit(solution)/shard_map/ppermute | solution.py:381
  15.5 12.5 %all-to-all-start = ((f32[8,8,272]{2,1,0:T(8,128)}), f32[8,8,272]{2,1,0:T(8,128)S(1)}, u32[]{:S(2)}, u32[]{:S(2)}) async-start(f32[8,8,272]{2,1,0:T(8,128)} %shard_map.138), calls=%async_computation | async-start | bytes 196608 | tf_op jit(solution)/shard_map/all_to_all | solution.py:368
  28.1 4.1 %collective-permute-start.4 = (f32[2,272]{1,0:T(2,128)S(1)}, f32[2,272]{1,0:T(2,128)S(1)}, u32[]{:S(2)}, u32[]{:S(2)}) collective-permute-start(f32[2,272]{1,0:T(2,128)S(1)} %shard_map.139), channel_id=1, source_target_pairs={{8,40},{24,56},{40,72},{56,88},{72,104},{88,120},{104,136},{120,15... | collective-permute-start | bytes 6536 | tf_op jit(solution)/shard_map/ppermute | solution.py:381
  28.7 6.4 %collective-permute-start.3 = (f32[2,272]{1,0:T(2,128)S(1)}, f32[2,272]{1,0:T(2,128)S(1)}, u32[]{:S(2)}, u32[]{:S(2)}) collective-permute-start(f32[2,272]{1,0:T(2,128)S(1)} %shard_map.139), channel_id=1, source_target_pairs={{0,16},{8,56},{16,32},{24,72},{32,48},{40,88},{48,64},{56,104},{64... | collective-permute-start | bytes 6536 | tf_op jit(solution)/shard_map/ppermute | solution.py:381
  38.0 12.6 %collective-permute-start.5 = (f32[8,1664]{1,0:T(8,128)S(1)}, f32[8,1664]{1,0:T(8,128)S(1)}, u32[]{:S(2)}, u32[]{:S(2)}) collective-permute-start(f32[8,1664]{1,0:T(8,128)S(1)} %get-tuple-element.37.own), channel_id=1, source_target_pairs={{0,8},{8,0},{16,24},{24,16},{32,40},{40,32},{48,56},{56,48},{64,72... | collective-permute-start | bytes 159752 | tf_op jit(solution)/shard_map/ppermute | solution.py:386
  53.2 10.3 %collective-permute-start.7 = (bf16[2,260,256]{2,1,0:T(8,128)(2,1)S(1)}, bf16[2,260,256]{2,1,0:T(8,128)(2,1)S(1)}, u32[]{:S(2)}, u32[]{:S(2)}) collective-permute-start(bf16[2,260,256]{2,1,0:T(8,128)(2,1)S(1)} %get-tuple-element.48), channel_id=1, source_target_pairs={{40,8},{56,24},{72,40},{88,56},{104,72},{120,88},{136,104},{152,12... | collective-permute-start | bytes 798728 | tf_op jit(solution)/shard_map/ppermute | solution.py:381
  53.9 17.0 %collective-permute-start.8 = (bf16[2,260,256]{2,1,0:T(8,128)(2,1)S(1)}, bf16[2,260,256]{2,1,0:T(8,128)(2,1)S(1)}, u32[]{:S(2)}, u32[]{:S(2)}) collective-permute-start(bf16[2,260,256]{2,1,0:T(8,128)(2,1)S(1)} %get-tuple-element.49), channel_id=1, source_target_pairs={{16,0},{32,16},{48,32},{56,8},{64,48},{72,24},{80,64},{88,40},{96,... | collective-permute-start | bytes 798728 | tf_op jit(solution)/shard_map/ppermute | solution.py:381
  58.0 16.8 %copy-start.2 = (bf16[260,384]{1,0:T(8,128)(2,1)S(1)}, bf16[260,384]{1,0:T(8,128)(2,1)}, u32[]{:S(2)}) copy-start(bf16[260,384]{1,0:T(8,128)(2,1)} %q_ref.5) | copy-start | bytes 599044
  58.0 16.8 %copy-start.4 = (bf16[260,128]{1,0:T(8,128)(2,1)S(1)}, bf16[260,128]{1,0:T(8,128)(2,1)}, u32[]{:S(2)}) copy-start(bf16[260,128]{1,0:T(8,128)(2,1)} %c_ref.5) | copy-start | bytes 199684
  58.0 16.8 %collective-permute-start.6 = (bf16[1632,128]{1,0:T(8,128)(2,1)S(1)}, bf16[1632,128]{1,0:T(8,128)(2,1)S(1)}, u32[]{:S(2)}, u32[]{:S(2)}) collective-permute-start(bf16[1632,128]{1,0:T(8,128)(2,1)S(1)} %get-tuple-element.47), channel_id=1, source_target_pairs={{0,8},{8,0},{16,24},{24,16},{32,40},{40,32},{48,56},{56,48},{64,72... | collective-permute-start | bytes 1253384 | tf_op jit(solution)/shard_map/ppermute | solution.py:386
  71.0 3.8 %collective-permute-start.9 = (bf16[260,256]{1,0:T(8,128)(2,1)S(1)}, bf16[260,256]{1,0:T(8,128)(2,1)S(1)}, u32[]{:S(2)}, u32[]{:S(2)}) collective-permute-start(bf16[260,256]{1,0:T(8,128)(2,1)S(1)} %get-tuple-element.51), channel_id=1, source_target_pairs={{0,8},{8,0},{16,24},{24,16},{32,40},{40,32},{48,56},{56,48},{64,72... | collective-permute-start | bytes 399368 | tf_op jit(solution)/shard_map/ppermute | solution.py:386

commit v6 on v4

--- a/solution.py
+++ b/solution.py
@@ -94,42 +94,42 @@
 
 
 def norms_body(
-    sums_ref, q_ref, k_ref, c_ref, v_ref, cv_ref, g_ref, q_gain, k_gain,
-    noisy_ref, clean_ref, out, wide, tall,
+    sums_ref, q_ref, k_ref, c_ref, v_ref, cv_ref, g_ref, q_gain, k_gain, noisy_ref, out, wide, tall
 ):
     q_inv, k_inv, c_inv = inverses(sums_ref)
     rows = k_ref.shape[0]
     slot = up(rows, PAD)
+    tall[0:rows, :LANES] = c_ref[...].astype(F32) * c_inv * k_gain[...]
+    tall[0:rows, LANES:] = cv_ref[...].astype(F32)
+    for h in range(GROUP):
+        cols = slice(h * HEAD_SIZE, (h + 1) * HEAD_SIZE)
+        gain = q_gain[:, cols] * (SCORE_SCALE * LOG2E)
+        at = (1 + h) * slot
+        tall[at : at + rows, :LANES] = q_ref[:, cols].astype(F32) * q_inv * gain
+        tall[at : at + rows, LANES:] = g_ref[:, cols].astype(F32)
+    for h in range(1 + GROUP):
+        tall[h * slot + rows : (h + 1) * slot] = jnp.zeros((slot - rows, 2 * LANES), F32)
+    out[...] = tall[...].astype(BF16)
     wide[rows:] = jnp.zeros((slot - rows, 2 * LANES), F32)
-    wide[0:rows, 0:LANES] = c_ref[...].astype(F32) * c_inv * k_gain[...]
-    wide[0:rows, LANES:] = cv_ref[...].astype(F32)
-    clean_ref[...] = wide[...].astype(BF16)
     wide[0:rows, 0:LANES] = k_ref[...].astype(F32) * k_inv * k_gain[...]
     wide[0:rows, LANES:] = v_ref[...].astype(F32)
     noisy_ref[...] = wide[...].astype(BF16)
-    for h in range(2 * GROUP):
-        tall[h * slot + rows : (h + 1) * slot] = jnp.zeros((slot - rows, LANES), F32)
-    for h in range(GROUP):
-        cols = slice(h * HEAD_SIZE, (h + 1) * HEAD_SIZE)
-        gain = q_gain[:, cols] * (SCORE_SCALE * LOG2E)
-        tall[h * slot : h * slot + rows, :] = q_ref[:, cols].astype(F32) * q_inv * gain
-        at = (GROUP + h) * slot
-        tall[at : at + rows, :] = g_ref[:, cols].astype(F32)
-    out[...] = tall[...].astype(BF16)
-
-
-def both(out, own, far, first, span):
+
+
+def both(out, own, far):
     core = lax.axis_index("seq") % 2
+    span = own.shape[0] // (1 + GROUP) * GROUP
+    first = own.shape[0] - span
 
     @pl.when(core == 0)
     def _():
-        out[0:span] = own[first : first + span]
-        out[span : 2 * span] = far[first : first + span]
+        out[0:span] = own[first:]
+        out[span : 2 * span] = far[first:]
 
     @pl.when(core == 1)
     def _():
-        out[0:span] = far[first : first + span]
-        out[span : 2 * span] = own[first : first + span]
+        out[0:span] = far[first:]
+        out[span : 2 * span] = own[first:]
 
     out[2 * span :] = jnp.zeros((out.shape[0] - 2 * span, out.shape[1]), out.dtype)
 
@@ -154,11 +154,10 @@
     return s[:whole], jnp.where(real, tail, HIDDEN)
 
 
-def noisy_body(own, far, keys, q_out, gt_out, e_out, sum_out, stats, g_rows):
-    span = own.shape[0] // 2
-    both(q_out, own, far, 0, span)
-    both(g_rows, own, far, span, span)
-    gt = g_rows[...].astype(F32).T
+def noisy_body(own, far, keys, q_out, gt_out, e_out, sum_out, stats, rows_ref):
+    both(rows_ref, own, far)
+    q_out[...] = rows_ref[:, :LANES]
+    gt = rows_ref[:, LANES:].astype(F32).T
     gt_out[...] = gt.astype(BF16)
     body, tail = scores(keys, q_out[...], TOKENS)
     whole = body.shape[0]
@@ -179,8 +178,9 @@
 
 
 def pair_body(own, far, out):
-    out[0] = own[...]
-    out[1] = far[...]
+    slot = out.shape[1]
+    out[0] = own[0:slot]
+    out[1] = far[0:slot]
 
 
 def clean_body(
@@ -300,16 +300,9 @@
     far_out[...] = (near[1].astype(F32) + far[1].astype(F32)).astype(BF16)
 
 
-def inner_body(
-    own, far, own_clean, far_clean, grads, q_ref, k_ref, c_ref, q_gain, k_gain,
-    attn_out, dq_out, clean_out, grad_v, grad_cv, out_ref,
-):
-    clean = own_clean[...] + far_clean[...].astype(F32)
-    clean_out[...] = clean
-    grad_cv[...] = clean[:, LANES:].astype(BF16)
+def settle_body(own, far, grads, q_ref, k_ref, q_gain, k_gain, attn_out, dq_out, grad_v, sums):
     grad_v[...] = grads[:, LANES:].astype(BF16)
-    part = to_lanes(clean[:, :LANES] * k_gain[...] * c_ref[...].astype(F32), 2)
-    part = part + to_lanes(grads[:, :LANES] * k_gain[...] * k_ref[...].astype(F32), 1)
+    part = to_lanes(grads[:, :LANES] * k_gain[...] * k_ref[...].astype(F32), 1)
     span = own.shape[0] // 2
     slot = span // GROUP
     rows = attn_out.shape[0]
@@ -319,7 +312,14 @@
         attn_out[:, cols] = total[h * slot : h * slot + rows].astype(BF16)
         at = span + h * slot
         dq_out[:, cols] = total[at : at + rows]
-    part = part + to_lanes(dq_out[...] * q_gain[...] * q_ref[...].astype(F32), 0)
+    sums[...] = part + to_lanes(dq_out[...] * q_gain[...] * q_ref[...].astype(F32), 0)
+
+
+def inner_body(own_clean, far_clean, c_ref, k_gain, sums, clean_out, grad_cv, out_ref):
+    clean = own_clean[...] + far_clean[...].astype(F32)
+    clean_out[...] = clean
+    grad_cv[...] = clean[:, LANES:].astype(BF16)
+    part = sums[...] + to_lanes(clean[:, :LANES] * k_gain[...] * c_ref[...].astype(F32), 2)
     for peer in range(out_ref.shape[0]):
         out_ref[peer] = part[:3]
 
@@ -395,18 +395,19 @@
     )(*fetched)
     sums = head_exchange(sums)
     pack = shape((slot, 2 * LANES), BF16)
-    noisy_kv, clean_kv, own = kernel_call(
+    packed = ((1 + GROUP) * slot, 2 * LANES)
+    noisy_kv, own = kernel_call(
         norms_body,
-        (pack, pack, shape((2 * span, LANES), BF16)),
+        (pack, shape(packed, BF16)),
         10**6,
-        [pltpu.VMEM((slot, 2 * LANES), F32), pltpu.VMEM((2 * span, LANES), F32)],
+        [pltpu.VMEM((slot, 2 * LANES), F32), pltpu.VMEM(packed, F32)],
         nargs=9,
     )(sums, noisy_q, noisy_k, clean_k, noisy_value, clean_value, out_grad, q_gain, k_gain)
+    far = core_swap(own)
     pair_kv = shape((2, slot, 2 * LANES), BF16)
-    clean_kv = kernel_call(pair_body, pair_kv, 10**6, nargs=2)(clean_kv, core_swap(clean_kv))
+    clean_kv = kernel_call(pair_body, pair_kv, 10**6, nargs=2)(own, far)
     near_kv = stretch_shift(clean_kv, 1, False)
     far_kv = stretch_shift(clean_kv, 1, True)
-    far = core_swap(own)
     q_all, g_turned, noisy_e, noisy_sum, noisy_stats = kernel_call(
         noisy_body,
         (
@@ -417,7 +418,7 @@
             stats,
         ),
         4 * product,
-        [pltpu.VMEM((queries, LANES), BF16)],
+        [pltpu.VMEM((queries, 2 * LANES), BF16)],
         nargs=3,
     )(own, far, noisy_kv)
     pair = shape((2, slot, queries), BF16)
@@ -461,21 +462,18 @@
         nargs=2,
     )(far_back, near_back)
     far_clean = core_swap(far_clean)
-    attn_out, dq, clean_grads, grad_v, grad_cv, inner = kernel_call(
+    attn_out, dq, grad_v, inner = kernel_call(
+        settle_body,
+        (query_grad, shape((rows, GROUP * LANES), F32), key_grad, shape((8, rows), F32)),
+        10**6,
+        nargs=7,
+    )(own, far, noisy_grads, noisy_q, noisy_k, q_gain, k_gain)
+    clean_grads, grad_cv, inner = kernel_call(
         inner_body,
-        (
-            query_grad,
-            shape((rows, GROUP * LANES), F32),
-            shape((rows, 2 * LANES), F32),
-            key_grad,
-            key_grad,
-            shape((peers, 3, rows), F32),
-        ),
+        (shape((rows, 2 * LANES), F32), key_grad, shape((peers, 3, rows), F32)),
         10**6,
-        nargs=10,
-    )(
-        own, far, own_clean, far_clean, noisy_grads, noisy_q, noisy_k, clean_k, q_gain, k_gain
-    )
+        nargs=5,
+    )(own_clean, far_clean, clean_k, k_gain, inner)
     inner = head_exchange(inner)
     grad_q, grad_k, grad_ck = kernel_call(
         finish_body, (query_grad, key_grad, key_grad), 10**6, nargs=10

time: 85.5 us -> 84 us (0.982)
  starting transfers between devices: 29.9 us -> 26.9 us
    ppermute x5 -> x4, starting transfers between devices: 15.9 us -> 13.3 us  [core_swap(): return lax.ppermute(value, 'seq', [(i, i ^ 1) for i in range(count)])]
    pallas_call x3 -> x4, Pallas kernels: 1.55 us -> 2.16 us  [the longest x1 1.02 us: on_device(): kernel_call(settle_body, (query_grad, shape((rows, GROUP * LANES), F32),...]
    ppermute x5 -> x4, waiting for transfers between devices: 2.81 us -> 2.96 us  [core_swap(): return lax.ppermute(value, 'seq', [(i, i ^ 1) for i in range(count)])]
  transfers between devices with their start and end apart: 10 -> 9, of which waited for: 6 -> 5; matrix products, arithmetic and copies ran while one was open for 0% -> 0% of each run, Pallas kernels for 4% -> 5%
where the time goes in v6:
time: 84 us; the launch traced here: 83.6 us
  waiting for transfers between devices  31.7 us (38%)
  starting transfers between devices  26.9 us (32%)
  Pallas kernels  13.8 us (16%)
  blocking collectives  10.1 us (12%)
  between operations  0.88 us (1%)
    ppermute x4, waiting for transfers between devices, stretch_shift(): return lax.ppermute(value, 'seq', pairs)  22.4 us
    ppermute x4, starting transfers between devices, core_swap(): return lax.ppermute(value, 'seq', [(i, i ^ 1) for i in range(count)])  13.3 us
    all_to_all x1, blocking collectives, head_exchange(): return lax.all_to_all(value, 'head', 0, 0)  10.1 us
    ppermute x4, starting transfers between devices, stretch_shift(): return lax.ppermute(value, 'seq', pairs)  8.16 us
    all_to_all x1, waiting for transfers between devices, head_exchange(): return lax.all_to_all(value, 'head', 0, 0)  6.29 us
    all_to_all x1, starting transfers between devices, head_exchange(): return lax.all_to_all(value, 'head', 0, 0)  5.44 us
    ppermute x4, waiting for transfers between devices, core_swap(): return lax.ppermute(value, 'seq', [(i, i ^ 1) for i in range(count)])  2.96 us
    pallas_call x1, Pallas kernels, on_device(): kernel_call(clean_grad_body, (pair_grad, pair_grad, pair, stats), 8 * pro...  2.71 us
  transfers between devices with their start and end apart: 9, of which 5 were waited for; matrix products, arithmetic and copies ran while one was open for 0% of the time, Pallas kernels for 5%

profile of v6, /device:TPU:256, one launch (start us, length us, event | category | flops | bytes accessed | tf_op | source)
XLA Modules:
  0.0 83.6 jit_solution(2290969862078334354)
XLA Ops:
  0.6 0.0 copy-start.2
  0.6 0.0 copy-start.1
  0.7 2.1 %shard_map.136 = f32[8,3,260]{2,1,0:T(4,128)} custom-call(bf16[260,384]{1,0:T(8,128)(2,1)} %q_ref.7, bf16[260,128]{1,0:T(8,128)(2,1)} %k_ref.7, bf16[260,128]{1,0:T(8,128)(2,1)} %c_ref.7), custom_call_target="tpu_custom_call" | custom-call | flops 10000000000 | bytes 1000000 | tf_op jit(solution)/shard_map/pallas_call | solution.py:387
  2.8 5.4 %all-to-all-start = ((f32[8,3,260]{2,1,0:T(4,128)}), f32[8,3,260]{2,1,0:T(4,128)S(1)}, u32[]{:S(2)}, u32[]{:S(2)}) async-start(f32[8,3,260]{2,1,0:T(4,128)} %shard_map.136), calls=%async_computation | async-start | bytes 98304 | tf_op jit(solution)/shard_map/all_to_all | solution.py:351
  8.3 6.3 %all-to-all-done.sums_ref = f32[8,3,260]{2,1,0:T(4,128)S(1)} async-done(((f32[8,3,260]{2,1,0:T(4,128)}), f32[8,3,260]{2,1,0:T(4,128)S(1)}, u32[]{:S(2)}, u32[]{:S(2)}) %all-to-all-start) | async-done | bytes 24992 | tf_op jit(solution)/shard_map/all_to_all | solution.py:351
  14.6 0.4 shard_map.137
  15.0 1.9 %collective-permute-start = (bf16[1088,256]{1,0:T(8,128)(2,1)S(1)}, bf16[1088,256]{1,0:T(8,128)(2,1)S(1)}, u32[]{:S(2)}, u32[]{:S(2)}) collective-permute-start(bf16[1088,256]{1,0:T(8,128)(2,1)S(1)} %get-tuple-element.36.own), channel_id=1, source_target_pairs={{0,8},{8,0},{16,24},{24,16},{32,40},{40,32},{48,56},{56,48},{64,72... | collective-permute-start | bytes 1671176 | tf_op jit(solution)/shard_map/ppermute | solution.py:369
  17.0 1.9 %collective-permute-done.far = bf16[1088,256]{1,0:T(8,128)(2,1)S(1)} collective-permute-done((bf16[1088,256]{1,0:T(8,128)(2,1)S(1)}, bf16[1088,256]{1,0:T(8,128)(2,1)S(1)}, u32[]{:S(2)}, u32[]{:S(2)}) %collective-permute-start) | collective-permute-done | bytes 557088 | tf_op jit(solution)/shard_map/ppermute | solution.py:369
  18.9 0.7 collective-permute-start.2
  19.6 4.5 %collective-permute-start.1 = (bf16[2,272,256]{2,1,0:T(8,128)(2,1)S(1)}, bf16[2,272,256]{2,1,0:T(8,128)(2,1)S(1)}, u32[]{:S(2)}, u32[]{:S(2)}) collective-permute-start(bf16[2,272,256]{2,1,0:T(8,128)(2,1)S(1)} %shard_map.138), channel_id=1, source_target_pairs={{0,16},{8,56},{16,32},{24,72},{32,48},{40,88},{48,64},{56,104},{64... | collective-permute-start | bytes 835592 | tf_op jit(solution)/shard_map/ppermute | solution.py:364
  24.1 0.1 copy.16.window_ref
  24.2 1.0 %shard_map.139 = (bf16[1664,128]{1,0:T(8,128)(2,1)S(1)}, bf16[128,1664]{1,0:T(8,128)(2,1)S(1)}, bf16[272,1664]{1,0:T(8,128)(2,1)S(1)}, f32[128,1664]{1,0:T(8,128)S(1)}, f32[8,1664]{1,0:T(8,128)S(1)}) custom-call(bf16[1088,256]{1,0:T(8,128)(2,1)S(1)} %get-tuple-element.36.own, bf16[1088,256]{1,0:T(8,128)(2,1)S(1)} %collective-permute-done.far, ...), custom_call_target="tpu_custom_call" | custom-call | flops 463470592 | bytes 2662400 | tf_op jit(solution)/shard_map/pallas_call | solution.py:411
  25.2 0.0 collective-permute-done.2.far
  25.2 15.7 %collective-permute-done.1.near = bf16[2,272,256]{2,1,0:T(8,128)(2,1)S(1)} collective-permute-done((bf16[2,272,256]{2,1,0:T(8,128)(2,1)S(1)}, bf16[2,272,256]{2,1,0:T(8,128)(2,1)S(1)}, u32[]{:S(2)}, u32[]{:S(2)}) %collective-permute-start.1) | collective-permute-done | bytes 278560 | tf_op jit(solution)/shard_map/ppermute | solution.py:364
  40.9 2.5 %shard_map.140 = (bf16[2,272,256]{2,1,0:T(8,128)(2,1)S(1)}, bf16[2,272,1664]{2,1,0:T(8,128)(2,1)S(1)}, f32[128,1664]{1,0:T(8,128)S(1)}, f32[8,1664]{1,0:T(8,128)S(1)}) custom-call(s32[32,2]{1,0:T(8,128)S(1)} %copy.16.window_ref, bf16[2,272,256]{2,1,0:T(8,128)(2,1)S(1)} %collective-permute-done.1.near, bf16[2,272,256]{2,1,0:T(8,128)(2,1)S(1)} %collective-permute-done.2.far, ...), custom_call_target="tpu_custom_call" | custom-call | flops 926941184 | bytes 2994176 | tf_op jit(solution)/shard_map/pallas_call | solution.py:425
  43.4 2.1 %collective-permute-start.3 = (f32[8,1664]{1,0:T(8,128)S(1)}, f32[8,1664]{1,0:T(8,128)S(1)}, u32[]{:S(2)}, u32[]{:S(2)}) collective-permute-start(f32[8,1664]{1,0:T(8,128)S(1)} %get-tuple-element.41.own), channel_id=1, source_target_pairs={{0,8},{8,0},{16,24},{24,16},{32,40},{40,32},{48,56},{56,48},{64,72... | collective-permute-start | bytes 159752 | tf_op jit(solution)/shard_map/ppermute | solution.py:369
  45.5 1.0 %collective-permute-done.3.far = f32[8,1664]{1,0:T(8,128)S(1)} collective-permute-done((f32[8,1664]{1,0:T(8,128)S(1)}, f32[8,1664]{1,0:T(8,128)S(1)}, u32[]{:S(2)}, u32[]{:S(2)}) %collective-permute-start.3) | collective-permute-done | bytes 53280 | tf_op jit(solution)/shard_map/ppermute | solution.py:369
  46.6 2.7 %shard_map.141 = (bf16[2,260,256]{2,1,0:T(8,128)(2,1)S(1)}, bf16[2,260,256]{2,1,0:T(8,128)(2,1)S(1)}, bf16[2,272,1664]{2,1,0:T(8,128)(2,1)S(1)}, f32[8,1664]{1,0:T(8,128)S(1)}) custom-call(s32[32,2]{1,0:T(8,128)S(1)} %copy.16.window_ref, f32[8,1664]{1,0:T(8,128)S(1)} %get-tuple-element.41.own, f32[8,1664]{1,0:T(8,128)S(1)} %collective-permute-done.3.far, ...), custom_call_target="tpu_custom_call" | custom-call | flops 926941184 | bytes 2396160 | tf_op jit(solution)/shard_map/pallas_call | solution.py:435
  49.3 0.7 collective-permute-start.5
  50.0 2.3 %collective-permute-start.6 = (bf16[2,260,256]{2,1,0:T(8,128)(2,1)S(1)}, bf16[2,260,256]{2,1,0:T(8,128)(2,1)S(1)}, u32[]{:S(2)}, u32[]{:S(2)}) collective-permute-start(bf16[2,260,256]{2,1,0:T(8,128)(2,1)S(1)} %get-tuple-element.54), channel_id=1, source_target_pairs={{16,0},{32,16},{48,32},{56,8},{64,48},{72,24},{80,64},{88,40},{96,... | collective-permute-start | bytes 798728 | tf_op jit(solution)/shard_map/ppermute | solution.py:364
  52.3 2.0 %shard_map.142 = (f32[260,256]{1,0:T(8,128)S(1)}, f32[1632,128]{1,0:T(8,128)S(1)}, bf16[1632,128]{1,0:T(8,128)(2,1)S(1)}) custom-call(f32[8,1664]{1,0:T(8,128)S(1)} %get-tuple-element.44.merged, bf16[1664,128]{1,0:T(8,128)(2,1)S(1)} %get-tuple-element.38.q_ref, bf16[128,1664]{1,0:T(8,128)(2,1)S(1)} %get-tuple-element.39.gt_ref, ...), custom_call_target="tpu_custom_call" | custom-call | flops 926941184 | bytes 1519616 | tf_op jit(solution)/shard_map/pallas_call | solution.py:444
  54.3 4.2 %collective-permute-start.4 = (bf16[1632,128]{1,0:T(8,128)(2,1)S(1)}, bf16[1632,128]{1,0:T(8,128)(2,1)S(1)}, u32[]{:S(2)}, u32[]{:S(2)}) collective-permute-start(bf16[1632,128]{1,0:T(8,128)(2,1)S(1)} %get-tuple-element.50), channel_id=1, source_target_pairs={{0,8},{8,0},{16,24},{24,16},{32,40},{40,32},{48,56},{56,48},{64,72... | collective-permute-start | bytes 1253384 | tf_op jit(solution)/shard_map/ppermute | solution.py:369
  58.5 0.0 collective-permute-done.5.far
  58.5 6.8 %collective-permute-done.6.near = bf16[2,260,256]{2,1,0:T(8,128)(2,1)S(1)} collective-permute-done((bf16[2,260,256]{2,1,0:T(8,128)(2,1)S(1)}, bf16[2,260,256]{2,1,0:T(8,128)(2,1)S(1)}, u32[]{:S(2)}, u32[]{:S(2)}) %collective-permute-start.6) | collective-permute-done | bytes 266272 | tf_op jit(solution)/shard_map/ppermute | solution.py:364
  65.3 0.1 shard_map.144
  65.4 5.1 %collective-permute-start.7 = (bf16[260,256]{1,0:T(8,128)(2,1)S(1)}, bf16[260,256]{1,0:T(8,128)(2,1)S(1)}, u32[]{:S(2)}, u32[]{:S(2)}) collective-permute-start(bf16[260,256]{1,0:T(8,128)(2,1)S(1)} %get-tuple-element.56), channel_id=1, source_target_pairs={{0,8},{8,0},{16,24},{24,16},{32,40},{40,32},{48,56},{56,48},{64,72... | collective-permute-start | bytes 399368 | tf_op jit(solution)/shard_map/ppermute | solution.py:369
  70.5 0.0 collective-permute-done.4.far
  70.5 1.0 %shard_map.143 = (bf16[260,384]{1,0:T(8,128)(2,1)}, f32[260,384]{1,0:T(8,128)S(1)}, bf16[260,128]{1,0:T(8,128)(2,1)}, f32[8,260]{1,0:T(8,128)S(1)}) custom-call(f32[1632,128]{1,0:T(8,128)S(1)} %get-tuple-element.49.own, bf16[1632,128]{1,0:T(8,128)(2,1)S(1)} %collective-permute-done.4.far, f32[260,256]{1,0:T(8,128)S(1)} %get-tuple-element.51.grads.noisy_ref, ...), custom_call_target="tpu_custom_call" | custom-call | flops 1000000 | bytes 673920 | tf_op jit(solution)/shard_map/pallas_call | solution.py:465
  71.5 0.0 collective-permute-done.7.far_clean
  71.5 0.7 shard_map.145
  72.2 10.1 %all_to_all.10.inner_ref = f32[8,3,260]{2,1,0:T(4,128)S(1)} all-to-all(f32[8,3,260]{2,1,0:T(4,128)S(1)} %get-tuple-element.58), channel_id=1, replica_groups=mesh['seq'=64,'head'=8] {'head'}, dimensions={0} | all-to-all | bytes 49920 | tf_op jit(solution)/shard_map/all_to_all | solution.py:351
  82.3 1.3 %shard_map.146 = (bf16[260,384]{1,0:T(8,128)(2,1)}, bf16[260,128]{1,0:T(8,128)(2,1)}, bf16[260,128]{1,0:T(8,128)(2,1)}) custom-call(f32[8,3,260]{2,1,0:T(4,128)S(1)} %all-to-all-done.sums_ref, f32[8,3,260]{2,1,0:T(4,128)S(1)} %all_to_all.10.inner_ref, bf16[260,384]{1,0:T(8,128)(2,1)S(1)} %copy-done, bf16[260,128]{1,0:T(8,128)(2,1)S(1)} %copy-done.1, ...), custom_call_target="tpu_custom_call" | custom-call | flops 1000000 | bytes 332800 | tf_op jit(solution)/shard_map/pallas_call | solution.py:478
  (18 shorter events, 0.1 us)
Async XLA Ops:
  0.6 13.9 %copy-start.2 = (bf16[260,128]{1,0:T(8,128)(2,1)S(1)}, bf16[260,128]{1,0:T(8,128)(2,1)}, u32[]{:S(2)}) copy-start(bf16[260,128]{1,0:T(8,128)(2,1)} %c_ref.7) | copy-start | bytes 199684
  0.6 13.9 %copy-start.1 = (bf16[260,128]{1,0:T(8,128)(2,1)S(1)}, bf16[260,128]{1,0:T(8,128)(2,1)}, u32[]{:S(2)}) copy-start(bf16[260,128]{1,0:T(8,128)(2,1)} %k_ref.7) | copy-start | bytes 199684
  0.7 13.9 %copy-start = (bf16[260,384]{1,0:T(8,128)(2,1)S(1)}, bf16[260,384]{1,0:T(8,128)(2,1)}, u32[]{:S(2)}) copy-start(bf16[260,384]{1,0:T(8,128)(2,1)} %q_ref.7) | copy-start | bytes 599044
  0.7 7.6 %copy-start.7 = (f32[384]{0:T(512)S(1)}, f32[384]{0:T(512)}, u32[]{:S(2)}) copy-start(f32[384]{0:T(512)} %param.14) | copy-start | bytes 4612
  0.7 13.9 %copy-start.3 = (bf16[260,384]{1,0:T(8,128)(2,1)S(1)}, bf16[260,384]{1,0:T(8,128)(2,1)}, u32[]{:S(2)}) copy-start(bf16[260,384]{1,0:T(8,128)(2,1)} %g_ref.1) | copy-start | bytes 599044
  0.7 13.9 %copy-start.6 = (f32[128]{0:T(128)S(1)}, f32[128]{0:T(128)}, u32[]{:S(2)}) copy-start(f32[128]{0:T(128)} %param.15) | copy-start | bytes 1540
  0.7 13.9 %copy-start.5 = (bf16[260,128]{1,0:T(8,128)(2,1)S(1)}, bf16[260,128]{1,0:T(8,128)(2,1)}, u32[]{:S(2)}) copy-start(bf16[260,128]{1,0:T(8,128)(2,1)} %cv_ref.1) | copy-start | bytes 199684
  0.7 13.9 %copy-start.4 = (bf16[260,128]{1,0:T(8,128)(2,1)S(1)}, bf16[260,128]{1,0:T(8,128)(2,1)}, u32[]{:S(2)}) copy-start(bf16[260,128]{1,0:T(8,128)(2,1)} %v_ref.1) | copy-start | bytes 199684
  2.8 21.3 %copy-start.8 = (s32[32,2]{0,1:T(2,128)S(1)}, s32[32,2]{0,1:T(2,128)}, u32[]{:S(2)}) copy-start(s32[32,2]{0,1:T(2,128)} %param.17) | copy-start | bytes 772
  2.8 11.7 %all-to-all-start = ((f32[8,3,260]{2,1,0:T(4,128)}), f32[8,3,260]{2,1,0:T(4,128)S(1)}, u32[]{:S(2)}, u32[]{:S(2)}) async-start(f32[8,3,260]{2,1,0:T(4,128)} %shard_map.136), calls=%async_computation | async-start | bytes 98304 | tf_op jit(solution)/shard_map/all_to_all | solution.py:351
  15.0 3.9 %collective-permute-start = (bf16[1088,256]{1,0:T(8,128)(2,1)S(1)}, bf16[1088,256]{1,0:T(8,128)(2,1)S(1)}, u32[]{:S(2)}, u32[]{:S(2)}) collective-permute-start(bf16[1088,256]{1,0:T(8,128)(2,1)S(1)} %get-tuple-element.36.own), channel_id=1, source_target_pairs={{0,8},{8,0},{16,24},{24,16},{32,40},{40,32},{48,56},{56,48},{64,72... | collective-permute-start | bytes 1671176 | tf_op jit(solution)/shard_map/ppermute | solution.py:369
  18.9 6.3 %collective-permute-start.2 = (bf16[2,272,256]{2,1,0:T(8,128)(2,1)S(1)}, bf16[2,272,256]{2,1,0:T(8,128)(2,1)S(1)}, u32[]{:S(2)}, u32[]{:S(2)}) collective-permute-start(bf16[2,272,256]{2,1,0:T(8,128)(2,1)S(1)} %shard_map.138), channel_id=1, source_target_pairs={{8,40},{24,56},{40,72},{56,88},{72,104},{88,120},{104,136},{120,15... | collective-permute-start | bytes 835592 | tf_op jit(solution)/shard_map/ppermute | solution.py:364
  19.6 21.3 %collective-permute-start.1 = (bf16[2,272,256]{2,1,0:T(8,128)(2,1)S(1)}, bf16[2,272,256]{2,1,0:T(8,128)(2,1)S(1)}, u32[]{:S(2)}, u32[]{:S(2)}) collective-permute-start(bf16[2,272,256]{2,1,0:T(8,128)(2,1)S(1)} %shard_map.138), channel_id=1, source_target_pairs={{0,16},{8,56},{16,32},{24,72},{32,48},{40,88},{48,64},{56,104},{64... | collective-permute-start | bytes 835592 | tf_op jit(solution)/shard_map/ppermute | solution.py:364
  43.4 3.1 %collective-permute-start.3 = (f32[8,1664]{1,0:T(8,128)S(1)}, f32[8,1664]{1,0:T(8,128)S(1)}, u32[]{:S(2)}, u32[]{:S(2)}) collective-permute-start(f32[8,1664]{1,0:T(8,128)S(1)} %get-tuple-element.41.own), channel_id=1, source_target_pairs={{0,8},{8,0},{16,24},{24,16},{32,40},{40,32},{48,56},{56,48},{64,72... | collective-permute-start | bytes 159752 | tf_op jit(solution)/shard_map/ppermute | solution.py:369
  49.3 9.2 %collective-permute-start.5 = (bf16[2,260,256]{2,1,0:T(8,128)(2,1)S(1)}, bf16[2,260,256]{2,1,0:T(8,128)(2,1)S(1)}, u32[]{:S(2)}, u32[]{:S(2)}) collective-permute-start(bf16[2,260,256]{2,1,0:T(8,128)(2,1)S(1)} %get-tuple-element.53), channel_id=1, source_target_pairs={{40,8},{56,24},{72,40},{88,56},{104,72},{120,88},{136,104},{152,12... | collective-permute-start | bytes 798728 | tf_op jit(solution)/shard_map/ppermute | solution.py:364
  50.0 15.3 %collective-permute-start.6 = (bf16[2,260,256]{2,1,0:T(8,128)(2,1)S(1)}, bf16[2,260,256]{2,1,0:T(8,128)(2,1)S(1)}, u32[]{:S(2)}, u32[]{:S(2)}) collective-permute-start(bf16[2,260,256]{2,1,0:T(8,128)(2,1)S(1)} %get-tuple-element.54), channel_id=1, source_target_pairs={{16,0},{32,16},{48,32},{56,8},{64,48},{72,24},{80,64},{88,40},{96,... | collective-permute-start | bytes 798728 | tf_op jit(solution)/shard_map/ppermute | solution.py:364
  54.3 16.2 %collective-permute-start.4 = (bf16[1632,128]{1,0:T(8,128)(2,1)S(1)}, bf16[1632,128]{1,0:T(8,128)(2,1)S(1)}, u32[]{:S(2)}, u32[]{:S(2)}) collective-permute-start(bf16[1632,128]{1,0:T(8,128)(2,1)S(1)} %get-tuple-element.50), channel_id=1, source_target_pairs={{0,8},{8,0},{16,24},{24,16},{32,40},{40,32},{48,56},{56,48},{64,72... | collective-permute-start | bytes 1253384 | tf_op jit(solution)/shard_map/ppermute | solution.py:369
  65.4 6.1 %collective-permute-start.7 = (bf16[260,256]{1,0:T(8,128)(2,1)S(1)}, bf16[260,256]{1,0:T(8,128)(2,1)S(1)}, u32[]{:S(2)}, u32[]{:S(2)}) collective-permute-start(bf16[260,256]{1,0:T(8,128)(2,1)S(1)} %get-tuple-element.56), channel_id=1, source_target_pairs={{0,8},{8,0},{16,24},{24,16},{32,40},{40,32},{48,56},{56,48},{64,72... | collective-permute-start | bytes 399368 | tf_op jit(solution)/shard_map/ppermute | solution.py:369

commit v7 on v6

--- a/solution.py
+++ b/solution.py
@@ -229,16 +229,13 @@
     stats[5:6] = jnp.sum(gt_ref[...].astype(F32) * sums, axis=0, keepdims=True)
 
 
-def key_grads(key_ref, e, gt, g, delta, q):
-    dp = dot(key_ref[:, LANES:], gt, 1, 0)
-    ds = (e.astype(F32) * (dp - delta)).astype(BF16)
-    dv = dot(e, g, 1, 0)
-    dk = dot(ds, q, 1, 0) * (1.0 / LOG2E)
-    return ds, dk, dv
+def products_body(keys, gt_ref, out):
+    for j in range(2):
+        out[j] = dot(keys[j, :, LANES:], gt_ref[...], 1, 0)
 
 
 def clean_grad_body(
-    window_ref, own, far, q_ref, gt_ref, keys, e_ref, near_out, far_out, ds_out, merged
+    window_ref, own, far, q_ref, gt_ref, dp_ref, e_ref, near_out, far_out, ds_out, merged
 ):
     use1, use2, use3 = listed(window_ref)
     first = lax.axis_index("seq") % 2 == 0
@@ -255,16 +252,18 @@
     merged[0:1] = noisy
     merged[1:2] = clean
     merged[2:3] = delta * noisy
-    gt = gt_ref[...].astype(F32) * clean
-    g = gt.T.astype(BF16)
-    gt = gt.astype(BF16)
+    gt = (gt_ref[...].astype(F32) * clean).astype(BF16)
+    delta = delta * clean
     q = q_ref[...]
     rows = near_out.shape[1]
     keep_near = jnp.where(jnp.where(first, use1, use3), 1.0, 0.0)
     keep_far = jnp.where(use2, 1.0, 0.0)
     for j in range(2):
-        ds, dk, dv = key_grads(keys.at[j], e_ref[j], gt, g, delta * clean, q)
+        e = e_ref[j]
+        ds = (e.astype(F32) * (dp_ref[j] * clean - delta)).astype(BF16)
         ds_out[j] = ds
+        dk = dot(ds, q, 1, 0) * (1.0 / LOG2E)
+        dv = dot(e, gt, 1, 1)
         for out, keep in ((near_out, keep_near), (far_out, keep_far)):
             out[j, :, :LANES] = (dk[:rows] * keep).astype(BF16)
             out[j, :, LANES:] = (dv[:rows] * keep).astype(BF16)
@@ -279,9 +278,12 @@
     mine = pl.ds(pl.multiple_of(core * span, 8), span)
     theirs = pl.ds(pl.multiple_of((1 - core) * span, 8), span)
     noisy = merged[0:1]
-    gt = gt_ref[...].astype(F32) * noisy
-    g = gt.T.astype(BF16)
-    ds, dk, dv = key_grads(keys, e_ref[...], gt.astype(BF16), g, merged[2:3], q_ref[...])
+    gt = (gt_ref[...].astype(F32) * noisy).astype(BF16)
+    e = e_ref[...]
+    dp = dot(keys[:, LANES:], gt, 1, 0)
+    ds = (e.astype(F32) * (dp - merged[2:3])).astype(BF16)
+    dk = dot(ds, q_ref[...], 1, 0) * (1.0 / LOG2E)
+    dv = dot(e, gt, 1, 1)
     rows = grads.shape[0]
     grads[:, :LANES] = dk[:rows]
     grads[:, LANES:] = dv[:rows]
@@ -300,51 +302,56 @@
     far_out[...] = (near[1].astype(F32) + far[1].astype(F32)).astype(BF16)
 
 
-def settle_body(own, far, grads, q_ref, k_ref, q_gain, k_gain, attn_out, dq_out, grad_v, sums):
+def settle_body(
+    sums_ref, own, far, grads, q_ref, k_ref, c_ref, q_gain, k_gain,
+    attn_out, grad_v, sums, q_push, q_pull, k_push, k_pull, c_scale, c_pull,
+):
+    q_inv, k_inv, c_inv = inverses(sums_ref)
     grad_v[...] = grads[:, LANES:].astype(BF16)
-    part = to_lanes(grads[:, :LANES] * k_gain[...] * k_ref[...].astype(F32), 1)
     span = own.shape[0] // 2
     slot = span // GROUP
     rows = attn_out.shape[0]
     total = own[...] + far[...].astype(F32)
+    cube = q_inv * q_inv * q_inv * (1.0 / (HQ * HEAD_SIZE))
+    inner = None
     for h in range(GROUP):
         cols = slice(h * HEAD_SIZE, (h + 1) * HEAD_SIZE)
         attn_out[:, cols] = total[h * slot : h * slot + rows].astype(BF16)
         at = span + h * slot
-        dq_out[:, cols] = total[at : at + rows]
-    sums[...] = part + to_lanes(dq_out[...] * q_gain[...] * q_ref[...].astype(F32), 0)
-
-
-def inner_body(own_clean, far_clean, c_ref, k_gain, sums, clean_out, grad_cv, out_ref):
+        scaled = total[at : at + rows] * q_gain[:, cols]
+        x = q_ref[:, cols].astype(F32)
+        q_push[:, cols] = scaled * q_inv
+        q_pull[:, cols] = x * cube
+        inner = scaled * x if inner is None else inner + scaled * x
+    width = 1.0 / (KEY_VALUE_HEADS * HEAD_SIZE)
+    x = k_ref[...].astype(F32)
+    scaled = grads[:, :LANES] * k_gain[...]
+    k_push[...] = scaled * k_inv
+    k_pull[...] = x * (k_inv * k_inv * k_inv * width)
+    c_scale[...] = c_inv
+    c_pull[...] = c_ref[...].astype(F32) * (c_inv * c_inv * c_inv * width)
+    sums[...] = to_lanes(inner, 0) + to_lanes(scaled * x, 1)
+
+
+def inner_body(own_clean, far_clean, c_ref, k_gain, c_scale, sums, c_push, grad_cv, out_ref):
     clean = own_clean[...] + far_clean[...].astype(F32)
-    clean_out[...] = clean
     grad_cv[...] = clean[:, LANES:].astype(BF16)
-    part = sums[...] + to_lanes(clean[:, :LANES] * k_gain[...] * c_ref[...].astype(F32), 2)
+    scaled = clean[:, :LANES] * k_gain[...]
+    c_push[...] = scaled * c_scale[...]
+    part = sums[...] + to_lanes(scaled * c_ref[...].astype(F32), 2)
     for peer in range(out_ref.shape[0]):
         out_ref[peer] = part[:3]
 
 
 def finish_body(
-    sums_ref, inner_ref, q_ref, k_ref, c_ref, q_gain, k_gain, dq_ref, noisy_ref, clean_ref,
-    grad_q, grad_k, grad_ck,
-):
-    q_inv, k_inv, c_inv = inverses(sums_ref)
+    inner_ref, q_push, q_pull, k_push, k_pull, c_push, c_pull, grad_q, grad_k, grad_ck
+):
     q_sum, k_sum, c_sum = to_rows(added(inner_ref))
-    q_pull = q_inv * q_inv * q_inv * (q_sum / (HQ * HEAD_SIZE))
     for h in range(GROUP):
         cols = slice(h * HEAD_SIZE, (h + 1) * HEAD_SIZE)
-        grad_q[:, cols] = (
-            q_inv * (dq_ref[:, cols] * q_gain[:, cols]) - q_ref[:, cols].astype(F32) * q_pull
-        ).astype(BF16)
-    width = KEY_VALUE_HEADS * HEAD_SIZE
-    for inv, total, mean, ref, out in (
-        (k_inv, noisy_ref, k_sum, k_ref, grad_k),
-        (c_inv, clean_ref, c_sum, c_ref, grad_ck),
-    ):
-        pull = inv * inv * inv * (mean / width)
-        out[...] = (
-            inv * (total[:, :LANES] * k_gain[...]) - ref[...].astype(F32) * pull
-        ).astype(BF16)
+        grad_q[:, cols] = (q_push[:, cols] - q_pull[:, cols] * q_sum).astype(BF16)
+    grad_k[...] = (k_push[...] - k_pull[...] * k_sum).astype(BF16)
+    grad_ck[...] = (c_push[...] - c_pull[...] * c_sum).astype(BF16)
 
 
 def head_exchange(value):
@@ -431,6 +438,9 @@
         nargs=6,
     )(window, near_kv, far_kv, q_all, g_turned, noisy_stats)
     far_stats = core_swap(own_stats)
+    products = kernel_call(
+        products_body, shape((2, slot, queries), F32), 2 * product, nargs=2
+    )(keys, g_turned)
     pair_grad = shape((2, rows, 2 * LANES), BF16)
     near_back, far_back, clean_ds, merged = kernel_call(
         clean_grad_body,
@@ -438,7 +448,7 @@
         8 * product,
         smem=(0,),
         nargs=7,
-    )(window, own_stats, far_stats, q_all, g_turned, keys, clean_e)
+    )(window, own_stats, far_stats, q_all, g_turned, products, clean_e)
     far_back = stretch_shift(far_back, -1, True)
     near_back = stretch_shift(near_back, -1, False)
     noisy_grads, own, far = kernel_call(
@@ -462,22 +472,25 @@
         nargs=2,
     )(far_back, near_back)
     far_clean = core_swap(far_clean)
-    attn_out, dq, grad_v, inner = kernel_call(
+    query_wide = shape((rows, GROUP * LANES), F32)
+    key_wide = shape((rows, LANES), F32)
+    attn_out, grad_v, inner, q_push, q_pull, k_push, k_pull, c_scale, c_pull = kernel_call(
         settle_body,
-        (query_grad, shape((rows, GROUP * LANES), F32), key_grad, shape((8, rows), F32)),
+        (query_grad, key_grad, shape((8, rows), F32), query_wide, query_wide)
+        + (key_wide,) * 4,
         10**6,
-        nargs=7,
-    )(own, far, noisy_grads, noisy_q, noisy_k, q_gain, k_gain)
-    clean_grads, grad_cv, inner = kernel_call(
+        nargs=9,
+    )(sums, own, far, noisy_grads, noisy_q, noisy_k, clean_k, q_gain, k_gain)
+    c_push, grad_cv, inner = kernel_call(
         inner_body,
-        (shape((rows, 2 * LANES), F32), key_grad, shape((peers, 3, rows), F32)),
+        (key_wide, key_grad, shape((peers, 3, rows), F32)),
         10**6,
-        nargs=5,
-    )(own_clean, far_clean, clean_k, k_gain, inner)
+        nargs=6,
+    )(own_clean, far_clean, clean_k, k_gain, c_scale, inner)
     inner = head_exchange(inner)
     grad_q, grad_k, grad_ck = kernel_call(
-        finish_body, (query_grad, key_grad, key_grad), 10**6, nargs=10
-    )(sums, inner, noisy_q, noisy_k, clean_k, q_gain, k_gain, dq, noisy_grads, clean_grads)
+        finish_body, (query_grad, key_grad, key_grad), 10**6, nargs=7
+    )(inner, q_push, q_pull, k_push, k_pull, c_push, c_pull)
     return (attn_out, grad_q, grad_k, grad_v, grad_ck, grad_cv)
 
 

time: 84 us -> 83.4 us (level)
    pallas_call x3 -> x4, Pallas kernels: 2.99 us -> 3.6 us  [the longest x1 1.17 us: on_device(): kernel_call(settle_body, (query_grad, key_grad, shape((8, rows), F32), qu...]
  transfers between devices with their start and end apart: 9 -> 9, of which waited for: 5 -> 5; matrix products, arithmetic and copies ran while one was open for 0% -> 0% of each run, Pallas kernels for 5% -> 6%
where the time goes in v7:
time: 83.4 us; the launch traced here: 83 us
  waiting for transfers between devices  31.1 us (37%)
  starting transfers between devices  26.7 us (32%)
  Pallas kernels  13.9 us (17%)
  blocking collectives  10.3 us (12%)
  between operations  0.88 us (1%)
    ppermute x4, waiting for transfers between devices, stretch_shift(): return lax.ppermute(value, 'seq', pairs)  22.5 us
    ppermute x4, starting transfers between devices, core_swap(): return lax.ppermute(value, 'seq', [(i, i ^ 1) for i in range(count)])  13.1 us
    all_to_all x1, blocking collectives, head_exchange(): return lax.all_to_all(value, 'head', 0, 0)  10.3 us
    ppermute x4, starting transfers between devices, stretch_shift(): return lax.ppermute(value, 'seq', pairs)  8.16 us
    all_to_all x1, waiting for transfers between devices, head_exchange(): return lax.all_to_all(value, 'head', 0, 0)  6.29 us
    all_to_all x1, starting transfers between devices, head_exchange(): return lax.all_to_all(value, 'head', 0, 0)  5.44 us
    pallas_call x1, Pallas kernels, on_device(): kernel_call(clean_body, (pair_kv, pair, turned, stats), 8 * product, [plt...  2.54 us
    ppermute x4, waiting for transfers between devices, core_swap(): return lax.ppermute(value, 'seq', [(i, i ^ 1) for i in range(count)])  2.3 us
  transfers between devices with their start and end apart: 9, of which 5 were waited for; matrix products, arithmetic and copies ran while one was open for 0% of the time, Pallas kernels for 6%

profile of v7, /device:TPU:256, one launch (start us, length us, event | category | flops | bytes accessed | tf_op | source)
XLA Modules:
  0.0 83.0 jit_solution(2884026466336700456)
XLA Ops:
  0.6 0.0 copy-start.1
  0.7 2.1 %shard_map.136 = f32[8,3,260]{2,1,0:T(4,128)} custom-call(bf16[260,384]{1,0:T(8,128)(2,1)} %q_ref.5, bf16[260,128]{1,0:T(8,128)(2,1)} %k_ref.5, bf16[260,128]{1,0:T(8,128)(2,1)} %c_ref.7), custom_call_target="tpu_custom_call" | custom-call | flops 10000000000 | bytes 1000000 | tf_op jit(solution)/shard_map/pallas_call | solution.py:394
  2.8 5.4 %all-to-all-start = ((f32[8,3,260]{2,1,0:T(4,128)}), f32[8,3,260]{2,1,0:T(4,128)S(1)}, u32[]{:S(2)}, u32[]{:S(2)}) async-start(f32[8,3,260]{2,1,0:T(4,128)} %shard_map.136), calls=%async_computation | async-start | bytes 98304 | tf_op jit(solution)/shard_map/all_to_all | solution.py:358
  8.3 6.3 %all-to-all-done.sums_ref = f32[8,3,260]{2,1,0:T(4,128)S(1)} async-done(((f32[8,3,260]{2,1,0:T(4,128)}), f32[8,3,260]{2,1,0:T(4,128)S(1)}, u32[]{:S(2)}, u32[]{:S(2)}) %all-to-all-start) | async-done | bytes 24992 | tf_op jit(solution)/shard_map/all_to_all | solution.py:358
  14.6 0.4 shard_map.137
  15.0 1.9 %collective-permute-start = (bf16[1088,256]{1,0:T(8,128)(2,1)S(1)}, bf16[1088,256]{1,0:T(8,128)(2,1)S(1)}, u32[]{:S(2)}, u32[]{:S(2)}) collective-permute-start(bf16[1088,256]{1,0:T(8,128)(2,1)S(1)} %get-tuple-element.41.own), channel_id=1, source_target_pairs={{0,8},{8,0},{16,24},{24,16},{32,40},{40,32},{48,56},{56,48},{64,72... | collective-permute-start | bytes 1671176 | tf_op jit(solution)/shard_map/ppermute | solution.py:376
  17.0 1.9 %collective-permute-done.far = bf16[1088,256]{1,0:T(8,128)(2,1)S(1)} collective-permute-done((bf16[1088,256]{1,0:T(8,128)(2,1)S(1)}, bf16[1088,256]{1,0:T(8,128)(2,1)S(1)}, u32[]{:S(2)}, u32[]{:S(2)}) %collective-permute-start) | collective-permute-done | bytes 557088 | tf_op jit(solution)/shard_map/ppermute | solution.py:376
  18.9 0.7 collective-permute-start.2
  19.6 4.5 %collective-permute-start.1 = (bf16[2,272,256]{2,1,0:T(8,128)(2,1)S(1)}, bf16[2,272,256]{2,1,0:T(8,128)(2,1)S(1)}, u32[]{:S(2)}, u32[]{:S(2)}) collective-permute-start(bf16[2,272,256]{2,1,0:T(8,128)(2,1)S(1)} %shard_map.138), channel_id=1, source_target_pairs={{0,16},{8,56},{16,32},{24,72},{32,48},{40,88},{48,64},{56,104},{64... | collective-permute-start | bytes 835592 | tf_op jit(solution)/shard_map/ppermute | solution.py:371
  24.1 0.1 copy.16.window_ref
  24.2 1.0 %shard_map.139 = (bf16[1664,128]{1,0:T(8,128)(2,1)S(1)}, bf16[128,1664]{1,0:T(8,128)(2,1)S(1)}, bf16[272,1664]{1,0:T(8,128)(2,1)S(1)}, f32[128,1664]{1,0:T(8,128)S(1)}, f32[8,1664]{1,0:T(8,128)S(1)}) custom-call(bf16[1088,256]{1,0:T(8,128)(2,1)S(1)} %get-tuple-element.41.own, bf16[1088,256]{1,0:T(8,128)(2,1)S(1)} %collective-permute-done.far, ...), custom_call_target="tpu_custom_call" | custom-call | flops 463470592 | bytes 2662400 | tf_op jit(solution)/shard_map/pallas_call | solution.py:418
  25.2 0.0 collective-permute-done.2.far
  25.2 15.7 %collective-permute-done.1.near = bf16[2,272,256]{2,1,0:T(8,128)(2,1)S(1)} collective-permute-done((bf16[2,272,256]{2,1,0:T(8,128)(2,1)S(1)}, bf16[2,272,256]{2,1,0:T(8,128)(2,1)S(1)}, u32[]{:S(2)}, u32[]{:S(2)}) %collective-permute-start.1) | collective-permute-done | bytes 278560 | tf_op jit(solution)/shard_map/ppermute | solution.py:371
  40.9 2.5 %shard_map.140 = (bf16[2,272,256]{2,1,0:T(8,128)(2,1)S(1)}, bf16[2,272,1664]{2,1,0:T(8,128)(2,1)S(1)}, f32[128,1664]{1,0:T(8,128)S(1)}, f32[8,1664]{1,0:T(8,128)S(1)}) custom-call(s32[32,2]{1,0:T(8,128)S(1)} %copy.16.window_ref, bf16[2,272,256]{2,1,0:T(8,128)(2,1)S(1)} %collective-permute-done.1.near, bf16[2,272,256]{2,1,0:T(8,128)(2,1)S(1)} %collective-permute-done.2.far, ...), custom_call_target="tpu_custom_call" | custom-call | flops 926941184 | bytes 2994176 | tf_op jit(solution)/shard_map/pallas_call | solution.py:432
  43.4 2.1 %collective-permute-start.3 = (f32[8,1664]{1,0:T(8,128)S(1)}, f32[8,1664]{1,0:T(8,128)S(1)}, u32[]{:S(2)}, u32[]{:S(2)}) collective-permute-start(f32[8,1664]{1,0:T(8,128)S(1)} %get-tuple-element.46.own), channel_id=1, source_target_pairs={{0,8},{8,0},{16,24},{24,16},{32,40},{40,32},{48,56},{56,48},{64,72... | collective-permute-start | bytes 159752 | tf_op jit(solution)/shard_map/ppermute | solution.py:376
  45.5 0.6 shard_map.141.dp_ref
  46.2 0.4 collective-permute-done.3.far
  46.6 2.2 %shard_map.142 = (bf16[2,260,256]{2,1,0:T(8,128)(2,1)S(1)}, bf16[2,260,256]{2,1,0:T(8,128)(2,1)S(1)}, bf16[2,272,1664]{2,1,0:T(8,128)(2,1)S(1)}, f32[8,1664]{1,0:T(8,128)S(1)}) custom-call(s32[32,2]{1,0:T(8,128)S(1)} %copy.16.window_ref, f32[8,1664]{1,0:T(8,128)S(1)} %get-tuple-element.46.own, f32[8,1664]{1,0:T(8,128)S(1)} %collective-permute-done.3.far, ...), custom_call_target="tpu_custom_call" | custom-call | flops 926941184 | bytes 2396160 | tf_op jit(solution)/shard_map/pallas_call | solution.py:445
  48.7 0.7 collective-permute-start.5
  49.4 2.3 %collective-permute-start.6 = (bf16[2,260,256]{2,1,0:T(8,128)(2,1)S(1)}, bf16[2,260,256]{2,1,0:T(8,128)(2,1)S(1)}, u32[]{:S(2)}, u32[]{:S(2)}) collective-permute-start(bf16[2,260,256]{2,1,0:T(8,128)(2,1)S(1)} %get-tuple-element.59), channel_id=1, source_target_pairs={{16,0},{32,16},{48,32},{56,8},{64,48},{72,24},{80,64},{88,40},{96,... | collective-permute-start | bytes 798728 | tf_op jit(solution)/shard_map/ppermute | solution.py:371
  51.7 2.0 %shard_map.143 = (f32[260,256]{1,0:T(8,128)S(1)}, f32[1632,128]{1,0:T(8,128)S(1)}, bf16[1632,128]{1,0:T(8,128)(2,1)S(1)}) custom-call(f32[8,1664]{1,0:T(8,128)S(1)} %get-tuple-element.49.merged, bf16[1664,128]{1,0:T(8,128)(2,1)S(1)} %get-tuple-element.43.q_ref, bf16[128,1664]{1,0:T(8,128)(2,1)S(1)} %get-tuple-element.44.gt_ref, ...), custom_call_target="tpu_custom_call" | custom-call | flops 926941184 | bytes 1519616 | tf_op jit(solution)/shard_map/pallas_call | solution.py:454
  53.7 4.2 %collective-permute-start.4 = (bf16[1632,128]{1,0:T(8,128)(2,1)S(1)}, bf16[1632,128]{1,0:T(8,128)(2,1)S(1)}, u32[]{:S(2)}, u32[]{:S(2)}) collective-permute-start(bf16[1632,128]{1,0:T(8,128)(2,1)S(1)} %get-tuple-element.55), channel_id=1, source_target_pairs={{0,8},{8,0},{16,24},{24,16},{32,40},{40,32},{48,56},{56,48},{64,72... | collective-permute-start | bytes 1253384 | tf_op jit(solution)/shard_map/ppermute | solution.py:376
  57.9 0.0 collective-permute-done.5.far
  58.0 6.8 %collective-permute-done.6.near = bf16[2,260,256]{2,1,0:T(8,128)(2,1)S(1)} collective-permute-done((bf16[2,260,256]{2,1,0:T(8,128)(2,1)S(1)}, bf16[2,260,256]{2,1,0:T(8,128)(2,1)S(1)}, u32[]{:S(2)}, u32[]{:S(2)}) %collective-permute-start.6) | collective-permute-done | bytes 266272 | tf_op jit(solution)/shard_map/ppermute | solution.py:371
  64.8 0.1 shard_map.145
  64.9 4.9 %collective-permute-start.7 = (bf16[260,256]{1,0:T(8,128)(2,1)S(1)}, bf16[260,256]{1,0:T(8,128)(2,1)S(1)}, u32[]{:S(2)}, u32[]{:S(2)}) collective-permute-start(bf16[260,256]{1,0:T(8,128)(2,1)S(1)} %get-tuple-element.61), channel_id=1, source_target_pairs={{0,8},{8,0},{16,24},{24,16},{32,40},{40,32},{48,56},{56,48},{64,72... | collective-permute-start | bytes 399368 | tf_op jit(solution)/shard_map/ppermute | solution.py:376
  69.7 0.0 collective-permute-done.4.far
  69.8 1.2 %shard_map.144 = (bf16[260,384]{1,0:T(8,128)(2,1)}, bf16[260,128]{1,0:T(8,128)(2,1)}, f32[8,260]{1,0:T(8,128)S(1)}, f32[260,384]{1,0:T(8,128)S(1)}, f32[260,384]...) custom-call(f32[8,3,260]{2,1,0:T(4,128)S(1)} %all-to-all-done.sums_r, ...), custom_call_target="tpu_custom_call" | custom-call | flops 1000000 | bytes 1605760 | tf_op jit(solution)/shard_map/pallas_call | solution.py:477
  70.9 0.0 collective-permute-done.7.far_clean
  70.9 0.7 shard_map.146
  71.6 10.3 %all_to_all.10.inner_ref = f32[8,3,260]{2,1,0:T(4,128)S(1)} all-to-all(f32[8,3,260]{2,1,0:T(4,128)S(1)} %get-tuple-element.64), channel_id=1, replica_groups=mesh['seq'=64,'head'=8] {'head'}, dimensions={0} | all-to-all | bytes 49920 | tf_op jit(solution)/shard_map/all_to_all | solution.py:358
  81.9 1.1 %shard_map.147 = (bf16[260,384]{1,0:T(8,128)(2,1)}, bf16[260,128]{1,0:T(8,128)(2,1)}, bf16[260,128]{1,0:T(8,128)(2,1)}) custom-call(f32[8,3,260]{2,1,0:T(4,128)S(1)} %all_to_all.10.inner_ref, f32[260,384]{1,0:T(8,128)S(1)} %get-tuple-element.65.q_push, f32[260,384]{1,0:T(8,128)S(1)} %get-tuple-element.66.q_pull, f32[260,128]{1,0:T(8,128)S(1)} %get-tuple-element.67.k_push, ...), custom_call_target="tpu_custom_call" | custom-call | flops 1000000 | bytes 332800 | tf_op jit(solution)/shard_map/pallas_call | solution.py:491
  (19 shorter events, 0.1 us)
Async XLA Ops:
  0.6 13.9 %copy-start.1 = (bf16[260,128]{1,0:T(8,128)(2,1)S(1)}, bf16[260,128]{1,0:T(8,128)(2,1)}, u32[]{:S(2)}) copy-start(bf16[260,128]{1,0:T(8,128)(2,1)} %c_ref.7) | copy-start | bytes 199684
  0.6 13.9 %copy-start.2 = (bf16[260,128]{1,0:T(8,128)(2,1)S(1)}, bf16[260,128]{1,0:T(8,128)(2,1)}, u32[]{:S(2)}) copy-start(bf16[260,128]{1,0:T(8,128)(2,1)} %k_ref.5) | copy-start | bytes 199684
  0.7 13.9 %copy-start = (bf16[260,384]{1,0:T(8,128)(2,1)S(1)}, bf16[260,384]{1,0:T(8,128)(2,1)}, u32[]{:S(2)}) copy-start(bf16[260,384]{1,0:T(8,128)(2,1)} %q_ref.5) | copy-start | bytes 599044
  0.7 7.6 %copy-start.7 = (f32[384]{0:T(512)S(1)}, f32[384]{0:T(512)}, u32[]{:S(2)}) copy-start(f32[384]{0:T(512)} %param.14) | copy-start | bytes 4612
  0.7 13.9 %copy-start.3 = (bf16[260,384]{1,0:T(8,128)(2,1)S(1)}, bf16[260,384]{1,0:T(8,128)(2,1)}, u32[]{:S(2)}) copy-start(bf16[260,384]{1,0:T(8,128)(2,1)} %g_ref.1) | copy-start | bytes 599044
  0.7 13.9 %copy-start.6 = (f32[128]{0:T(128)S(1)}, f32[128]{0:T(128)}, u32[]{:S(2)}) copy-start(f32[128]{0:T(128)} %param.15) | copy-start | bytes 1540
  0.7 13.9 %copy-start.5 = (bf16[260,128]{1,0:T(8,128)(2,1)S(1)}, bf16[260,128]{1,0:T(8,128)(2,1)}, u32[]{:S(2)}) copy-start(bf16[260,128]{1,0:T(8,128)(2,1)} %cv_ref.1) | copy-start | bytes 199684
  0.7 13.9 %copy-start.4 = (bf16[260,128]{1,0:T(8,128)(2,1)S(1)}, bf16[260,128]{1,0:T(8,128)(2,1)}, u32[]{:S(2)}) copy-start(bf16[260,128]{1,0:T(8,128)(2,1)} %v_ref.1) | copy-start | bytes 199684
  2.8 21.3 %copy-start.8 = (s32[32,2]{0,1:T(2,128)S(1)}, s32[32,2]{0,1:T(2,128)}, u32[]{:S(2)}) copy-start(s32[32,2]{0,1:T(2,128)} %param.17) | copy-start | bytes 772
  2.8 11.7 %all-to-all-start = ((f32[8,3,260]{2,1,0:T(4,128)}), f32[8,3,260]{2,1,0:T(4,128)S(1)}, u32[]{:S(2)}, u32[]{:S(2)}) async-start(f32[8,3,260]{2,1,0:T(4,128)} %shard_map.136), calls=%async_computation | async-start | bytes 98304 | tf_op jit(solution)/shard_map/all_to_all | solution.py:358
  15.0 3.9 %collective-permute-start = (bf16[1088,256]{1,0:T(8,128)(2,1)S(1)}, bf16[1088,256]{1,0:T(8,128)(2,1)S(1)}, u32[]{:S(2)}, u32[]{:S(2)}) collective-permute-start(bf16[1088,256]{1,0:T(8,128)(2,1)S(1)} %get-tuple-element.41.own), channel_id=1, source_target_pairs={{0,8},{8,0},{16,24},{24,16},{32,40},{40,32},{48,56},{56,48},{64,72... | collective-permute-start | bytes 1671176 | tf_op jit(solution)/shard_map/ppermute | solution.py:376
  18.9 6.3 %collective-permute-start.2 = (bf16[2,272,256]{2,1,0:T(8,128)(2,1)S(1)}, bf16[2,272,256]{2,1,0:T(8,128)(2,1)S(1)}, u32[]{:S(2)}, u32[]{:S(2)}) collective-permute-start(bf16[2,272,256]{2,1,0:T(8,128)(2,1)S(1)} %shard_map.138), channel_id=1, source_target_pairs={{8,40},{24,56},{40,72},{56,88},{72,104},{88,120},{104,136},{120,15... | collective-permute-start | bytes 835592 | tf_op jit(solution)/shard_map/ppermute | solution.py:371
  19.6 21.3 %collective-permute-start.1 = (bf16[2,272,256]{2,1,0:T(8,128)(2,1)S(1)}, bf16[2,272,256]{2,1,0:T(8,128)(2,1)S(1)}, u32[]{:S(2)}, u32[]{:S(2)}) collective-permute-start(bf16[2,272,256]{2,1,0:T(8,128)(2,1)S(1)} %shard_map.138), channel_id=1, source_target_pairs={{0,16},{8,56},{16,32},{24,72},{32,48},{40,88},{48,64},{56,104},{64... | collective-permute-start | bytes 835592 | tf_op jit(solution)/shard_map/ppermute | solution.py:371
  43.4 3.1 %collective-permute-start.3 = (f32[8,1664]{1,0:T(8,128)S(1)}, f32[8,1664]{1,0:T(8,128)S(1)}, u32[]{:S(2)}, u32[]{:S(2)}) collective-permute-start(f32[8,1664]{1,0:T(8,128)S(1)} %get-tuple-element.46.own), channel_id=1, source_target_pairs={{0,8},{8,0},{16,24},{24,16},{32,40},{40,32},{48,56},{56,48},{64,72... | collective-permute-start | bytes 159752 | tf_op jit(solution)/shard_map/ppermute | solution.py:376
  48.7 9.2 %collective-permute-start.5 = (bf16[2,260,256]{2,1,0:T(8,128)(2,1)S(1)}, bf16[2,260,256]{2,1,0:T(8,128)(2,1)S(1)}, u32[]{:S(2)}, u32[]{:S(2)}) collective-permute-start(bf16[2,260,256]{2,1,0:T(8,128)(2,1)S(1)} %get-tuple-element.58), channel_id=1, source_target_pairs={{40,8},{56,24},{72,40},{88,56},{104,72},{120,88},{136,104},{152,12... | collective-permute-start | bytes 798728 | tf_op jit(solution)/shard_map/ppermute | solution.py:371
  49.4 15.4 %collective-permute-start.6 = (bf16[2,260,256]{2,1,0:T(8,128)(2,1)S(1)}, bf16[2,260,256]{2,1,0:T(8,128)(2,1)S(1)}, u32[]{:S(2)}, u32[]{:S(2)}) collective-permute-start(bf16[2,260,256]{2,1,0:T(8,128)(2,1)S(1)} %get-tuple-element.59), channel_id=1, source_target_pairs={{16,0},{32,16},{48,32},{56,8},{64,48},{72,24},{80,64},{88,40},{96,... | collective-permute-start | bytes 798728 | tf_op jit(solution)/shard_map/ppermute | solution.py:371
  53.7 16.0 %collective-permute-start.4 = (bf16[1632,128]{1,0:T(8,128)(2,1)S(1)}, bf16[1632,128]{1,0:T(8,128)(2,1)S(1)}, u32[]{:S(2)}, u32[]{:S(2)}) collective-permute-start(bf16[1632,128]{1,0:T(8,128)(2,1)S(1)} %get-tuple-element.55), channel_id=1, source_target_pairs={{0,8},{8,0},{16,24},{24,16},{32,40},{40,32},{48,56},{56,48},{64,72... | collective-permute-start | bytes 1253384 | tf_op jit(solution)/shard_map/ppermute | solution.py:376
  64.9 6.1 %collective-permute-start.7 = (bf16[260,256]{1,0:T(8,128)(2,1)S(1)}, bf16[260,256]{1,0:T(8,128)(2,1)S(1)}, u32[]{:S(2)}, u32[]{:S(2)}) collective-permute-start(bf16[260,256]{1,0:T(8,128)(2,1)S(1)} %get-tuple-element.61), channel_id=1, source_target_pairs={{0,8},{8,0},{16,24},{24,16},{32,40},{40,32},{48,56},{56,48},{64,72... | collective-permute-start | bytes 399368 | tf_op jit(solution)/shard_map/ppermute | solution.py:376

commit v8 on v7

--- a/solution.py
+++ b/solution.py
@@ -55,10 +55,12 @@
     return high, (x - high.astype(F32)).astype(BF16)
 
 
-def to_lanes(x, row):
-    pick = (lax.broadcasted_iota(jnp.int32, (8, x.shape[1]), 0) == row).astype(BF16)
-    high, low = halves(x)
-    return dot(pick, high, 1, 1) + dot(pick, low, 1, 1)
+def to_lanes(arrays, first):
+    span = 2 * LANES * len(arrays)
+    row = lax.broadcasted_iota(jnp.int32, (8, span), 0)
+    group = lax.broadcasted_iota(jnp.int32, (8, span), 1) // (2 * LANES)
+    pick = (row == group + first).astype(BF16)
+    return dot(pick, jnp.concatenate([h for x in arrays for h in halves(x)], axis=1), 1, 1)
 
 
 def to_rows(x):
@@ -84,11 +86,13 @@
 
 
 def squares_body(q_ref, k_ref, c_ref, out_ref):
-    rows = None
-    for i, ref in enumerate((q_ref, k_ref, c_ref)):
-        x = ref[...].astype(F32)
-        part = to_lanes(x * x, i)
-        rows = part if rows is None else rows + part
+    total = None
+    for h in range(GROUP):
+        x = q_ref[:, h * HEAD_SIZE : (h + 1) * HEAD_SIZE].astype(F32)
+        total = x * x if total is None else total + x * x
+    k = k_ref[...].astype(F32)
+    c = c_ref[...].astype(F32)
+    rows = to_lanes([total, k * k, c * c], 0)
     for peer in range(out_ref.shape[0]):
         out_ref[peer] = rows[:3]
 
@@ -178,25 +182,33 @@
 
 
 def pair_body(own, far, out):
-    slot = out.shape[1]
-    out[0] = own[0:slot]
-    out[1] = far[0:slot]
+    rows = out.shape[1]
+    slot = up(rows, PAD)
+    for j, ref in enumerate((own, far)):
+        out[j] = ref[0:slot].astype(F32)[:rows].astype(BF16)
 
 
 def clean_body(
-    window_ref, near, far, q_ref, gt_ref, noisy_stats, keys, e_out, sum_out, stats, s_ref
+    window_ref, near, far, q_ref, gt_ref, noisy_stats, keys, e_out, dp_out, stats, s_ref
 ):
     use1, use2, use3 = listed(window_ref)
     first = lax.axis_index("seq") % 2 == 0
     from_far = jnp.logical_not(first) & use2
 
+    def take(ref):
+        rows = ref.shape[1]
+        for j in range(2):
+            s_ref[j, 0:rows, 0 : 2 * LANES] = ref[j].astype(F32)
+            s_ref[j, rows:, 0 : 2 * LANES] = jnp.zeros_like(s_ref[j, rows:, 0 : 2 * LANES])
+            keys[j] = s_ref[j, :, 0 : 2 * LANES].astype(BF16)
+
     @pl.when(from_far)
     def _():
-        keys[...] = far[...]
+        take(far)
 
     @pl.when(jnp.logical_not(from_far))
     def _():
-        keys[...] = near[...]
+        take(near)
 
     hide = jnp.where(jnp.where(first, use1, use2 | use3), 0.0, HIDDEN)
     q = q_ref[...]
@@ -213,25 +225,20 @@
         )
         top = here if top is None else jnp.maximum(top, here)
     total = None
-    sums = None
+    delta = None
     for j in range(2):
         e = jnp.exp2(s_ref[j] - top)
+        e_out[j] = e.astype(BF16)
+        dp = dot(keys[j, :, LANES:], gt_ref[...], 1, 0)
+        dp_out[j] = dp
         part = jnp.sum(e, axis=0, keepdims=True)
-        low = e.astype(BF16)
-        e_out[j] = low
-        share = dot(keys[j, :, LANES:], low, 0, 0)
+        share = jnp.sum(e * dp, axis=0, keepdims=True)
         total = part if total is None else total + part
-        sums = share if sums is None else sums + share
-    sum_out[...] = sums
+        delta = share if delta is None else delta + share
     stats[...] = noisy_stats[...]
     stats[3:4] = top
     stats[4:5] = total
-    stats[5:6] = jnp.sum(gt_ref[...].astype(F32) * sums, axis=0, keepdims=True)
-
-
-def products_body(keys, gt_ref, out):
-    for j in range(2):
-        out[j] = dot(keys[j, :, LANES:], gt_ref[...], 1, 0)
+    stats[5:6] = delta
 
 
 def clean_grad_body(
@@ -270,7 +277,7 @@
 
 
 def noisy_grad_body(
-    merged, q_ref, gt_ref, keys, clean_keys, e_ref, ds_ref, noisy_sum, clean_sum,
+    merged, q_ref, gt_ref, keys, clean_keys, e_ref, clean_e, ds_ref, noisy_sum,
     grads, own, far, wide,
 ):
     core = lax.axis_index("seq") % 2
@@ -290,14 +297,16 @@
     dq = dot(keys[:, :LANES], ds, 0, 0)
     for j in range(2):
         dq = dq + dot(clean_keys[j, :, :LANES], ds_ref[j], 0, 0)
-    wide[0] = (noisy_sum[...] * noisy + clean_sum[...] * merged[1:2]).T
+    clean_sum = dot(clean_keys[0, :, LANES:], clean_e[0], 0, 0)
+    clean_sum = clean_sum + dot(clean_keys[1, :, LANES:], clean_e[1], 0, 0)
+    wide[0] = (noisy_sum[...] * noisy + clean_sum * merged[1:2]).T
     wide[1] = (dq * SCORE_SCALE).T
     for i in range(2):
         own[i * span : (i + 1) * span] = wide[i, mine]
         far[i * span : (i + 1) * span] = wide[i, theirs].astype(BF16)
 
 
-def join_body(far, near, own_out, far_out):
+def join_body(near, far, own_out, far_out):
     own_out[...] = near[0].astype(F32) + far[0].astype(F32)
     far_out[...] = (near[1].astype(F32) + far[1].astype(F32)).astype(BF16)
 
@@ -330,7 +339,7 @@
     k_pull[...] = x * (k_inv * k_inv * k_inv * width)
     c_scale[...] = c_inv
     c_pull[...] = c_ref[...].astype(F32) * (c_inv * c_inv * c_inv * width)
-    sums[...] = to_lanes(inner, 0) + to_lanes(scaled * x, 1)
+    sums[...] = to_lanes([inner, scaled * x], 0)
 
 
 def inner_body(own_clean, far_clean, c_ref, k_gain, c_scale, sums, c_push, grad_cv, out_ref):
@@ -338,7 +347,7 @@
     grad_cv[...] = clean[:, LANES:].astype(BF16)
     scaled = clean[:, :LANES] * k_gain[...]
     c_push[...] = scaled * c_scale[...]
-    part = sums[...] + to_lanes(scaled * c_ref[...].astype(F32), 2)
+    part = sums[...] + to_lanes([scaled * c_ref[...].astype(F32)], 2)
     for peer in range(out_ref.shape[0]):
         out_ref[peer] = part[:3]
 
@@ -412,7 +421,8 @@
     )(sums, noisy_q, noisy_k, clean_k, noisy_value, clean_value, out_grad, q_gain, k_gain)
     far = core_swap(own)
     pair_kv = shape((2, slot, 2 * LANES), BF16)
-    clean_kv = kernel_call(pair_body, pair_kv, 10**6, nargs=2)(own, far)
+    flown = shape((2, rows, 2 * LANES), BF16)
+    clean_kv = kernel_call(pair_body, flown, 10**6, nargs=2)(own, far)
     near_kv = stretch_shift(clean_kv, 1, False)
     far_kv = stretch_shift(clean_kv, 1, True)
     q_all, g_turned, noisy_e, noisy_sum, noisy_stats = kernel_call(
@@ -429,18 +439,15 @@
         nargs=3,
     )(own, far, noisy_kv)
     pair = shape((2, slot, queries), BF16)
-    keys, clean_e, clean_sum, own_stats = kernel_call(
+    keys, clean_e, products, own_stats = kernel_call(
         clean_body,
-        (pair_kv, pair, turned, stats),
+        (pair_kv, pair, shape((2, slot, queries), F32), stats),
         8 * product,
         [pltpu.VMEM((2, slot, queries), F32)],
         smem=(0,),
         nargs=6,
     )(window, near_kv, far_kv, q_all, g_turned, noisy_stats)
     far_stats = core_swap(own_stats)
-    products = kernel_call(
-        products_body, shape((2, slot, queries), F32), 2 * product, nargs=2
-    )(keys, g_turned)
     pair_grad = shape((2, rows, 2 * LANES), BF16)
     near_back, far_back, clean_ds, merged = kernel_call(
         clean_grad_body,
@@ -449,8 +456,8 @@
         smem=(0,),
         nargs=7,
     )(window, own_stats, far_stats, q_all, g_turned, products, clean_e)
+    near_back = stretch_shift(near_back, -1, False)
     far_back = stretch_shift(far_back, -1, True)
-    near_back = stretch_shift(near_back, -1, False)
     noisy_grads, own, far = kernel_call(
         noisy_grad_body,
         (
@@ -461,7 +468,7 @@
         8 * product,
         [pltpu.VMEM((2, queries, LANES), F32)],
         nargs=9,
-    )(merged, q_all, g_turned, noisy_kv, keys, noisy_e, clean_ds, noisy_sum, clean_sum)
+    )(merged, q_all, g_turned, noisy_kv, keys, noisy_e, clean_e, clean_ds, noisy_sum)
     far = core_swap(far)
     key_grad = shape((rows, LANES), BF16)
     query_grad = shape((rows, GROUP * LANES), BF16)
@@ -470,7 +477,7 @@
         (shape((rows, 2 * LANES), F32), shape((rows, 2 * LANES), BF16)),
         10**10,
         nargs=2,
-    )(far_back, near_back)
+    )(near_back, far_back)
     far_clean = core_swap(far_clean)
     query_wide = shape((rows, GROUP * LANES), F32)
     key_wide = shape((rows, LANES), F32)

time: 83.4 us -> 82.6 us (level)
  the two profiles are of different devices: /device:TPU:256 before, /device:TPU:240 now
where the time goes in v8:
time: 82.6 us; the launch traced here: 82.2 us
  starting transfers between devices  30 us (36%)
  waiting for transfers between devices  27.4 us (33%)
  Pallas kernels  13.5 us (16%)
  blocking collectives  10.2 us (12%)
  between operations  0.87 us (1%)
    ppermute x4, waiting for transfers between devices, stretch_shift(): return lax.ppermute(value, 'seq', pairs)  18.4 us
    ppermute x4, starting transfers between devices, core_swap(): return lax.ppermute(value, 'seq', [(i, i ^ 1) for i in range(count)])  15.4 us
    all_to_all x1, blocking collectives, head_exchange(): return lax.all_to_all(value, 'head', 0, 0)  10.2 us
    ppermute x4, starting transfers between devices, stretch_shift(): return lax.ppermute(value, 'seq', pairs)  10.1 us
    all_to_all x1, waiting for transfers between devices, head_exchange(): return lax.all_to_all(value, 'head', 0, 0)  6.29 us
    all_to_all x1, starting transfers between devices, head_exchange(): return lax.all_to_all(value, 'head', 0, 0)  4.55 us
    ppermute x4, waiting for transfers between devices, core_swap(): return lax.ppermute(value, 'seq', [(i, i ^ 1) for i in range(count)])  2.79 us
    pallas_call x1, Pallas kernels, on_device(): kernel_call(noisy_grad_body, (shape((rows, 2 * LANES), F32), shape((2 * s...  2.5 us
  transfers between devices with their start and end apart: 9, of which 5 were waited for; matrix products, arithmetic and copies ran while one was open for 0% of the time, Pallas kernels for 6%

profile of v8, /device:TPU:240, one launch (start us, length us, event | category | flops | bytes accessed | tf_op | source)
XLA Modules:
  0.0 82.2 jit_solution(14211161758475635157)
XLA Ops:
  0.7 2.0 %shard_map.136 = f32[8,3,260]{2,1,0:T(4,128)} custom-call(bf16[260,384]{1,0:T(8,128)(2,1)} %q_ref.5, bf16[260,128]{1,0:T(8,128)(2,1)} %k_ref.5, bf16[260,128]{1,0:T(8,128)(2,1)} %c_ref.7), custom_call_target="tpu_custom_call" | custom-call | flops 10000000000 | bytes 1000000 | tf_op jit(solution)/shard_map/pallas_call | solution.py:403
  2.7 4.5 %all-to-all-start = ((f32[8,3,260]{2,1,0:T(4,128)}), f32[8,3,260]{2,1,0:T(4,128)S(1)}, u32[]{:S(2)}, u32[]{:S(2)}) async-start(f32[8,3,260]{2,1,0:T(4,128)} %shard_map.136), calls=%async_computation | async-start | bytes 98304 | tf_op jit(solution)/shard_map/all_to_all | solution.py:367
  7.3 6.3 %all-to-all-done.sums_ref = f32[8,3,260]{2,1,0:T(4,128)S(1)} async-done(((f32[8,3,260]{2,1,0:T(4,128)}), f32[8,3,260]{2,1,0:T(4,128)S(1)}, u32[]{:S(2)}, u32[]{:S(2)}) %all-to-all-start) | async-done | bytes 24992 | tf_op jit(solution)/shard_map/all_to_all | solution.py:367
  13.6 0.0 copy-done.1
  13.6 0.0 copy-done
  13.6 0.4 shard_map.137
  14.1 1.9 %collective-permute-start = (bf16[1088,256]{1,0:T(8,128)(2,1)S(1)}, bf16[1088,256]{1,0:T(8,128)(2,1)S(1)}, u32[]{:S(2)}, u32[]{:S(2)}) collective-permute-start(bf16[1088,256]{1,0:T(8,128)(2,1)S(1)} %get-tuple-element.41.own), channel_id=1, source_target_pairs={{0,8},{8,0},{16,24},{24,16},{32,40},{40,32},{48,56},{56,48},{64,72... | collective-permute-start | bytes 1671176 | tf_op jit(solution)/shard_map/ppermute | solution.py:385
  16.0 1.9 %collective-permute-done.far = bf16[1088,256]{1,0:T(8,128)(2,1)S(1)} collective-permute-done((bf16[1088,256]{1,0:T(8,128)(2,1)S(1)}, bf16[1088,256]{1,0:T(8,128)(2,1)S(1)}, u32[]{:S(2)}, u32[]{:S(2)}) %collective-permute-start) | collective-permute-done | bytes 557088 | tf_op jit(solution)/shard_map/ppermute | solution.py:385
  17.9 0.7 collective-permute-start.2
  18.6 5.7 %collective-permute-start.1 = (bf16[2,260,256]{2,1,0:T(8,128)(2,1)S(1)}, bf16[2,260,256]{2,1,0:T(8,128)(2,1)S(1)}, u32[]{:S(2)}, u32[]{:S(2)}) collective-permute-start(bf16[2,260,256]{2,1,0:T(8,128)(2,1)S(1)} %shard_map.138), channel_id=1, source_target_pairs={{0,16},{8,56},{16,32},{24,72},{32,48},{40,88},{48,64},{56,104},{64... | collective-permute-start | bytes 798728 | tf_op jit(solution)/shard_map/ppermute | solution.py:380
  24.4 0.1 copy.16.window_ref
  24.4 1.0 %shard_map.139 = (bf16[1664,128]{1,0:T(8,128)(2,1)S(1)}, bf16[128,1664]{1,0:T(8,128)(2,1)S(1)}, bf16[272,1664]{1,0:T(8,128)(2,1)S(1)}, f32[128,1664]{1,0:T(8,128)S(1)}, f32[8,1664]{1,0:T(8,128)S(1)}) custom-call(bf16[1088,256]{1,0:T(8,128)(2,1)S(1)} %get-tuple-element.41.own, bf16[1088,256]{1,0:T(8,128)(2,1)S(1)} %collective-permute-done.far, ...), custom_call_target="tpu_custom_call" | custom-call | flops 463470592 | bytes 2662400 | tf_op jit(solution)/shard_map/pallas_call | solution.py:428
  25.5 0.0 collective-permute-done.2.far
  25.5 10.2 %collective-permute-done.1.near = bf16[2,260,256]{2,1,0:T(8,128)(2,1)S(1)} collective-permute-done((bf16[2,260,256]{2,1,0:T(8,128)(2,1)S(1)}, bf16[2,260,256]{2,1,0:T(8,128)(2,1)S(1)}, u32[]{:S(2)}, u32[]{:S(2)}) %collective-permute-start.1) | collective-permute-done | bytes 266272 | tf_op jit(solution)/shard_map/ppermute | solution.py:380
  35.7 2.3 %shard_map.140 = (bf16[2,272,256]{2,1,0:T(8,128)(2,1)S(1)}, bf16[2,272,1664]{2,1,0:T(8,128)(2,1)S(1)}, f32[2,272,1664]{2,1,0:T(8,128)S(1)}, f32[8,1664]{1,0:T(8,128)S(1)}) custom-call(s32[32,2]{1,0:T(8,128)S(1)} %copy.16.window_ref, bf16[2,260,256]{2,1,0:T(8,128)(2,1)S(1)} %collective-permute-done.1.near, ...), custom_call_target="tpu_custom_call" | custom-call | flops 926941184 | bytes 5763072 | tf_op jit(solution)/shard_map/pallas_call | solution.py:442
  38.0 4.1 %collective-permute-start.3 = (f32[8,1664]{1,0:T(8,128)S(1)}, f32[8,1664]{1,0:T(8,128)S(1)}, u32[]{:S(2)}, u32[]{:S(2)}) collective-permute-start(f32[8,1664]{1,0:T(8,128)S(1)} %get-tuple-element.46.own), channel_id=1, source_target_pairs={{0,8},{8,0},{16,24},{24,16},{32,40},{40,32},{48,56},{56,48},{64,72... | collective-permute-start | bytes 159752 | tf_op jit(solution)/shard_map/ppermute | solution.py:385
  42.1 0.9 %collective-permute-done.3.far = f32[8,1664]{1,0:T(8,128)S(1)} collective-permute-done((f32[8,1664]{1,0:T(8,128)S(1)}, f32[8,1664]{1,0:T(8,128)S(1)}, u32[]{:S(2)}, u32[]{:S(2)}) %collective-permute-start.3) | collective-permute-done | bytes 53280 | tf_op jit(solution)/shard_map/ppermute | solution.py:385
  43.0 2.2 %shard_map.141 = (bf16[2,260,256]{2,1,0:T(8,128)(2,1)S(1)}, bf16[2,260,256]{2,1,0:T(8,128)(2,1)S(1)}, bf16[2,272,1664]{2,1,0:T(8,128)(2,1)S(1)}, f32[8,1664]{1,0:T(8,128)S(1)}) custom-call(s32[32,2]{1,0:T(8,128)S(1)} %copy.16.window_ref, f32[8,1664]{1,0:T(8,128)S(1)} %get-tuple-element.46.own, f32[8,1664]{1,0:T(8,128)S(1)} %collective-permute-done.3.far, ...), custom_call_target="tpu_custom_call" | custom-call | flops 926941184 | bytes 2396160 | tf_op jit(solution)/shard_map/pallas_call | solution.py:452
  45.1 3.0 %collective-permute-start.5 = (bf16[2,260,256]{2,1,0:T(8,128)(2,1)S(1)}, bf16[2,260,256]{2,1,0:T(8,128)(2,1)S(1)}, u32[]{:S(2)}, u32[]{:S(2)}) collective-permute-start(bf16[2,260,256]{2,1,0:T(8,128)(2,1)S(1)} %get-tuple-element.58), channel_id=1, source_target_pairs={{16,0},{32,16},{48,32},{56,8},{64,48},{72,24},{80,64},{88,40},{96,... | collective-permute-start | bytes 798728 | tf_op jit(solution)/shard_map/ppermute | solution.py:380
  48.1 0.7 collective-permute-start.6
  48.8 2.5 %shard_map.142 = (f32[260,256]{1,0:T(8,128)S(1)}, f32[1632,128]{1,0:T(8,128)S(1)}, bf16[1632,128]{1,0:T(8,128)(2,1)S(1)}) custom-call(f32[8,1664]{1,0:T(8,128)S(1)} %get-tuple-element.49.merged, bf16[1664,128]{1,0:T(8,128)(2,1)S(1)} %get-tuple-element.43.q_ref, bf16[128,1664]{1,0:T(8,128)(2,1)S(1)} %get-tuple-element.44.gt_ref, ...), custom_call_target="tpu_custom_call" | custom-call | flops 926941184 | bytes 1519616 | tf_op jit(solution)/shard_map/pallas_call | solution.py:461
  51.3 5.4 %collective-permute-start.4 = (bf16[1632,128]{1,0:T(8,128)(2,1)S(1)}, bf16[1632,128]{1,0:T(8,128)(2,1)S(1)}, u32[]{:S(2)}, u32[]{:S(2)}) collective-permute-start(bf16[1632,128]{1,0:T(8,128)(2,1)S(1)} %get-tuple-element.55), channel_id=1, source_target_pairs={{0,8},{8,0},{16,24},{24,16},{32,40},{40,32},{48,56},{56,48},{64,72... | collective-permute-start | bytes 1253384 | tf_op jit(solution)/shard_map/ppermute | solution.py:385
  56.8 8.2 %collective-permute-done.5.near = bf16[2,260,256]{2,1,0:T(8,128)(2,1)S(1)} collective-permute-done((bf16[2,260,256]{2,1,0:T(8,128)(2,1)S(1)}, bf16[2,260,256]{2,1,0:T(8,128)(2,1)S(1)}, u32[]{:S(2)}, u32[]{:S(2)}) %collective-permute-start.5) | collective-permute-done | bytes 266272 | tf_op jit(solution)/shard_map/ppermute | solution.py:380
  64.9 0.0 collective-permute-done.6.far
  64.9 0.1 shard_map.144
  65.0 4.0 %collective-permute-start.7 = (bf16[260,256]{1,0:T(8,128)(2,1)S(1)}, bf16[260,256]{1,0:T(8,128)(2,1)S(1)}, u32[]{:S(2)}, u32[]{:S(2)}) collective-permute-start(bf16[260,256]{1,0:T(8,128)(2,1)S(1)} %get-tuple-element.61), channel_id=1, source_target_pairs={{0,8},{8,0},{16,24},{24,16},{32,40},{40,32},{48,56},{56,48},{64,72... | collective-permute-start | bytes 399368 | tf_op jit(solution)/shard_map/ppermute | solution.py:385
  69.0 0.0 collective-permute-done.4.far
  69.0 1.2 %shard_map.143 = (bf16[260,384]{1,0:T(8,128)(2,1)}, bf16[260,128]{1,0:T(8,128)(2,1)}, f32[8,260]{1,0:T(8,128)S(1)}, f32[260,384]{1,0:T(8,128)S(1)}, f32[260,384]...) custom-call(f32[8,3,260]{2,1,0:T(4,128)S(1)} %all-to-all-done.sums_r, ...), custom_call_target="tpu_custom_call" | custom-call | flops 1000000 | bytes 1605760 | tf_op jit(solution)/shard_map/pallas_call | solution.py:484
  70.2 0.0 collective-permute-done.7.far_clean
  70.2 0.7 shard_map.145
  70.9 10.2 %all_to_all.10.inner_ref = f32[8,3,260]{2,1,0:T(4,128)S(1)} all-to-all(f32[8,3,260]{2,1,0:T(4,128)S(1)} %get-tuple-element.64), channel_id=1, replica_groups=mesh['seq'=64,'head'=8] {'head'}, dimensions={0} | all-to-all | bytes 49920 | tf_op jit(solution)/shard_map/all_to_all | solution.py:367
  81.1 1.1 %shard_map.146 = (bf16[260,384]{1,0:T(8,128)(2,1)}, bf16[260,128]{1,0:T(8,128)(2,1)}, bf16[260,128]{1,0:T(8,128)(2,1)}) custom-call(f32[8,3,260]{2,1,0:T(4,128)S(1)} %all_to_all.10.inner_ref, f32[260,384]{1,0:T(8,128)S(1)} %get-tuple-element.65.q_push, f32[260,384]{1,0:T(8,128)S(1)} %get-tuple-element.66.q_pull, f32[260,128]{1,0:T(8,128)S(1)} %get-tuple-element.67.k_push, ...), custom_call_target="tpu_custom_call" | custom-call | flops 1000000 | bytes 332800 | tf_op jit(solution)/shard_map/pallas_call | solution.py:498
  (18 shorter events, 0.1 us)
Async XLA Ops:
  0.6 13.0 %copy-start.1 = (bf16[260,128]{1,0:T(8,128)(2,1)S(1)}, bf16[260,128]{1,0:T(8,128)(2,1)}, u32[]{:S(2)}) copy-start(bf16[260,128]{1,0:T(8,128)(2,1)} %c_ref.7) | copy-start | bytes 199684
  0.6 12.9 %copy-start.2 = (bf16[260,128]{1,0:T(8,128)(2,1)S(1)}, bf16[260,128]{1,0:T(8,128)(2,1)}, u32[]{:S(2)}) copy-start(bf16[260,128]{1,0:T(8,128)(2,1)} %k_ref.5) | copy-start | bytes 199684
  0.7 12.9 %copy-start = (bf16[260,384]{1,0:T(8,128)(2,1)S(1)}, bf16[260,384]{1,0:T(8,128)(2,1)}, u32[]{:S(2)}) copy-start(bf16[260,384]{1,0:T(8,128)(2,1)} %q_ref.5) | copy-start | bytes 599044
  0.7 6.6 %copy-start.7 = (f32[384]{0:T(512)S(1)}, f32[384]{0:T(512)}, u32[]{:S(2)}) copy-start(f32[384]{0:T(512)} %param.14) | copy-start | bytes 4612
  0.7 12.9 %copy-start.3 = (bf16[260,384]{1,0:T(8,128)(2,1)S(1)}, bf16[260,384]{1,0:T(8,128)(2,1)}, u32[]{:S(2)}) copy-start(bf16[260,384]{1,0:T(8,128)(2,1)} %g_ref.1) | copy-start | bytes 599044
  0.7 12.9 %copy-start.6 = (f32[128]{0:T(128)S(1)}, f32[128]{0:T(128)}, u32[]{:S(2)}) copy-start(f32[128]{0:T(128)} %param.15) | copy-start | bytes 1540
  0.7 12.9 %copy-start.5 = (bf16[260,128]{1,0:T(8,128)(2,1)S(1)}, bf16[260,128]{1,0:T(8,128)(2,1)}, u32[]{:S(2)}) copy-start(bf16[260,128]{1,0:T(8,128)(2,1)} %cv_ref.1) | copy-start | bytes 199684
  0.7 12.9 %copy-start.4 = (bf16[260,128]{1,0:T(8,128)(2,1)S(1)}, bf16[260,128]{1,0:T(8,128)(2,1)}, u32[]{:S(2)}) copy-start(bf16[260,128]{1,0:T(8,128)(2,1)} %v_ref.1) | copy-start | bytes 199684
  2.7 21.6 %copy-start.8 = (s32[32,2]{0,1:T(2,128)S(1)}, s32[32,2]{0,1:T(2,128)}, u32[]{:S(2)}) copy-start(s32[32,2]{0,1:T(2,128)} %param.17) | copy-start | bytes 772
  2.7 10.8 %all-to-all-start = ((f32[8,3,260]{2,1,0:T(4,128)}), f32[8,3,260]{2,1,0:T(4,128)S(1)}, u32[]{:S(2)}, u32[]{:S(2)}) async-start(f32[8,3,260]{2,1,0:T(4,128)} %shard_map.136), calls=%async_computation | async-start | bytes 98304 | tf_op jit(solution)/shard_map/all_to_all | solution.py:367
  14.1 3.9 %collective-permute-start = (bf16[1088,256]{1,0:T(8,128)(2,1)S(1)}, bf16[1088,256]{1,0:T(8,128)(2,1)S(1)}, u32[]{:S(2)}, u32[]{:S(2)}) collective-permute-start(bf16[1088,256]{1,0:T(8,128)(2,1)S(1)} %get-tuple-element.41.own), channel_id=1, source_target_pairs={{0,8},{8,0},{16,24},{24,16},{32,40},{40,32},{48,56},{56,48},{64,72... | collective-permute-start | bytes 1671176 | tf_op jit(solution)/shard_map/ppermute | solution.py:385
  17.9 7.5 %collective-permute-start.2 = (bf16[2,260,256]{2,1,0:T(8,128)(2,1)S(1)}, bf16[2,260,256]{2,1,0:T(8,128)(2,1)S(1)}, u32[]{:S(2)}, u32[]{:S(2)}) collective-permute-start(bf16[2,260,256]{2,1,0:T(8,128)(2,1)S(1)} %shard_map.138), channel_id=1, source_target_pairs={{8,40},{24,56},{40,72},{56,88},{72,104},{88,120},{104,136},{120,15... | collective-permute-start | bytes 798728 | tf_op jit(solution)/shard_map/ppermute | solution.py:380
  18.6 17.0 %collective-permute-start.1 = (bf16[2,260,256]{2,1,0:T(8,128)(2,1)S(1)}, bf16[2,260,256]{2,1,0:T(8,128)(2,1)S(1)}, u32[]{:S(2)}, u32[]{:S(2)}) collective-permute-start(bf16[2,260,256]{2,1,0:T(8,128)(2,1)S(1)} %shard_map.138), channel_id=1, source_target_pairs={{0,16},{8,56},{16,32},{24,72},{32,48},{40,88},{48,64},{56,104},{64... | collective-permute-start | bytes 798728 | tf_op jit(solution)/shard_map/ppermute | solution.py:380
  38.0 5.0 %collective-permute-start.3 = (f32[8,1664]{1,0:T(8,128)S(1)}, f32[8,1664]{1,0:T(8,128)S(1)}, u32[]{:S(2)}, u32[]{:S(2)}) collective-permute-start(f32[8,1664]{1,0:T(8,128)S(1)} %get-tuple-element.46.own), channel_id=1, source_target_pairs={{0,8},{8,0},{16,24},{24,16},{32,40},{40,32},{48,56},{56,48},{64,72... | collective-permute-start | bytes 159752 | tf_op jit(solution)/shard_map/ppermute | solution.py:385
  45.1 19.8 %collective-permute-start.5 = (bf16[2,260,256]{2,1,0:T(8,128)(2,1)S(1)}, bf16[2,260,256]{2,1,0:T(8,128)(2,1)S(1)}, u32[]{:S(2)}, u32[]{:S(2)}) collective-permute-start(bf16[2,260,256]{2,1,0:T(8,128)(2,1)S(1)} %get-tuple-element.58), channel_id=1, source_target_pairs={{16,0},{32,16},{48,32},{56,8},{64,48},{72,24},{80,64},{88,40},{96,... | collective-permute-start | bytes 798728 | tf_op jit(solution)/shard_map/ppermute | solution.py:380
  48.1 16.8 %collective-permute-start.6 = (bf16[2,260,256]{2,1,0:T(8,128)(2,1)S(1)}, bf16[2,260,256]{2,1,0:T(8,128)(2,1)S(1)}, u32[]{:S(2)}, u32[]{:S(2)}) collective-permute-start(bf16[2,260,256]{2,1,0:T(8,128)(2,1)S(1)} %get-tuple-element.59), channel_id=1, source_target_pairs={{40,8},{56,24},{72,40},{88,56},{104,72},{120,88},{136,104},{152,12... | collective-permute-start | bytes 798728 | tf_op jit(solution)/shard_map/ppermute | solution.py:380
  51.3 17.7 %collective-permute-start.4 = (bf16[1632,128]{1,0:T(8,128)(2,1)S(1)}, bf16[1632,128]{1,0:T(8,128)(2,1)S(1)}, u32[]{:S(2)}, u32[]{:S(2)}) collective-permute-start(bf16[1632,128]{1,0:T(8,128)(2,1)S(1)} %get-tuple-element.55), channel_id=1, source_target_pairs={{0,8},{8,0},{16,24},{24,16},{32,40},{40,32},{48,56},{56,48},{64,72... | collective-permute-start | bytes 1253384 | tf_op jit(solution)/shard_map/ppermute | solution.py:385
  65.0 5.2 %collective-permute-start.7 = (bf16[260,256]{1,0:T(8,128)(2,1)S(1)}, bf16[260,256]{1,0:T(8,128)(2,1)S(1)}, u32[]{:S(2)}, u32[]{:S(2)}) collective-permute-start(bf16[260,256]{1,0:T(8,128)(2,1)S(1)} %get-tuple-element.61), channel_id=1, source_target_pairs={{0,8},{8,0},{16,24},{24,16},{32,40},{40,32},{48,56},{56,48},{64,72... | collective-permute-start | bytes 399368 | tf_op jit(solution)/shard_map/ppermute | solution.py:385

commit v9 on v8

--- a/solution.py
+++ b/solution.py
@@ -189,7 +189,7 @@
 
 
 def clean_body(
-    window_ref, near, far, q_ref, gt_ref, noisy_stats, keys, e_out, dp_out, stats, s_ref
+    window_ref, far, near, q_ref, gt_ref, noisy_stats, keys, e_out, dp_out, stats, s_ref
 ):
     use1, use2, use3 = listed(window_ref)
     first = lax.axis_index("seq") % 2 == 0
@@ -423,8 +423,8 @@
     pair_kv = shape((2, slot, 2 * LANES), BF16)
     flown = shape((2, rows, 2 * LANES), BF16)
     clean_kv = kernel_call(pair_body, flown, 10**6, nargs=2)(own, far)
+    far_kv = stretch_shift(clean_kv, 1, True)
     near_kv = stretch_shift(clean_kv, 1, False)
-    far_kv = stretch_shift(clean_kv, 1, True)
     q_all, g_turned, noisy_e, noisy_sum, noisy_stats = kernel_call(
         noisy_body,
         (
@@ -446,7 +446,7 @@
         [pltpu.VMEM((2, slot, queries), F32)],
         smem=(0,),
         nargs=6,
-    )(window, near_kv, far_kv, q_all, g_turned, noisy_stats)
+    )(window, far_kv, near_kv, q_all, g_turned, noisy_stats)
     far_stats = core_swap(own_stats)
     pair_grad = shape((2, rows, 2 * LANES), BF16)
     near_back, far_back, clean_ds, merged = kernel_call(

time: 82.6 us -> 83.5 us (1.011)
  the two profiles are of different devices: /device:TPU:240 before, /device:TPU:224 now
where the time goes in v9:
time: 83.5 us; the launch traced here: 83.1 us
  starting transfers between devices  35.2 us (42%)
  waiting for transfers between devices  17.1 us (20%)
  blocking collectives  16.2 us (19%)
  Pallas kernels  13.5 us (16%)
  between operations  0.88 us (1%)
    ppermute x4, starting transfers between devices, core_swap(): return lax.ppermute(value, 'seq', [(i, i ^ 1) for i in range(count)])  22.6 us
    all_to_all x1, blocking collectives, head_exchange(): return lax.all_to_all(value, 'head', 0, 0)  16.2 us
    ppermute x4, waiting for transfers between devices, stretch_shift(): return lax.ppermute(value, 'seq', pairs)  8.01 us
    ppermute x4, starting transfers between devices, stretch_shift(): return lax.ppermute(value, 'seq', pairs)  8.01 us
    all_to_all x1, waiting for transfers between devices, head_exchange(): return lax.all_to_all(value, 'head', 0, 0)  6.29 us
    all_to_all x1, starting transfers between devices, head_exchange(): return lax.all_to_all(value, 'head', 0, 0)  4.55 us
    ppermute x4, waiting for transfers between devices, core_swap(): return lax.ppermute(value, 'seq', [(i, i ^ 1) for i in range(count)])  2.79 us
    pallas_call x1, Pallas kernels, on_device(): kernel_call(noisy_grad_body, (shape((rows, 2 * LANES), F32), shape((2 * s...  2.5 us
  transfers between devices with their start and end apart: 9, of which 4 were waited for; matrix products, arithmetic and copies ran while one was open for 0% of the time, Pallas kernels for 6%

profile of v9, /device:TPU:224, one launch (start us, length us, event | category | flops | bytes accessed | tf_op | source)
XLA Modules:
  0.0 83.1 jit_solution(1911531557122949216)
XLA Ops:
  0.7 2.0 %shard_map.136 = f32[8,3,260]{2,1,0:T(4,128)} custom-call(bf16[260,384]{1,0:T(8,128)(2,1)} %q_ref.5, bf16[260,128]{1,0:T(8,128)(2,1)} %k_ref.5, bf16[260,128]{1,0:T(8,128)(2,1)} %c_ref.7), custom_call_target="tpu_custom_call" | custom-call | flops 10000000000 | bytes 1000000 | tf_op jit(solution)/shard_map/pallas_call | solution.py:403
  2.7 4.5 %all-to-all-start = ((f32[8,3,260]{2,1,0:T(4,128)}), f32[8,3,260]{2,1,0:T(4,128)S(1)}, u32[]{:S(2)}, u32[]{:S(2)}) async-start(f32[8,3,260]{2,1,0:T(4,128)} %shard_map.136), calls=%async_computation | async-start | bytes 98304 | tf_op jit(solution)/shard_map/all_to_all | solution.py:367
  7.3 6.3 %all-to-all-done.sums_ref = f32[8,3,260]{2,1,0:T(4,128)S(1)} async-done(((f32[8,3,260]{2,1,0:T(4,128)}), f32[8,3,260]{2,1,0:T(4,128)S(1)}, u32[]{:S(2)}, u32[]{:S(2)}) %all-to-all-start) | async-done | bytes 24992 | tf_op jit(solution)/shard_map/all_to_all | solution.py:367
  13.6 0.0 copy-done.1
  13.6 0.0 copy-done
  13.6 0.4 shard_map.137
  14.1 1.9 %collective-permute-start = (bf16[1088,256]{1,0:T(8,128)(2,1)S(1)}, bf16[1088,256]{1,0:T(8,128)(2,1)S(1)}, u32[]{:S(2)}, u32[]{:S(2)}) collective-permute-start(bf16[1088,256]{1,0:T(8,128)(2,1)S(1)} %get-tuple-element.41.own), channel_id=1, source_target_pairs={{0,8},{8,0},{16,24},{24,16},{32,40},{40,32},{48,56},{56,48},{64,72... | collective-permute-start | bytes 1671176 | tf_op jit(solution)/shard_map/ppermute | solution.py:385
  16.0 1.9 %collective-permute-done.far = bf16[1088,256]{1,0:T(8,128)(2,1)S(1)} collective-permute-done((bf16[1088,256]{1,0:T(8,128)(2,1)S(1)}, bf16[1088,256]{1,0:T(8,128)(2,1)S(1)}, u32[]{:S(2)}, u32[]{:S(2)}) %collective-permute-start) | collective-permute-done | bytes 557088 | tf_op jit(solution)/shard_map/ppermute | solution.py:385
  17.9 2.7 %collective-permute-start.2 = (bf16[2,260,256]{2,1,0:T(8,128)(2,1)S(1)}, bf16[2,260,256]{2,1,0:T(8,128)(2,1)S(1)}, u32[]{:S(2)}, u32[]{:S(2)}) collective-permute-start(bf16[2,260,256]{2,1,0:T(8,128)(2,1)S(1)} %shard_map.138), channel_id=1, source_target_pairs={{0,16},{8,56},{16,32},{24,72},{32,48},{40,88},{48,64},{56,104},{64... | collective-permute-start | bytes 798728 | tf_op jit(solution)/shard_map/ppermute | solution.py:380
  20.6 0.7 collective-permute-start.1
  21.3 0.1 copy.16.window_ref
  21.4 1.0 %shard_map.139 = (bf16[1664,128]{1,0:T(8,128)(2,1)S(1)}, bf16[128,1664]{1,0:T(8,128)(2,1)S(1)}, bf16[272,1664]{1,0:T(8,128)(2,1)S(1)}, f32[128,1664]{1,0:T(8,128)S(1)}, f32[8,1664]{1,0:T(8,128)S(1)}) custom-call(bf16[1088,256]{1,0:T(8,128)(2,1)S(1)} %get-tuple-element.41.own, bf16[1088,256]{1,0:T(8,128)(2,1)S(1)} %collective-permute-done.far, ...), custom_call_target="tpu_custom_call" | custom-call | flops 463470592 | bytes 2662400 | tf_op jit(solution)/shard_map/pallas_call | solution.py:428
  22.5 8.0 %collective-permute-done.2.near = bf16[2,260,256]{2,1,0:T(8,128)(2,1)S(1)} collective-permute-done((bf16[2,260,256]{2,1,0:T(8,128)(2,1)S(1)}, bf16[2,260,256]{2,1,0:T(8,128)(2,1)S(1)}, u32[]{:S(2)}, u32[]{:S(2)}) %collective-permute-start.2) | collective-permute-done | bytes 266272 | tf_op jit(solution)/shard_map/ppermute | solution.py:380
  30.5 0.0 collective-permute-done.1.far
  30.5 2.3 %shard_map.140 = (bf16[2,272,256]{2,1,0:T(8,128)(2,1)S(1)}, bf16[2,272,1664]{2,1,0:T(8,128)(2,1)S(1)}, f32[2,272,1664]{2,1,0:T(8,128)S(1)}, f32[8,1664]{1,0:T(8,128)S(1)}) custom-call(s32[32,2]{1,0:T(8,128)S(1)} %copy.16.window_ref, bf16[2,260,256]{2,1,0:T(8,128)(2,1)S(1)} %collective-permute-done.1.far, ...), custom_call_target="tpu_custom_call" | custom-call | flops 926941184 | bytes 5763072 | tf_op jit(solution)/shard_map/pallas_call | solution.py:442
  32.8 8.0 %collective-permute-start.3 = (f32[8,1664]{1,0:T(8,128)S(1)}, f32[8,1664]{1,0:T(8,128)S(1)}, u32[]{:S(2)}, u32[]{:S(2)}) collective-permute-start(f32[8,1664]{1,0:T(8,128)S(1)} %get-tuple-element.46.own), channel_id=1, source_target_pairs={{0,8},{8,0},{16,24},{24,16},{32,40},{40,32},{48,56},{56,48},{64,72... | collective-permute-start | bytes 159752 | tf_op jit(solution)/shard_map/ppermute | solution.py:385
  40.8 0.9 %collective-permute-done.3.far = f32[8,1664]{1,0:T(8,128)S(1)} collective-permute-done((f32[8,1664]{1,0:T(8,128)S(1)}, f32[8,1664]{1,0:T(8,128)S(1)}, u32[]{:S(2)}, u32[]{:S(2)}) %collective-permute-start.3) | collective-permute-done | bytes 53280 | tf_op jit(solution)/shard_map/ppermute | solution.py:385
  41.7 2.2 %shard_map.141 = (bf16[2,260,256]{2,1,0:T(8,128)(2,1)S(1)}, bf16[2,260,256]{2,1,0:T(8,128)(2,1)S(1)}, bf16[2,272,1664]{2,1,0:T(8,128)(2,1)S(1)}, f32[8,1664]{1,0:T(8,128)S(1)}) custom-call(s32[32,2]{1,0:T(8,128)S(1)} %copy.16.window_ref, f32[8,1664]{1,0:T(8,128)S(1)} %get-tuple-element.46.own, f32[8,1664]{1,0:T(8,128)S(1)} %collective-permute-done.3.far, ...), custom_call_target="tpu_custom_call" | custom-call | flops 926941184 | bytes 2396160 | tf_op jit(solution)/shard_map/pallas_call | solution.py:452
  43.9 4.0 %collective-permute-start.5 = (bf16[2,260,256]{2,1,0:T(8,128)(2,1)S(1)}, bf16[2,260,256]{2,1,0:T(8,128)(2,1)S(1)}, u32[]{:S(2)}, u32[]{:S(2)}) collective-permute-start(bf16[2,260,256]{2,1,0:T(8,128)(2,1)S(1)} %get-tuple-element.58), channel_id=1, source_target_pairs={{16,0},{32,16},{48,32},{56,8},{64,48},{72,24},{80,64},{88,40},{96,... | collective-permute-start | bytes 798728 | tf_op jit(solution)/shard_map/ppermute | solution.py:380
  47.9 0.7 collective-permute-start.6
  48.6 2.5 %shard_map.142 = (f32[260,256]{1,0:T(8,128)S(1)}, f32[1632,128]{1,0:T(8,128)S(1)}, bf16[1632,128]{1,0:T(8,128)(2,1)S(1)}) custom-call(f32[8,1664]{1,0:T(8,128)S(1)} %get-tuple-element.49.merged, bf16[1664,128]{1,0:T(8,128)(2,1)S(1)} %get-tuple-element.43.q_ref, bf16[128,1664]{1,0:T(8,128)(2,1)S(1)} %get-tuple-element.44.gt_ref, ...), custom_call_target="tpu_custom_call" | custom-call | flops 926941184 | bytes 1519616 | tf_op jit(solution)/shard_map/pallas_call | solution.py:461
  51.1 4.6 %collective-permute-start.4 = (bf16[1632,128]{1,0:T(8,128)(2,1)S(1)}, bf16[1632,128]{1,0:T(8,128)(2,1)S(1)}, u32[]{:S(2)}, u32[]{:S(2)}) collective-permute-start(bf16[1632,128]{1,0:T(8,128)(2,1)S(1)} %get-tuple-element.55), channel_id=1, source_target_pairs={{0,8},{8,0},{16,24},{24,16},{32,40},{40,32},{48,56},{56,48},{64,72... | collective-permute-start | bytes 1253384 | tf_op jit(solution)/shard_map/ppermute | solution.py:385
  55.7 0.0 collective-permute-done.5.near
  55.7 0.0 collective-permute-done.6.far
  55.7 0.1 shard_map.144
  55.7 8.1 %collective-permute-start.7 = (bf16[260,256]{1,0:T(8,128)(2,1)S(1)}, bf16[260,256]{1,0:T(8,128)(2,1)S(1)}, u32[]{:S(2)}, u32[]{:S(2)}) collective-permute-start(bf16[260,256]{1,0:T(8,128)(2,1)S(1)} %get-tuple-element.61), channel_id=1, source_target_pairs={{0,8},{8,0},{16,24},{24,16},{32,40},{40,32},{48,56},{56,48},{64,72... | collective-permute-start | bytes 399368 | tf_op jit(solution)/shard_map/ppermute | solution.py:385
  63.8 0.0 collective-permute-done.4.far
  63.9 1.2 %shard_map.143 = (bf16[260,384]{1,0:T(8,128)(2,1)}, bf16[260,128]{1,0:T(8,128)(2,1)}, f32[8,260]{1,0:T(8,128)S(1)}, f32[260,384]{1,0:T(8,128)S(1)}, f32[260,384]...) custom-call(f32[8,3,260]{2,1,0:T(4,128)S(1)} %all-to-all-done.sums_r, ...), custom_call_target="tpu_custom_call" | custom-call | flops 1000000 | bytes 1605760 | tf_op jit(solution)/shard_map/pallas_call | solution.py:484
  65.1 0.0 collective-permute-done.7.far_clean
  65.1 0.7 shard_map.145
  65.7 16.2 %all_to_all.10.inner_ref = f32[8,3,260]{2,1,0:T(4,128)S(1)} all-to-all(f32[8,3,260]{2,1,0:T(4,128)S(1)} %get-tuple-element.64), channel_id=1, replica_groups=mesh['seq'=64,'head'=8] {'head'}, dimensions={0} | all-to-all | bytes 49920 | tf_op jit(solution)/shard_map/all_to_all | solution.py:367
  82.0 1.1 %shard_map.146 = (bf16[260,384]{1,0:T(8,128)(2,1)}, bf16[260,128]{1,0:T(8,128)(2,1)}, bf16[260,128]{1,0:T(8,128)(2,1)}) custom-call(f32[8,3,260]{2,1,0:T(4,128)S(1)} %all_to_all.10.inner_ref, f32[260,384]{1,0:T(8,128)S(1)} %get-tuple-element.65.q_push, f32[260,384]{1,0:T(8,128)S(1)} %get-tuple-element.66.q_pull, f32[260,128]{1,0:T(8,128)S(1)} %get-tuple-element.67.k_push, ...), custom_call_target="tpu_custom_call" | custom-call | flops 1000000 | bytes 332800 | tf_op jit(solution)/shard_map/pallas_call | solution.py:498
  (18 shorter events, 0.1 us)
Async XLA Ops:
  0.6 13.0 %copy-start.1 = (bf16[260,128]{1,0:T(8,128)(2,1)S(1)}, bf16[260,128]{1,0:T(8,128)(2,1)}, u32[]{:S(2)}) copy-start(bf16[260,128]{1,0:T(8,128)(2,1)} %c_ref.7) | copy-start | bytes 199684
  0.6 12.9 %copy-start.2 = (bf16[260,128]{1,0:T(8,128)(2,1)S(1)}, bf16[260,128]{1,0:T(8,128)(2,1)}, u32[]{:S(2)}) copy-start(bf16[260,128]{1,0:T(8,128)(2,1)} %k_ref.5) | copy-start | bytes 199684
  0.7 12.9 %copy-start = (bf16[260,384]{1,0:T(8,128)(2,1)S(1)}, bf16[260,384]{1,0:T(8,128)(2,1)}, u32[]{:S(2)}) copy-start(bf16[260,384]{1,0:T(8,128)(2,1)} %q_ref.5) | copy-start | bytes 599044
  0.7 6.6 %copy-start.7 = (f32[384]{0:T(512)S(1)}, f32[384]{0:T(512)}, u32[]{:S(2)}) copy-start(f32[384]{0:T(512)} %param.14) | copy-start | bytes 4612
  0.7 12.9 %copy-start.3 = (bf16[260,384]{1,0:T(8,128)(2,1)S(1)}, bf16[260,384]{1,0:T(8,128)(2,1)}, u32[]{:S(2)}) copy-start(bf16[260,384]{1,0:T(8,128)(2,1)} %g_ref.1) | copy-start | bytes 599044
  0.7 12.9 %copy-start.6 = (f32[128]{0:T(128)S(1)}, f32[128]{0:T(128)}, u32[]{:S(2)}) copy-start(f32[128]{0:T(128)} %param.15) | copy-start | bytes 1540
  0.7 12.9 %copy-start.5 = (bf16[260,128]{1,0:T(8,128)(2,1)S(1)}, bf16[260,128]{1,0:T(8,128)(2,1)}, u32[]{:S(2)}) copy-start(bf16[260,128]{1,0:T(8,128)(2,1)} %cv_ref.1) | copy-start | bytes 199684
  0.7 12.9 %copy-start.4 = (bf16[260,128]{1,0:T(8,128)(2,1)S(1)}, bf16[260,128]{1,0:T(8,128)(2,1)}, u32[]{:S(2)}) copy-start(bf16[260,128]{1,0:T(8,128)(2,1)} %v_ref.1) | copy-start | bytes 199684
  2.7 18.6 %copy-start.8 = (s32[32,2]{0,1:T(2,128)S(1)}, s32[32,2]{0,1:T(2,128)}, u32[]{:S(2)}) copy-start(s32[32,2]{0,1:T(2,128)} %param.17) | copy-start | bytes 772
  2.7 10.8 %all-to-all-start = ((f32[8,3,260]{2,1,0:T(4,128)}), f32[8,3,260]{2,1,0:T(4,128)S(1)}, u32[]{:S(2)}, u32[]{:S(2)}) async-start(f32[8,3,260]{2,1,0:T(4,128)} %shard_map.136), calls=%async_computation | async-start | bytes 98304 | tf_op jit(solution)/shard_map/all_to_all | solution.py:367
  14.1 3.9 %collective-permute-start = (bf16[1088,256]{1,0:T(8,128)(2,1)S(1)}, bf16[1088,256]{1,0:T(8,128)(2,1)S(1)}, u32[]{:S(2)}, u32[]{:S(2)}) collective-permute-start(bf16[1088,256]{1,0:T(8,128)(2,1)S(1)} %get-tuple-element.41.own), channel_id=1, source_target_pairs={{0,8},{8,0},{16,24},{24,16},{32,40},{40,32},{48,56},{56,48},{64,72... | collective-permute-start | bytes 1671176 | tf_op jit(solution)/shard_map/ppermute | solution.py:385
  17.9 12.5 %collective-permute-start.2 = (bf16[2,260,256]{2,1,0:T(8,128)(2,1)S(1)}, bf16[2,260,256]{2,1,0:T(8,128)(2,1)S(1)}, u32[]{:S(2)}, u32[]{:S(2)}) collective-permute-start(bf16[2,260,256]{2,1,0:T(8,128)(2,1)S(1)} %shard_map.138), channel_id=1, source_target_pairs={{0,16},{8,56},{16,32},{24,72},{32,48},{40,88},{48,64},{56,104},{64... | collective-permute-start | bytes 798728 | tf_op jit(solution)/shard_map/ppermute | solution.py:380
  20.6 9.8 %collective-permute-start.1 = (bf16[2,260,256]{2,1,0:T(8,128)(2,1)S(1)}, bf16[2,260,256]{2,1,0:T(8,128)(2,1)S(1)}, u32[]{:S(2)}, u32[]{:S(2)}) collective-permute-start(bf16[2,260,256]{2,1,0:T(8,128)(2,1)S(1)} %shard_map.138), channel_id=1, source_target_pairs={{8,40},{24,56},{40,72},{56,88},{72,104},{88,120},{104,136},{120,15... | collective-permute-start | bytes 798728 | tf_op jit(solution)/shard_map/ppermute | solution.py:380
  32.8 8.9 %collective-permute-start.3 = (f32[8,1664]{1,0:T(8,128)S(1)}, f32[8,1664]{1,0:T(8,128)S(1)}, u32[]{:S(2)}, u32[]{:S(2)}) collective-permute-start(f32[8,1664]{1,0:T(8,128)S(1)} %get-tuple-element.46.own), channel_id=1, source_target_pairs={{0,8},{8,0},{16,24},{24,16},{32,40},{40,32},{48,56},{56,48},{64,72... | collective-permute-start | bytes 159752 | tf_op jit(solution)/shard_map/ppermute | solution.py:385
  43.9 11.8 %collective-permute-start.5 = (bf16[2,260,256]{2,1,0:T(8,128)(2,1)S(1)}, bf16[2,260,256]{2,1,0:T(8,128)(2,1)S(1)}, u32[]{:S(2)}, u32[]{:S(2)}) collective-permute-start(bf16[2,260,256]{2,1,0:T(8,128)(2,1)S(1)} %get-tuple-element.58), channel_id=1, source_target_pairs={{16,0},{32,16},{48,32},{56,8},{64,48},{72,24},{80,64},{88,40},{96,... | collective-permute-start | bytes 798728 | tf_op jit(solution)/shard_map/ppermute | solution.py:380
  47.9 7.8 %collective-permute-start.6 = (bf16[2,260,256]{2,1,0:T(8,128)(2,1)S(1)}, bf16[2,260,256]{2,1,0:T(8,128)(2,1)S(1)}, u32[]{:S(2)}, u32[]{:S(2)}) collective-permute-start(bf16[2,260,256]{2,1,0:T(8,128)(2,1)S(1)} %get-tuple-element.59), channel_id=1, source_target_pairs={{40,8},{56,24},{72,40},{88,56},{104,72},{120,88},{136,104},{152,12... | collective-permute-start | bytes 798728 | tf_op jit(solution)/shard_map/ppermute | solution.py:380
  51.1 12.8 %collective-permute-start.4 = (bf16[1632,128]{1,0:T(8,128)(2,1)S(1)}, bf16[1632,128]{1,0:T(8,128)(2,1)S(1)}, u32[]{:S(2)}, u32[]{:S(2)}) collective-permute-start(bf16[1632,128]{1,0:T(8,128)(2,1)S(1)} %get-tuple-element.55), channel_id=1, source_target_pairs={{0,8},{8,0},{16,24},{24,16},{32,40},{40,32},{48,56},{56,48},{64,72... | collective-permute-start | bytes 1253384 | tf_op jit(solution)/shard_map/ppermute | solution.py:385
  55.7 9.3 %collective-permute-start.7 = (bf16[260,256]{1,0:T(8,128)(2,1)S(1)}, bf16[260,256]{1,0:T(8,128)(2,1)S(1)}, u32[]{:S(2)}, u32[]{:S(2)}) collective-permute-start(bf16[260,256]{1,0:T(8,128)(2,1)S(1)} %get-tuple-element.61), channel_id=1, source_target_pairs={{0,8},{8,0},{16,24},{24,16},{32,40},{40,32},{48,56},{56,48},{64,72... | collective-permute-start | bytes 399368 | tf_op jit(solution)/shard_map/ppermute | solution.py:385
